TPU v7x, 1024 devices: a whole 8x8x8 slice. The times are simulated.
1024 devices in a mesh: gx: 8 (over x_lo, core), gy: 128 (over x_hi, z, y).
Axes of the slice: x: 8 (x_hi: 2, x_lo: 4; x = x_hi * 4 + x_lo), y: 8, z: 8, core: 2. Of those that a mesh axis runs over, the one named last changes fastest.
Arguments:
- tokens: bfloat16 [256, 18432], P('gy', 'gx'), may hold values from -6 to 6
- w_query: bfloat16 [18432, 12288], P('gx', 'gy'), may hold values from -0.046875 to 0.046875
- w_gate_up: bfloat16 [18432, 2, 36864], P('gx', None, 'gy'), may hold values from -0.046875 to 0.046875
- key_cache: bfloat16 [256, 2048, 256], P('gy', 'gx'), may hold values from -480 to 480
- value_cache: bfloat16 [256, 2048, 256], P('gy', 'gx'), may hold values from -6 to 6
- new_kv: bfloat16 [256, 2, 256], P('gy'), may hold values from -6 to 6
- lengths: int32 [256], P('gy'), may hold values from 256 to 2048, as said below
Outputs:
- hidden: bfloat16 [256, 36864], P('gx', 'gy')
- attended: bfloat16 [256, 12288], P('gy', 'gx')
Inputs may be any that keep to these rules, and one draw needn't show every extreme that they name: `lengths`: the number of filled slots of each sequence; some sequence has all 2048 filled.
All inputs are finite; a program needn't handle non-finite values.
Results may differ from a plain program's by a relative error of at most 0.02.
Values may be sent and summed in bfloat16 or wider, within the bound.
No kernel may reach another device: no remote copies, remote signals or barrier semaphores. Data moves between devices by JAX's collectives and lax.ppermute only.
A program may use at most 32 MiB of HBM per device.

v0:
```python
import jax
import jax.numpy as jnp
from jax import lax
from jax.sharding import PartitionSpec as P

NEG = -1e30


def merged(part, axis, combine):
    gathered = jax.tree.map(lambda a: lax.all_gather(a, axis), part)

    def take(source):
        return jax.tree.map(lambda a: lax.dynamic_index_in_dim(a, source, 0, False), gathered)

    return lax.fori_loop(
        1, lax.axis_size(axis), lambda source, state: combine(state, take(source)), take(0)
    )


def merge_parts(first, second):
    top = jnp.maximum(first[0], second[0])
    left = jnp.exp(first[0] - top)
    right = jnp.exp(second[0] - top)
    total = first[1] * left + second[1] * right
    mixed = first[2] * left[..., None] + second[2] * right[..., None]
    return (top, total, mixed)


def body(tokens, w_query, w_gate_up, key_cache, value_cache, new_kv, lengths):
    gathered = lax.all_gather(tokens, "gy", axis=0, tiled=True)
    width = w_gate_up.shape[2]
    w_flat = w_gate_up.reshape(w_gate_up.shape[0], 2 * width)
    share = lax.psum_scatter(
        jnp.dot(gathered, w_flat, preferred_element_type=jnp.float32),
        "gx",
        scatter_dimension=0,
        tiled=True,
    )
    hidden = (jax.nn.silu(share[:, :width]) * share[:, width:]).astype(jnp.bfloat16)
    partial_value = jnp.dot(gathered, w_query, preferred_element_type=jnp.float32)
    summed = lax.psum(partial_value, "gx")
    query = lax.all_to_all(
        summed.astype(jnp.bfloat16), "gy", split_axis=0, concat_axis=1, tiled=True
    )
    seqs, block_len, head_dim = key_cache.shape
    heads = query.shape[1] // head_dim
    per_dev = heads // lax.axis_size("gx")
    place = lax.axis_index("gx")
    scale = head_dim ** (-0.5)
    query3 = query.reshape(seqs, heads, head_dim).astype(jnp.float32)
    scores = jnp.einsum("rhd,rld->rhl", query3, key_cache.astype(jnp.float32)) * scale
    positions = place * block_len + jnp.arange(block_len, dtype=jnp.int32)
    valid = positions[None, :] < lengths[:, None]
    scores = jnp.where(valid[:, None, :], scores, NEG)
    top = jnp.max(scores, axis=2)
    probs = jnp.where(valid[:, None, :], jnp.exp(scores - top[..., None]), 0.0)
    total = jnp.sum(probs, axis=2)
    mixed = jnp.einsum("rhl,rld->rhd", probs, value_cache.astype(jnp.float32))
    top, total, mixed = merged((top, total, mixed), "gx", merge_parts)
    top = lax.dynamic_slice_in_dim(top, place * per_dev, per_dev, 1)
    total = lax.dynamic_slice_in_dim(total, place * per_dev, per_dev, 1)
    mixed = lax.dynamic_slice_in_dim(mixed, place * per_dev, per_dev, 1)
    own_query = lax.dynamic_slice_in_dim(query3, place * per_dev, per_dev, 1)
    key_new = new_kv[:, 0, :].astype(jnp.float32)
    value_new = new_kv[:, 1, :].astype(jnp.float32)
    own = jnp.sum(own_query * key_new[:, None, :], axis=2) * scale
    final_top = jnp.maximum(top, own)
    old_weight = jnp.exp(top - final_top)
    own_prob = jnp.exp(own - final_top)
    numer = mixed * old_weight[..., None] + own_prob[..., None] * value_new[:, None, :]
    denom = total * old_weight + own_prob
    attended = (numer / denom[..., None]).reshape(seqs, per_dev * head_dim).astype(jnp.bfloat16)
    return (hidden, attended)


def solution(mesh):
    return jax.shard_map(
        body,
        mesh=mesh,
        in_specs=(
            P("gy", "gx"),
            P("gx", "gy"),
            P("gx", None, "gy"),
            P("gy", "gx", None),
            P("gy", "gx", None),
            P("gy", None, None),
            P("gy"),
        ),
        out_specs=(P("gx", "gy"), P("gy", "gx")),
        check_vma=False,
    )
```

profile of v0, /device:TPU:1, one launch (start us, length us, event | category | flops | bytes accessed | tf_op | source)
XLA Modules:
  0.0 274.1 jit_solution(18398973159125503826)
XLA Ops:
  7.2 0.0 copy-start
  7.2 0.0 all-gather.8.cloned.1.call-start
  7.2 0.7 all-gather.8.cloned.1.call-update
  7.9 0.8 slice_convert_fusion
  8.7 0.6 copy.20
  9.3 0.6 copy.19
  9.9 0.7 broadcast_compare_fusion
  10.6 0.0 copy-start.1
  10.6 144.8 %all-gather.8.cloned.1.call-done = bf16[128,2,2304]{2,1,0:T(2,128)(2,1)} async-done(((bf16[1,2,2304]{2,1,0:T(2,128)(2,1)}), bf16[128,2,2304]{2,1,0:T(2,128)(2,1)}) %all-gather.8.cloned.1.call-update) | async-done | bytes 1179664 | tf_op jit(solution)/shard_map/all_gather | solution.py:30
  155.4 3.6 %reshape.63 = bf16[256,2304]{1,0:T(8,128)(2,1)} reshape(bf16[128,2,2304]{2,1,0:T(2,128)(2,1)} %all-gather.8.cloned.1.call-done) | data formatting | bytes 2359296
  159.0 0.0 copy-done.1
  159.0 1.8 fusion.19
  160.8 26.9 %psum.7 = bf16[256,96]{0,1:T(8,128)(2,1)S(1)} all-reduce(f32[256,96]{0,1:T(8,128)S(1)} %fusion.19), channel_id=1, replica_groups=mesh['gx'=8,'gy'=128] {'gx'}, use_global_device_ids=true, to_apply=%region_1.2 | all-reduce | flops 24576 | bytes 147456 | tf_op jit(solution)/shard_map/psum | solution.py:41
  187.7 0.7 copy.12
  188.4 10.8 %all-to-all-start = ((bf16[128,2,96]{2,1,0:T(2,128)(2,1)}), bf16[128,2,96]{2,1,0:T(2,128)(2,1)S(1)}, u32[]{:S(2)}, u32[]{:S(2)}) async-start(bf16[128,2,96]{2,1,0:T(2,128)(2,1)} %bitcast.5), calls=%async_computation.1 | async-start | bytes 131072 | tf_op jit(solution)/shard_map/all_to_all | solution.py:42
  199.2 0.0 reduce-scatter.2.cloned.1.call-start
  199.3 0.0 copy-done
  199.3 0.0 copy-start.3
  199.3 3.3 %fusion.18 = f32[256,576]{1,0:T(8,128)} fusion(bf16[256,2304]{1,0:T(8,128)(2,1)} %reshape.63, bf16[2304,576]{0,1:T(8,128)(2,1)S(1)} %bitcast.46), kind=kOutput, calls=%fused_computation.38 | convolution fusion | flops 679477248 | bytes 4423680 | tf_op jit(solution)/shard_map/dot_general | solution.py:34
  202.6 0.0 copy-start.2
  202.6 0.0 reduce-scatter.2.cloned.1.call-update
  202.6 12.3 %all-to-all-done = bf16[128,2,96]{2,1,0:T(2,128)(2,1)S(1)} async-done(((bf16[128,2,96]{2,1,0:T(2,128)(2,1)}), bf16[128,2,96]{2,1,0:T(2,128)(2,1)S(1)}, u32[]{:S(2)}, u32[]{:S(2)}) %all-to-all-start) | async-done | bytes 49184 | tf_op jit(solution)/shard_map/all_to_all | solution.py:42
  214.9 0.1 reshape.50
  215.1 0.0 copy-done.3
  215.1 0.0 copy-start.4
  215.1 0.3 fusion.17
  215.3 13.8 %all-gather.4 = f32[8,2,48]{2,1,0:T(2,128)S(1)} all-gather(f32[1,2,48]{2,1,0:T(2,128)S(1)} %bitcast.49), channel_id=2, replica_groups=mesh['gx'=8,'gy'=128] {'gx'}, dimensions={0}, use_global_device_ids=true | all-gather | bytes 3456 | tf_op jit(solution)/shard_map/all_gather | solution.py:10
  229.1 0.2 fusion.5
  229.3 10.4 %all-gather.5 = f32[8,2,48]{2,1,0:T(2,128)S(1)} all-gather(f32[1,2,48]{2,1,0:T(2,128)S(1)} %bitcast.54), channel_id=3, replica_groups=mesh['gx'=8,'gy'=128] {'gx'}, dimensions={0}, use_global_device_ids=true | all-gather | bytes 3456 | tf_op jit(solution)/shard_map/all_gather | solution.py:10
  239.7 0.0 copy-start.5
  239.7 0.0 copy-done.4
  239.7 0.6 copy-done.5
  240.3 0.0 copy-done.2
  240.3 0.2 fusion.4
  240.5 17.1 %all-gather.2 = f32[16,48,256]{2,1,0:T(8,128)S(1)} all-gather(f32[2,48,256]{2,1,0:T(8,128)S(1)} %fusion.4), channel_id=4, replica_groups=mesh['gx'=8,'gy'=128] {'gx'}, dimensions={0}, use_global_device_ids=true | all-gather | bytes 884736 | tf_op jit(solution)/shard_map/all_gather | solution.py:10
  257.6 5.8 %while.19 = (s32[]{:T(128)}, f32[2,48]{1,0:T(2,128)S(1)}, f32[2,48]{1,0:T(2,128)S(1)}, f32[2,48,256]{2,1,0:T(8,128)S(1)}, f32[8,2,48]{2,1,0:T(2,128)S(1)}, /*ind...) while((s32[]{:T(128)}, f32[2,48]{1,0:T(2,128)S(1)}, ...), condition=%wide.region_5.6_spmd, body=%wide.region_4.5_spmd.sunk | while | flops 74309 | bytes 298903 | solution.py:15
  257.6 0.7 fusion.29
  258.3 0.1 fusion.30
  258.4 0.7 fusion.29
  259.1 0.1 fusion.30
  259.2 0.7 fusion.29
  259.9 0.1 fusion.30
  260.1 0.7 fusion.29
  260.8 0.1 fusion.30
  260.9 0.7 fusion.29
  261.6 0.1 fusion.30
  261.7 0.7 fusion.29
  262.4 0.1 fusion.30
  262.6 0.7 fusion.29
  263.3 0.1 fusion.30
  263.4 0.8 multiply_reduce_fusion
  264.2 0.1 multiply_add_fusion
  264.3 0.8 fusion.10
  265.0 0.6 copy.16
  265.6 0.0 reduce-scatter.2.cloned.1.call-done
  265.6 1.6 fusion.6
  (5 shorter events, 0.0 us)
Async XLA Ops:
  7.2 192.1 %copy-start = (bf16[2304,2,288]{0,2,1:T(8,128)(2,1)S(1)}, bf16[2304,2,288]{0,2,1:T(8,128)(2,1)}, u32[]{:S(2)}) copy-start(bf16[2304,2,288]{0,2,1:T(8,128)(2,1)} %param.11) | copy-start | bytes 7962628
  7.2 148.2 %all-gather.8.cloned.1.call-start = ((), (), s32[]{:S(2)}) async-start(), calls=%async_computation.3 | async-start | bytes 1188864 | tf_op jit(solution)/shard_map/all_gather | solution.py:30
  10.6 148.4 %copy-start.1 = (bf16[2304,96]{0,1:T(8,128)(2,1)S(1)}, bf16[2304,96]{0,1:T(8,128)(2,1)}, u32[]{:S(2)}) copy-start(bf16[2304,96]{0,1:T(8,128)(2,1)} %param.10) | copy-start | bytes 1327108
  188.4 26.5 %all-to-all-start = ((bf16[128,2,96]{2,1,0:T(2,128)(2,1)}), bf16[128,2,96]{2,1,0:T(2,128)(2,1)S(1)}, u32[]{:S(2)}, u32[]{:S(2)}) async-start(bf16[128,2,96]{2,1,0:T(2,128)(2,1)} %bitcast.5), calls=%async_computation.1 | async-start | bytes 131072 | tf_op jit(solution)/shard_map/all_to_all | solution.py:42
  199.2 66.4 %reduce-scatter.2.cloned.1.call-start = ((), (), s32[]{:S(2)}) async-start(), calls=%async_computation.2 | async-start | bytes 737280 | tf_op jit(solution)/shard_map/reduce_scatter | solution.py:33
  199.3 15.8 %copy-start.3 = (bf16[2,256,256]{2,1,0:T(8,128)(2,1)S(1)}, bf16[2,256,256]{2,1,0:T(8,128)(2,1)}, u32[]{:S(2)}) copy-start(bf16[2,256,256]{2,1,0:T(8,128)(2,1)} %param.12) | copy-start | bytes 786436
  202.6 37.7 %copy-start.2 = (bf16[2,256,256]{2,1,0:T(8,128)(2,1)S(1)}, bf16[2,256,256]{2,1,0:T(8,128)(2,1)}, u32[]{:S(2)}) copy-start(bf16[2,256,256]{2,1,0:T(8,128)(2,1)} %param.13) | copy-start | bytes 786436
  215.1 24.6 %copy-start.4 = (bf16[2,48,256]{2,1,0:T(8,128)(2,1)}, bf16[2,48,256]{2,1,0:T(8,128)(2,1)S(1)}, u32[]{:S(2)}) copy-start(bf16[2,48,256]{2,1,0:T(8,128)(2,1)S(1)} %reshape.50) | copy-start | bytes 147460
  239.7 0.6 copy-start.5
Sparse Core Ops, SparseCore 0:
  13.8 141.5 all-gather.7
  203.5 45.5 reduce-scatter.1
where the time goes:
time: 275 us; the launch traced here: 274 us
  waiting for transfers between devices  158 us (57%)
  blocking collectives  68.1 us (25%)
  between operations  14.1 us (5%)
  starting transfers between devices  10.9 us (4%)
  other arithmetic  10.5 us (4%)
  local copies, waits for them, and re-layouts  6.88 us (3%)
  matrix products  5.52 us (2%)
    all_gather x1, waiting for transfers between devices, body(): gathered = lax.all_gather(tokens, 'gy', axis=0, tiled=True)  145 us
    all_gather x3, blocking collectives, merged(): gathered = jax.tree.map(lambda a: lax.all_gather(a, axis), part)  41.2 us
    psum x1, blocking collectives, body(): summed = lax.psum(partial_value, 'gx')  26.9 us
    all_to_all x1, waiting for transfers between devices, body(): lax.all_to_all(summed.astype(jnp.bfloat16), 'gy', split_axis=0, concat_ax...  12.3 us
    all_to_all x1, starting transfers between devices, body(): lax.all_to_all(summed.astype(jnp.bfloat16), 'gy', split_axis=0, concat_ax...  10.8 us
    unnamed x16, local copies, waits for them, and re-layouts  6.01 us
  transfers between devices with their start and end apart: 3, of which 2 were waited for; matrix products, arithmetic and copies ran while one was open for 5% of the time, Pallas kernels for 0%

commit v1 on v0

v1 whole, which is shorter than its diff:
```python
import jax
import jax.numpy as jnp
from jax import lax
from jax.experimental import pallas as pl
from jax.experimental.pallas import tpu as pltpu
from jax.sharding import Mesh, PartitionSpec as P

NEG = -1e30
GX = ("xl", "core")
GY = ("xh", "z", "y")
ALL = GX + GY
LATTICE = ("xh", "z", "y")
PLANE = ("core", "z", "y")


def far_groups():
    return [
        [xh * 64 + (zh * 2 + zlo) * 8 + yh * 2 + ylo for xh in range(2) for zh in range(4) for yh in range(4)]
        for zlo in range(2)
        for ylo in range(2)
    ]


def near_groups():
    groups = []
    for core in range(2):
        for zb in range(4):
            for yb in range(4):
                zs = sorted(((2 * zb + i + core) % 8 for i in range(2)), key=lambda v: v % 2)
                ys = sorted(((2 * yb + i + core) % 8 for i in range(2)), key=lambda v: v % 2)
                groups.append([core * 64 + z * 8 + y for z in zs for y in ys])
    return groups


def query_groups():
    def half(g, h):
        return [g * 128 + h * 16 + i for i in range(16)]

    pairs = [(g, h) for g in range(8) for h in range(g + 1, 8)]
    return [half(g, h) + half(h, g) for g, h in pairs] + [half(g, g) + half(g + 1, g + 1) for g in range(0, 8, 2)]


def exchange(x, axis, groups=None):
    return lax.all_to_all(x, axis, 0, 0, axis_index_groups=groups, tiled=True)


def spread(x, axis, n, groups=None):
    return exchange(jnp.broadcast_to(x[None], (n,) + x.shape), axis, groups)


def beside(x):
    return lax.ppermute(x, "xl", [(i, i ^ 1) for i in range(4)])


def across(x):
    return lax.ppermute(x, "xl", [(i, i ^ 2) for i in range(4)])


def other_core(x):
    return lax.ppermute(x, "core", [(0, 1), (1, 0)])


NT = (((1,), (1,)), ((), ()))
LIMIT = pltpu.CompilerParams(vmem_limit_bytes=16 * 2**20)


def project_kernel(x_ref, wg_ref, wq_ref, out_ref, acc_ref):
    x = x_ref[...]
    width, qw = wg_ref.shape[0], wq_ref.shape[0]
    gate_up = lax.dot_general(x, wg_ref[...], NT, preferred_element_type=jnp.float32)
    query = lax.dot_general(x, wq_ref[...], NT, preferred_element_type=jnp.float32)
    for p in range(4):
        rows = slice(p * 64, p * 64 + 64)
        acc_ref[:, p * 8 : p * 8 + 8, :width] = gate_up[rows].reshape(8, 8, width)
        part = query[rows].reshape(8, 8, qw)
        acc_ref[:, p * 8 : p * 8 + 8, width : width + qw] = part
        acc_ref[:, p * 8 : p * 8 + 8, width + qw :] = part - part.astype(jnp.bfloat16).astype(jnp.float32)
    out_ref[...] = acc_ref[...].astype(jnp.bfloat16)


def project(rows, w_query, w_gate_up):
    d, _, width = w_gate_up.shape
    wg = w_gate_up.transpose(1, 2, 0).reshape(2 * width, d)
    wq = w_query.T
    shape = (8, rows.shape[0] // 8, 2 * width + 2 * wq.shape[0])
    return pl.pallas_call(
        project_kernel,
        out_shape=jax.ShapeDtypeStruct(shape, jnp.bfloat16),
        scratch_shapes=[pltpu.VMEM(shape, jnp.float32)],
        compiler_params=LIMIT,
    )(rows, wg, wq)


def attend_kernel(order, place_ref, lengths_ref, q_ref, *refs):
    n = len(order)
    keys, values, (mine_ref, theirs_ref) = refs[:n], refs[n : 2 * n], refs[2 * n :]
    seqs, block_len, head_dim = keys[0].shape
    scale = head_dim ** (-0.5)
    slot = lax.broadcasted_iota(jnp.int32, (16, block_len), 1)
    for r in range(seqs):
        q = q_ref[r]
        scores, valid = [], []
        for j, flip in enumerate(order):
            s = lax.dot_general(q, keys[j][r], NT, preferred_element_type=jnp.float32) * scale
            start = jnp.bitwise_xor(place_ref[0], flip) * block_len
            valid.append(slot + start < lengths_ref[r])
            scores.append(jnp.where(valid[j], s, NEG))
        top = scores[0]
        for s in scores[1:]:
            top = jnp.maximum(top, s)
        top = jnp.max(top, axis=1, keepdims=True)
        total = jnp.zeros((16, 1), jnp.float32)
        mixed = jnp.zeros((16, head_dim), jnp.float32)
        for j in range(n):
            p = jnp.where(valid[j], jnp.exp(scores[j] - top), 0.0)
            total += jnp.sum(p, axis=1, keepdims=True)
            mixed += jnp.dot(p.astype(jnp.bfloat16), values[j][r], preferred_element_type=jnp.float32)
        for ref, rows in ((mine_ref, slice(0, 8)), (theirs_ref, slice(8, 16))):
            ref[r, :, :head_dim] = mixed[rows]
            lane = lax.broadcasted_iota(jnp.int32, (8, 128), 1)
            ref[r, :, head_dim:] = jnp.where(lane < 64, top[rows], total[rows])


def attend(place, lengths, queries, keys, values, order):
    seqs, _, head_dim = queries.shape
    smem, vmem = pl.BlockSpec(memory_space=pltpu.SMEM), pl.BlockSpec(memory_space=pltpu.VMEM)
    out = jax.ShapeDtypeStruct((seqs, 8, head_dim + 128), jnp.float32)

    def kernel(*refs):
        attend_kernel(order, *refs)

    return pl.pallas_call(
        kernel,
        in_specs=[smem, smem] + [vmem] * (1 + 2 * len(order)),
        out_specs=(vmem, vmem),
        out_shape=(out, out),
        compiler_params=LIMIT,
    )(place.reshape(1).astype(jnp.int32), lengths, queries, *keys, *values)


def finish_kernel(heads, mine_ref, theirs_ref, q_ref, new_ref, out_ref):
    seqs, _, head_dim = q_ref.shape
    scale = head_dim ** (-0.5)
    results = []
    for r in range(seqs):
        mine, theirs = mine_ref[r], theirs_ref[r]
        new = new_ref[r].astype(jnp.float32)
        q = q_ref[r].astype(jnp.float32)[:8]
        own = jnp.sum(q * new[0:1], axis=1, keepdims=True) * scale
        tops = [p[:, head_dim : head_dim + 1] for p in (mine, theirs)]
        sums = [p[:, head_dim + 64 : head_dim + 65] for p in (mine, theirs)]
        top = jnp.maximum(jnp.maximum(tops[0], tops[1]), own)
        w0, w1, w2 = jnp.exp(tops[0] - top), jnp.exp(tops[1] - top), jnp.exp(own - top)
        numer = mine[:, :head_dim] * w0 + theirs[:, :head_dim] * w1 + w2 * new[1:2]
        results.append(numer / (sums[0] * w0 + sums[1] * w1 + w2))
    for h in range(heads):
        rows = jnp.concatenate([x[h : h + 1] for x in results], axis=0)
        out_ref[:, h * head_dim : (h + 1) * head_dim] = rows.astype(jnp.bfloat16)


def finish(mine, theirs, queries, new_kv, heads):
    def kernel(*refs):
        finish_kernel(heads, *refs)

    seqs, _, head_dim = queries.shape
    return pl.pallas_call(
        kernel,
        out_shape=jax.ShapeDtypeStruct((seqs, heads * head_dim), jnp.bfloat16),
        compiler_params=LIMIT,
    )(mine, theirs, queries, new_kv)


def body(tokens, w_query, w_gate_up, key_cache, value_cache, new_kv, lengths):
    f32, bf16 = jnp.float32, jnp.bfloat16
    d, width, qw = tokens.shape[1], w_gate_up.shape[2], w_query.shape[1]
    seqs, _, head_dim = key_cache.shape

    keys_b = beside(key_cache)
    rows = spread(tokens, LATTICE, 32, far_groups()).reshape(64, d)
    rows, keys_b = lax.optimization_barrier((rows, keys_b))
    values_b, keys_c = beside(value_cache), other_core(key_cache)
    rows = spread(rows, PLANE, 4, near_groups()).reshape(256, d)
    rows, values_b, keys_c = lax.optimization_barrier((rows, values_b, keys_c))
    values_c, keys_d, values_d = other_core(value_cache), other_core(keys_b), other_core(values_b)

    got = exchange(project(rows, w_query, w_gate_up), GX).astype(f32)
    total = jnp.sum(got, axis=0)
    hidden = (jax.nn.silu(total[:, :width]) * total[:, width : 2 * width]).astype(bf16)
    hidden = hidden.reshape(2, 2, 4, 2, width).transpose(0, 2, 1, 3, 4).reshape(32, width)
    query = (total[:, 2 * width : 2 * width + qw] + total[:, 2 * width + qw :]).astype(bf16)

    query = query.reshape(2, 2, 4, 2, qw).transpose(0, 2, 1, 3, 4).reshape(16, 2, qw)
    query = exchange(jnp.concatenate([query, query], axis=0), ALL, query_groups())
    place = lax.axis_index(GX)
    block = lax.axis_index("xh") * 4 + lax.axis_index("z") // 2
    sender = jnp.where(place == block, place % 2, (place < block).astype(place.dtype))
    query = lax.dynamic_slice_in_dim(query, sender * 16, 16, 0)
    per_dev = 16 * qw // head_dim
    query = query.transpose(1, 0, 2).reshape(seqs, per_dev, head_dim)
    query = jnp.pad(query, ((0, 0), (0, 8 - per_dev), (0, 0)))
    queries = jnp.concatenate([query, across(query)], axis=1)

    keys = (key_cache, keys_b, keys_c, keys_d)
    values = (value_cache, values_b, values_c, values_d)
    mine, theirs = attend(place, lengths, queries, keys, values, (0, 2, 1, 3))
    attended = finish(mine, across(theirs), queries, new_kv, per_dev)
    return (hidden, attended)


def solution(mesh):
    fine = Mesh(mesh.devices.reshape(4, 2, 2, 8, 8), GX + GY)
    return jax.shard_map(
        body,
        mesh=fine,
        in_specs=(
            P(GY, GX),
            P(GX, GY),
            P(GX, None, GY),
            P(GY, GX, None),
            P(GY, GX, None),
            P(GY, None, None),
            P(GY),
        ),
        out_specs=(P(GX, GY), P(GY, GX)),
        check_vma=False,
    )
```

time: 275 us -> 121 us (0.44)
  the two profiles are of different devices: /device:TPU:1 before, /device:TPU:14 now
where the time goes in v1:
time: 121 us; the launch traced here: 120 us
  starting transfers between devices  80.1 us (66%)
  waiting for transfers between devices  28 us (23%)
  local copies, waits for them, and re-layouts  5.99 us (5%)
  Pallas kernels  4.66 us (4%)
    all_to_all x4, starting transfers between devices, exchange(): return lax.all_to_all(x, axis, 0, 0, axis_index_groups=groups, tiled=True)  49.5 us
    all_to_all x4, waiting for transfers between devices, exchange(): return lax.all_to_all(x, axis, 0, 0, axis_index_groups=groups, tiled=True)  22.2 us
    ppermute x2, starting transfers between devices, across(): return lax.ppermute(x, 'xl', [(i, i ^ 2) for i in range(4)])  13.9 us
    ppermute x4, starting transfers between devices, other_core(): return lax.ppermute(x, 'core', [(0, 1), (1, 0)])  9.5 us
    ppermute x2, starting transfers between devices, beside(): return lax.ppermute(x, 'xl', [(i, i ^ 1) for i in range(4)])  7.24 us
    ppermute x2, waiting for transfers between devices, beside(): return lax.ppermute(x, 'xl', [(i, i ^ 1) for i in range(4)])  3.18 us
    broadcast_in_dim x2, local copies, waits for them, and re-layouts, spread(): return exchange(jnp.broadcast_to(x[None], (n,) + x.shape), axis, groups)  2.69 us
    ppermute x2, waiting for transfers between devices, across(): return lax.ppermute(x, 'xl', [(i, i ^ 2) for i in range(4)])  2.63 us
  transfers between devices with their start and end apart: 12, of which 7 were waited for; matrix products, arithmetic and copies ran while one was open for 1% of the time, Pallas kernels for 0%

profile of v1, /device:TPU:14, one launch (start us, length us, event | category | flops | bytes accessed | tf_op | source)
XLA Modules:
  0.0 119.8 jit_solution(10106034363979562919)
XLA Ops:
  0.6 1.6 %broadcast_in_dim.4 = bf16[32,2,2304]{2,1,0:T(2,128)(2,1)} broadcast(bf16[2,2304]{1,0:T(2,128)(2,1)} %param.7), dimensions={1,2} | broadcast | bytes 304128 | tf_op jit(solution)/shard_map/broadcast_in_dim | solution.py:48
  2.2 27.0 %all-to-all-start = ((bf16[32,2,2304]{2,1,0:T(2,128)(2,1)}), bf16[32,2,2304]{2,1,0:T(2,128)(2,1)S(1)}, u32[]{:S(2)}, u32[]{:S(2)}) async-start(bf16[32,2,2304]{2,1,0:T(2,128)(2,1)} %broadcast_in_dim.4), calls=%async_computation | async-start | bytes 589824 | tf_op jit(solution)/shard_map/all_to_all | solution.py:44
  29.2 3.3 %collective-permute-start = (bf16[2,256,256]{2,1,0:T(8,128)(2,1)}, bf16[2,256,256]{2,1,0:T(8,128)(2,1)S(1)}, u32[]{:S(2)}, u32[]{:S(2)}) collective-permute-start(bf16[2,256,256]{2,1,0:T(8,128)(2,1)} %refs_3_.2), channel_id=1, source_target_pairs={{0,256},{256,0},{512,768},{768,512},{1,257},{257,1},{513,769},{769... | collective-permute-start | bytes 786440 | tf_op jit(solution)/shard_map/ppermute | solution.py:52
  32.6 11.4 %all-to-all-done = bf16[32,2,2304]{2,1,0:T(2,128)(2,1)S(1)} async-done(((bf16[32,2,2304]{2,1,0:T(2,128)(2,1)}), bf16[32,2,2304]{2,1,0:T(2,128)(2,1)S(1)}, u32[]{:S(2)}, u32[]{:S(2)}) %all-to-all-start) | async-done | bytes 294944 | tf_op jit(solution)/shard_map/all_to_all | solution.py:44
  43.9 0.1 reshape.33
  44.0 0.0 collective-permute-done.refs_4_
  44.0 1.1 broadcast_in_dim.5
  45.2 0.0 copy-start.3
  45.2 0.0 copy-start.2
  45.2 0.0 copy-start.1
  45.2 3.8 %all-to-all-start.1 = ((bf16[4,64,2304]{2,1,0:T(8,128)(2,1)}), bf16[4,64,2304]{2,1,0:T(8,128)(2,1)S(1)}, u32[]{:S(2)}, u32[]{:S(2)}) async-start(bf16[4,64,2304]{2,1,0:T(8,128)(2,1)} %broadcast_in_dim.5), calls=%async_computation.1 | async-start | bytes 2359296 | tf_op jit(solution)/shard_map/all_to_all | solution.py:44
  49.0 0.0 copy-done.3
  49.0 3.9 %collective-permute-start.1 = (bf16[2,256,256]{2,1,0:T(8,128)(2,1)S(1)}, bf16[2,256,256]{2,1,0:T(8,128)(2,1)S(1)}, u32[]{:S(2)}, u32[]{:S(2)}) collective-permute-start(bf16[2,256,256]{2,1,0:T(8,128)(2,1)S(1)} %copy-done.3), channel_id=1, source_target_pairs={{0,256},{256,0},{512,768},{768,512},{1,257},{257,1},{513,769},{769... | collective-permute-start | bytes 786440 | tf_op jit(solution)/shard_map/ppermute | solution.py:52
  52.9 0.0 copy-done.2
  52.9 3.1 %collective-permute-start.2 = (bf16[2,256,256]{2,1,0:T(8,128)(2,1)S(1)}, bf16[2,256,256]{2,1,0:T(8,128)(2,1)S(1)}, u32[]{:S(2)}, u32[]{:S(2)}) collective-permute-start(bf16[2,256,256]{2,1,0:T(8,128)(2,1)S(1)} %copy-done.2), channel_id=1, source_target_pairs={{0,128},{128,0},{1,129},{129,1},{2,130},{130,2},{3,131},{131,3},{4... | collective-permute-start | bytes 786440 | tf_op jit(solution)/shard_map/ppermute | solution.py:60
  56.0 3.2 %collective-permute-done.1.refs_8_ = bf16[2,256,256]{2,1,0:T(8,128)(2,1)S(1)} collective-permute-done((bf16[2,256,256]{2,1,0:T(8,128)(2,1)S(1)}, bf16[2,256,256]{2,1,0:T(8,128)(2,1)S(1)}, u32[]{:S(2)}, u32[]{:S(2)}) %collective-permute-start.1) | collective-permute-done | bytes 262176 | tf_op jit(solution)/shard_map/ppermute | solution.py:52
  59.2 0.0 collective-permute-done.2.refs_5_
  59.2 0.1 all-to-all-done.1
  59.3 0.0 copy-done.1
  59.3 0.0 copy-start
  59.3 1.7 %copy-done = bf16[2304,2,288]{0,2,1:T(8,128)(2,1)S(1)} copy-done((bf16[2304,2,288]{0,2,1:T(8,128)(2,1)S(1)}, bf16[2304,2,288]{0,2,1:T(8,128)(2,1)}, u32[]{:S(2)}) %copy-start) | copy-done | bytes 2654232
  61.0 2.3 %shard_map.86 = bf16[8,32,768]{2,1,0:T(8,128)(2,1)} custom-call(bf16[256,2304]{1,0:T(8,128)(2,1)S(1)} %bitcast.13, bf16[576,2304]{1,0:T(8,128)(2,1)S(1)} %bitcast.14, bf16[96,2304]{1,0:T(8,128)(2,1)S(1)} %bitcast.15), custom_call_target="tpu_custom_call" | custom-call | tf_op jit(solution)/shard_map/pallas_call | solution.py:86
  63.3 0.0 copy-start.5
  63.3 6.7 %all-to-all-start.2 = ((bf16[8,32,768]{2,1,0:T(8,128)(2,1)}), bf16[8,32,768]{2,1,0:T(8,128)(2,1)S(1)}, u32[]{:S(2)}, u32[]{:S(2)}) async-start(bf16[8,32,768]{2,1,0:T(8,128)(2,1)} %shard_map.86), calls=%async_computation.2 | async-start | bytes 786432 | tf_op jit(solution)/shard_map/all_to_all | solution.py:44
  70.0 2.0 %collective-permute-start.5 = (bf16[2,256,256]{2,1,0:T(8,128)(2,1)S(1)}, bf16[2,256,256]{2,1,0:T(8,128)(2,1)S(1)}, u32[]{:S(2)}, u32[]{:S(2)}) collective-permute-start(bf16[2,256,256]{2,1,0:T(8,128)(2,1)S(1)} %copy-done.3), channel_id=1, source_target_pairs={{0,128},{128,0},{1,129},{129,1},{2,130},{130,2},{3,131},{131,3},{4... | collective-permute-start | bytes 786440 | tf_op jit(solution)/shard_map/ppermute | solution.py:60
  72.1 2.3 %collective-permute-start.4 = (bf16[2,256,256]{2,1,0:T(8,128)(2,1)S(1)}, bf16[2,256,256]{2,1,0:T(8,128)(2,1)S(1)}, u32[]{:S(2)}, u32[]{:S(2)}) collective-permute-start(bf16[2,256,256]{2,1,0:T(8,128)(2,1)S(1)} %collective-permute-done.refs_4_), channel_id=1, source_target_pairs={{0,128},{128,0},{1,129},{129,1},{2,130},{130,2},{3,131},{131,3},{4... | collective-permute-start | bytes 786440 | tf_op jit(solution)/shard_map/ppermute | solution.py:60
  74.4 2.1 %collective-permute-start.6 = (bf16[2,256,256]{2,1,0:T(8,128)(2,1)S(1)}, bf16[2,256,256]{2,1,0:T(8,128)(2,1)S(1)}, u32[]{:S(2)}, u32[]{:S(2)}) collective-permute-start(bf16[2,256,256]{2,1,0:T(8,128)(2,1)S(1)} %collective-permute-done.1.refs_8_), channel_id=1, source_target_pairs={{0,128},{128,0},{1,129},{129,1},{2,130},{130,2},{3,131},{131,3},{4... | collective-permute-start | bytes 786440 | tf_op jit(solution)/shard_map/ppermute | solution.py:60
  76.4 3.8 %all-to-all-done.2 = bf16[8,32,768]{2,1,0:T(8,128)(2,1)S(1)} async-done(((bf16[8,32,768]{2,1,0:T(8,128)(2,1)}), bf16[8,32,768]{2,1,0:T(8,128)(2,1)S(1)}, u32[]{:S(2)}, u32[]{:S(2)}) %all-to-all-start.2) | async-done | bytes 393248 | tf_op jit(solution)/shard_map/all_to_all | solution.py:44
  80.2 0.1 convert_reduce_fusion
  80.3 0.1 fusion.1
  80.4 0.6 copy.13
  81.0 12.0 %all-to-all-start.3 = ((bf16[32,2,96]{2,1,0:T(2,128)(2,1)}), bf16[32,2,96]{2,1,0:T(2,128)(2,1)S(1)}, u32[]{:S(2)}, u32[]{:S(2)}) async-start(bf16[32,2,96]{2,1,0:T(2,128)(2,1)} %copy.13), calls=%async_computation.3 | async-start | bytes 32768 | tf_op jit(solution)/shard_map/all_to_all | solution.py:44
  93.0 7.0 %all-to-all-done.3 = bf16[32,2,96]{2,1,0:T(2,128)(2,1)S(1)} async-done(((bf16[32,2,96]{2,1,0:T(2,128)(2,1)}), bf16[32,2,96]{2,1,0:T(2,128)(2,1)S(1)}, u32[]{:S(2)}, u32[]{:S(2)}) %all-to-all-start.3) | async-done | bytes 12320 | tf_op jit(solution)/shard_map/all_to_all | solution.py:44
  100.0 0.1 reshape.41
  100.1 9.1 %collective-permute-start.3 = (bf16[2,8,256]{2,1,0:T(8,128)(2,1)S(1)}, bf16[2,8,256]{2,1,0:T(8,128)(2,1)S(1)}, u32[]{:S(2)}, u32[]{:S(2)}) collective-permute-start(bf16[2,8,256]{2,1,0:T(8,128)(2,1)S(1)} %pad.4), channel_id=1, source_target_pairs={{0,512},{256,768},{512,0},{768,256},{1,513},{257,769},{513,1},{769... | collective-permute-start | bytes 24584 | tf_op jit(solution)/shard_map/ppermute | solution.py:56
  109.2 1.6 %collective-permute-done.3 = bf16[2,8,256]{2,1,0:T(8,128)(2,1)S(1)} collective-permute-done((bf16[2,8,256]{2,1,0:T(8,128)(2,1)S(1)}, bf16[2,8,256]{2,1,0:T(8,128)(2,1)S(1)}, u32[]{:S(2)}, u32[]{:S(2)}) %collective-permute-start.3) | collective-permute-done | bytes 8224 | tf_op jit(solution)/shard_map/ppermute | solution.py:56
  110.8 0.0 collective-permute-done.5.refs_9_
  110.8 0.0 collective-permute-done.4.refs_6_
  110.8 0.0 collective-permute-done.6.refs_10_
  110.8 0.0 copy-done.5
  110.8 0.0 copy-start.4
  110.8 1.5 %shard_map.87 = (f32[2,8,384]{2,1,0:T(8,128)S(1)}, f32[2,8,384]{2,1,0:T(8,128)S(1)}) custom-call(s32[1]{0:T(128)} %bitcast.5.refs_0_, s32[2]{0:T(128)S(1)} %copy-done.5, bf16[2,16,256]{2,1,0:T(8,128)(2,1)S(1)} %pad_maximum_fusion.1.refs_2_, bf16[2,256,256]{2,1,0:T(8,128)(2,1)S(1)} %copy-done.2, bf16[2,256,256]{2,1,0:T(8,128)(2,1)S(1)} %collective-permute-done.refs_4_, ...), custom_call_target="tpu_custom_call" | custom-call | tf_op jit(solution)/shard_map/pallas_call | solution.py:132
  112.4 4.8 %collective-permute-start.7 = (f32[2,8,384]{2,1,0:T(8,128)S(1)}, f32[2,8,384]{2,1,0:T(8,128)S(1)}, u32[]{:S(2)}, u32[]{:S(2)}) collective-permute-start(f32[2,8,384]{2,1,0:T(8,128)S(1)} %get-tuple-element.15), channel_id=1, source_target_pairs={{0,512},{256,768},{512,0},{768,256},{1,513},{257,769},{513,1},{769... | collective-permute-start | bytes 73736 | tf_op jit(solution)/shard_map/ppermute | solution.py:56
  117.2 0.1 fusion
  117.3 0.6 reshape.37
  118.0 1.0 collective-permute-done.7.refs_1_
  119.0 0.0 copy-done.4
  119.0 0.9 shard_map.88
  (8 shorter events, 0.1 us)
Async XLA Ops:
  2.2 41.7 %all-to-all-start = ((bf16[32,2,2304]{2,1,0:T(2,128)(2,1)}), bf16[32,2,2304]{2,1,0:T(2,128)(2,1)S(1)}, u32[]{:S(2)}, u32[]{:S(2)}) async-start(bf16[32,2,2304]{2,1,0:T(2,128)(2,1)} %broadcast_in_dim.4), calls=%async_computation | async-start | bytes 589824 | tf_op jit(solution)/shard_map/all_to_all | solution.py:44
  29.2 14.8 %collective-permute-start = (bf16[2,256,256]{2,1,0:T(8,128)(2,1)}, bf16[2,256,256]{2,1,0:T(8,128)(2,1)S(1)}, u32[]{:S(2)}, u32[]{:S(2)}) collective-permute-start(bf16[2,256,256]{2,1,0:T(8,128)(2,1)} %refs_3_.2), channel_id=1, source_target_pairs={{0,256},{256,0},{512,768},{768,512},{1,257},{257,1},{513,769},{769... | collective-permute-start | bytes 786440 | tf_op jit(solution)/shard_map/ppermute | solution.py:52
  45.2 3.8 %copy-start.3 = (bf16[2,256,256]{2,1,0:T(8,128)(2,1)S(1)}, bf16[2,256,256]{2,1,0:T(8,128)(2,1)}, u32[]{:S(2)}) copy-start(bf16[2,256,256]{2,1,0:T(8,128)(2,1)} %refs_7_.1) | copy-start | bytes 786436
  45.2 7.7 %copy-start.2 = (bf16[2,256,256]{2,1,0:T(8,128)(2,1)S(1)}, bf16[2,256,256]{2,1,0:T(8,128)(2,1)}, u32[]{:S(2)}) copy-start(bf16[2,256,256]{2,1,0:T(8,128)(2,1)} %refs_3_.2) | copy-start | bytes 786436
  45.2 14.1 %copy-start.1 = (bf16[2304,96]{0,1:T(8,128)(2,1)S(1)}, bf16[2304,96]{0,1:T(8,128)(2,1)}, u32[]{:S(2)}) copy-start(bf16[2304,96]{0,1:T(8,128)(2,1)} %param.8) | copy-start | bytes 1327108
  45.2 14.1 %all-to-all-start.1 = ((bf16[4,64,2304]{2,1,0:T(8,128)(2,1)}), bf16[4,64,2304]{2,1,0:T(8,128)(2,1)S(1)}, u32[]{:S(2)}, u32[]{:S(2)}) async-start(bf16[4,64,2304]{2,1,0:T(8,128)(2,1)} %broadcast_in_dim.5), calls=%async_computation.1 | async-start | bytes 2359296 | tf_op jit(solution)/shard_map/all_to_all | solution.py:44
  49.0 10.2 %collective-permute-start.1 = (bf16[2,256,256]{2,1,0:T(8,128)(2,1)S(1)}, bf16[2,256,256]{2,1,0:T(8,128)(2,1)S(1)}, u32[]{:S(2)}, u32[]{:S(2)}) collective-permute-start(bf16[2,256,256]{2,1,0:T(8,128)(2,1)S(1)} %copy-done.3), channel_id=1, source_target_pairs={{0,256},{256,0},{512,768},{768,512},{1,257},{257,1},{513,769},{769... | collective-permute-start | bytes 786440 | tf_op jit(solution)/shard_map/ppermute | solution.py:52
  52.9 6.3 %collective-permute-start.2 = (bf16[2,256,256]{2,1,0:T(8,128)(2,1)S(1)}, bf16[2,256,256]{2,1,0:T(8,128)(2,1)S(1)}, u32[]{:S(2)}, u32[]{:S(2)}) collective-permute-start(bf16[2,256,256]{2,1,0:T(8,128)(2,1)S(1)} %copy-done.2), channel_id=1, source_target_pairs={{0,128},{128,0},{1,129},{129,1},{2,130},{130,2},{3,131},{131,3},{4... | collective-permute-start | bytes 786440 | tf_op jit(solution)/shard_map/ppermute | solution.py:60
  59.3 1.8 %copy-start = (bf16[2304,2,288]{0,2,1:T(8,128)(2,1)S(1)}, bf16[2304,2,288]{0,2,1:T(8,128)(2,1)}, u32[]{:S(2)}) copy-start(bf16[2304,2,288]{0,2,1:T(8,128)(2,1)} %param.9) | copy-start | bytes 7962628
  63.3 47.5 %copy-start.5 = (s32[2]{0:T(128)S(1)}, s32[2]{0:T(128)}, u32[]{:S(2)}) copy-start(s32[2]{0:T(128)} %refs_1_.1) | copy-start | bytes 28
  63.3 16.9 %all-to-all-start.2 = ((bf16[8,32,768]{2,1,0:T(8,128)(2,1)}), bf16[8,32,768]{2,1,0:T(8,128)(2,1)S(1)}, u32[]{:S(2)}, u32[]{:S(2)}) async-start(bf16[8,32,768]{2,1,0:T(8,128)(2,1)} %shard_map.86), calls=%async_computation.2 | async-start | bytes 786432 | tf_op jit(solution)/shard_map/all_to_all | solution.py:44
  70.0 40.8 %collective-permute-start.5 = (bf16[2,256,256]{2,1,0:T(8,128)(2,1)S(1)}, bf16[2,256,256]{2,1,0:T(8,128)(2,1)S(1)}, u32[]{:S(2)}, u32[]{:S(2)}) collective-permute-start(bf16[2,256,256]{2,1,0:T(8,128)(2,1)S(1)} %copy-done.3), channel_id=1, source_target_pairs={{0,128},{128,0},{1,129},{129,1},{2,130},{130,2},{3,131},{131,3},{4... | collective-permute-start | bytes 786440 | tf_op jit(solution)/shard_map/ppermute | solution.py:60
  72.1 38.7 %collective-permute-start.4 = (bf16[2,256,256]{2,1,0:T(8,128)(2,1)S(1)}, bf16[2,256,256]{2,1,0:T(8,128)(2,1)S(1)}, u32[]{:S(2)}, u32[]{:S(2)}) collective-permute-start(bf16[2,256,256]{2,1,0:T(8,128)(2,1)S(1)} %collective-permute-done.refs_4_), channel_id=1, source_target_pairs={{0,128},{128,0},{1,129},{129,1},{2,130},{130,2},{3,131},{131,3},{4... | collective-permute-start | bytes 786440 | tf_op jit(solution)/shard_map/ppermute | solution.py:60
  74.4 36.4 %collective-permute-start.6 = (bf16[2,256,256]{2,1,0:T(8,128)(2,1)S(1)}, bf16[2,256,256]{2,1,0:T(8,128)(2,1)S(1)}, u32[]{:S(2)}, u32[]{:S(2)}) collective-permute-start(bf16[2,256,256]{2,1,0:T(8,128)(2,1)S(1)} %collective-permute-done.1.refs_8_), channel_id=1, source_target_pairs={{0,128},{128,0},{1,129},{129,1},{2,130},{130,2},{3,131},{131,3},{4... | collective-permute-start | bytes 786440 | tf_op jit(solution)/shard_map/ppermute | solution.py:60
  81.0 19.0 %all-to-all-start.3 = ((bf16[32,2,96]{2,1,0:T(2,128)(2,1)}), bf16[32,2,96]{2,1,0:T(2,128)(2,1)S(1)}, u32[]{:S(2)}, u32[]{:S(2)}) async-start(bf16[32,2,96]{2,1,0:T(2,128)(2,1)} %copy.13), calls=%async_computation.3 | async-start | bytes 32768 | tf_op jit(solution)/shard_map/all_to_all | solution.py:44
  100.1 10.7 %collective-permute-start.3 = (bf16[2,8,256]{2,1,0:T(8,128)(2,1)S(1)}, bf16[2,8,256]{2,1,0:T(8,128)(2,1)S(1)}, u32[]{:S(2)}, u32[]{:S(2)}) collective-permute-start(bf16[2,8,256]{2,1,0:T(8,128)(2,1)S(1)} %pad.4), channel_id=1, source_target_pairs={{0,512},{256,768},{512,0},{768,256},{1,513},{257,769},{513,1},{769... | collective-permute-start | bytes 24584 | tf_op jit(solution)/shard_map/ppermute | solution.py:56
  110.8 8.2 %copy-start.4 = (bf16[2,2,256]{2,1,0:T(2,128)(2,1)S(1)}, bf16[2,2,256]{2,1,0:T(2,128)(2,1)}, u32[]{:S(2)}) copy-start(bf16[2,2,256]{2,1,0:T(2,128)(2,1)} %refs_3_.3) | copy-start | bytes 6148
  112.4 6.6 %collective-permute-start.7 = (f32[2,8,384]{2,1,0:T(8,128)S(1)}, f32[2,8,384]{2,1,0:T(8,128)S(1)}, u32[]{:S(2)}, u32[]{:S(2)}) collective-permute-start(f32[2,8,384]{2,1,0:T(8,128)S(1)} %get-tuple-element.15), channel_id=1, source_target_pairs={{0,512},{256,768},{512,0},{768,256},{1,513},{257,769},{513,1},{769... | collective-permute-start | bytes 73736 | tf_op jit(solution)/shard_map/ppermute | solution.py:56

commit v2 on v1

--- a/solution.py
+++ b/solution.py
@@ -33,11 +33,20 @@
 
 
 def query_groups():
-    def half(g, h):
-        return [g * 128 + h * 16 + i for i in range(16)]
-
-    pairs = [(g, h) for g in range(8) for h in range(g + 1, 8)]
-    return [half(g, h) + half(h, g) for g, h in pairs] + [half(g, g) + half(g + 1, g + 1) for g in range(0, 8, 2)]
+    def half(g, h, lo):
+        return [g * 128 + h * 16 + lo * 8 + y for y in range(8)]
+
+    groups = []
+    for lo in range(2):
+        groups += [half(g, h, lo) + half(h, g, lo) for g in range(8) for h in range(g + 1, 8)]
+        groups += [half(g, g, lo) + half(g + 1, g + 1, lo) for g in range(0, 8, 2)]
+    return groups
+
+
+def column_groups():
+    return [
+        [(hi * 2 + xlo) * 8 + zh * 2 + zlo for hi in range(2) for zlo in range(2)] for xlo in range(2) for zh in range(4)
+    ]
 
 
 def exchange(x, axis, groups=None):
@@ -64,31 +73,29 @@
 LIMIT = pltpu.CompilerParams(vmem_limit_bytes=16 * 2**20)
 
 
-def project_kernel(x_ref, wg_ref, wq_ref, out_ref, acc_ref):
-    x = x_ref[...]
-    width, qw = wg_ref.shape[0], wq_ref.shape[0]
-    gate_up = lax.dot_general(x, wg_ref[...], NT, preferred_element_type=jnp.float32)
-    query = lax.dot_general(x, wq_ref[...], NT, preferred_element_type=jnp.float32)
+def project_kernel(qw, x_ref, w_ref, out_ref, acc_ref):
+    full = lax.dot_general(x_ref[...], w_ref[...], NT, preferred_element_type=jnp.float32)
+    width = full.shape[1]
+    query = full[:, width - qw :]
+    low = query - query.astype(jnp.bfloat16).astype(jnp.float32)
     for p in range(4):
         rows = slice(p * 64, p * 64 + 64)
-        acc_ref[:, p * 8 : p * 8 + 8, :width] = gate_up[rows].reshape(8, 8, width)
-        part = query[rows].reshape(8, 8, qw)
-        acc_ref[:, p * 8 : p * 8 + 8, width : width + qw] = part
-        acc_ref[:, p * 8 : p * 8 + 8, width + qw :] = part - part.astype(jnp.bfloat16).astype(jnp.float32)
+        acc_ref[:, p * 8 : p * 8 + 8, :width] = full[rows].reshape(8, 8, width)
+        acc_ref[:, p * 8 : p * 8 + 8, width:] = low[rows].reshape(8, 8, qw)
     out_ref[...] = acc_ref[...].astype(jnp.bfloat16)
 
 
-def project(rows, w_query, w_gate_up):
-    d, _, width = w_gate_up.shape
-    wg = w_gate_up.transpose(1, 2, 0).reshape(2 * width, d)
-    wq = w_query.T
-    shape = (8, rows.shape[0] // 8, 2 * width + 2 * wq.shape[0])
+def project(rows, weights, qw):
+    def kernel(*refs):
+        project_kernel(qw, *refs)
+
+    shape = (8, rows.shape[0] // 8, weights.shape[0] + qw)
     return pl.pallas_call(
-        project_kernel,
+        kernel,
         out_shape=jax.ShapeDtypeStruct(shape, jnp.bfloat16),
         scratch_shapes=[pltpu.VMEM(shape, jnp.float32)],
         compiler_params=LIMIT,
-    )(rows, wg, wq)
+    )(rows, weights)
 
 
 def attend_kernel(order, place_ref, lengths_ref, q_ref, *refs):
@@ -175,30 +182,36 @@
     d, width, qw = tokens.shape[1], w_gate_up.shape[2], w_query.shape[1]
     seqs, _, head_dim = key_cache.shape
 
-    keys_b = beside(key_cache)
+    keys_b, keys_c = beside(key_cache), other_core(key_cache)
+    weights = jnp.concatenate([w_gate_up.transpose(1, 2, 0).reshape(2 * width, d), w_query.T], axis=0)
     rows = spread(tokens, LATTICE, 32, far_groups()).reshape(64, d)
-    rows, keys_b = lax.optimization_barrier((rows, keys_b))
-    values_b, keys_c = beside(value_cache), other_core(key_cache)
+    rows, weights, keys_b, keys_c = lax.optimization_barrier((rows, weights, keys_b, keys_c))
+    values_b = beside(value_cache)
     rows = spread(rows, PLANE, 4, near_groups()).reshape(256, d)
-    rows, values_b, keys_c = lax.optimization_barrier((rows, values_b, keys_c))
+    rows, values_b = lax.optimization_barrier((rows, values_b))
     values_c, keys_d, values_d = other_core(value_cache), other_core(keys_b), other_core(values_b)
 
-    got = exchange(project(rows, w_query, w_gate_up), GX).astype(f32)
+    got = exchange(project(rows, weights, qw), GX).astype(f32)
     total = jnp.sum(got, axis=0)
     hidden = (jax.nn.silu(total[:, :width]) * total[:, width : 2 * width]).astype(bf16)
     hidden = hidden.reshape(2, 2, 4, 2, width).transpose(0, 2, 1, 3, 4).reshape(32, width)
     query = (total[:, 2 * width : 2 * width + qw] + total[:, 2 * width + qw :]).astype(bf16)
 
-    query = query.reshape(2, 2, 4, 2, qw).transpose(0, 2, 1, 3, 4).reshape(16, 2, qw)
+    query = query.reshape(2, 2, 4, 2, qw).transpose(2, 1, 0, 3, 4).reshape(8, 4, qw)
     query = exchange(jnp.concatenate([query, query], axis=0), ALL, query_groups())
     place = lax.axis_index(GX)
     block = lax.axis_index("xh") * 4 + lax.axis_index("z") // 2
     sender = jnp.where(place == block, place % 2, (place < block).astype(place.dtype))
-    query = lax.dynamic_slice_in_dim(query, sender * 16, 16, 0)
+    query = lax.dynamic_slice_in_dim(query, sender * 8, 8, 0)
+    query = query.reshape(8, 2, seqs, qw).transpose(1, 2, 0, 3).reshape(2, seqs, 8 * qw)
+    query = jnp.concatenate([query, query], axis=0)
+    query = exchange(query, ("xl", "z"), column_groups())
     per_dev = 16 * qw // head_dim
-    query = query.transpose(1, 0, 2).reshape(seqs, per_dev, head_dim)
-    query = jnp.pad(query, ((0, 0), (0, 8 - per_dev), (0, 0)))
-    queries = jnp.concatenate([query, across(query)], axis=1)
+    query = query.reshape(2, 2, seqs, 8 * qw).transpose(0, 2, 1, 3).reshape(2, seqs, per_dev, head_dim)
+    query = jnp.pad(query, ((0, 0), (0, 0), (0, 8 - per_dev), (0, 0)))
+    upper = lax.axis_index("xl") >= 2
+    own, other = jnp.where(upper, query[1], query[0]), jnp.where(upper, query[0], query[1])
+    queries = jnp.concatenate([own, other], axis=1)
 
     keys = (key_cache, keys_b, keys_c, keys_d)
     values = (value_cache, values_b, values_c, values_d)

time: 121 us -> 127 us (1.050)
  blocking collectives: 0 us -> 15.3 us
  waiting for transfers between devices: 28 us -> 19.8 us
  starting transfers between devices: 80.1 us -> 73.7 us
  other arithmetic: 0.22 us -> 2.95 us
  local copies, waits for them, and re-layouts: 5.99 us -> 7.83 us
    all_to_all x0 -> x1, blocking collectives: none -> 15.3 us  [exchange(): return lax.all_to_all(x, axis, 0, 0, axis_index_groups=groups, tiled=True)]
    all_to_all x4, waiting for transfers between devices: 22.2 us -> 12.3 us  [exchange(): return lax.all_to_all(x, axis, 0, 0, axis_index_groups=groups, tiled=True)]
    ppermute x2 -> x1, starting transfers between devices: 13.9 us -> 4.24 us  [across(): return lax.ppermute(x, 'xl', [(i, i ^ 2) for i in range(4)])]
    all_to_all x4, starting transfers between devices: 49.5 us -> 54.1 us  [exchange(): return lax.all_to_all(x, axis, 0, 0, axis_index_groups=groups, tiled=True)]
    ppermute x2, waiting for transfers between devices: 3.18 us -> 5.91 us  [beside(): return lax.ppermute(x, 'xl', [(i, i ^ 1) for i in range(4)])]
    concatenate x1 -> x3, other arithmetic: 0.01 us -> 2.72 us  [the longest x1 2.1 us: body(): jnp.concatenate([w_gate_up.transpose(1, 2, 0).reshape(2 * width, d), w_qu...]
    reshape x1, local copies, waits for them, and re-layouts: 0.11 us -> 1.78 us  [body(): rows = spread(tokens, LATTICE, 32, far_groups()).reshape(64, d)]
    ppermute x4, starting transfers between devices: 9.5 us -> 8.16 us  [other_core(): return lax.ppermute(x, 'core', [(0, 1), (1, 0)])]
  transfers between devices with their start and end apart: 12 -> 11, of which waited for: 7 -> 6; matrix products, arithmetic and copies ran while one was open for 1% -> 4% of each run, Pallas kernels for 0% -> 0%
where the time goes in v2:
time: 127 us; the launch traced here: 126 us
  starting transfers between devices  73.7 us (58%)
  waiting for transfers between devices  19.8 us (16%)
  blocking collectives  15.3 us (12%)
  local copies, waits for them, and re-layouts  7.83 us (6%)
  Pallas kernels  5.51 us (4%)
  other arithmetic  2.95 us (2%)
    all_to_all x4, starting transfers between devices, exchange(): return lax.all_to_all(x, axis, 0, 0, axis_index_groups=groups, tiled=True)  54.1 us
    all_to_all x1, blocking collectives, exchange(): return lax.all_to_all(x, axis, 0, 0, axis_index_groups=groups, tiled=True)  15.3 us
    all_to_all x4, waiting for transfers between devices, exchange(): return lax.all_to_all(x, axis, 0, 0, axis_index_groups=groups, tiled=True)  12.3 us
    ppermute x4, starting transfers between devices, other_core(): return lax.ppermute(x, 'core', [(0, 1), (1, 0)])  8.16 us
    ppermute x2, starting transfers between devices, beside(): return lax.ppermute(x, 'xl', [(i, i ^ 1) for i in range(4)])  7.16 us
    ppermute x2, waiting for transfers between devices, beside(): return lax.ppermute(x, 'xl', [(i, i ^ 1) for i in range(4)])  5.91 us
    ppermute x1, starting transfers between devices, across(): return lax.ppermute(x, 'xl', [(i, i ^ 2) for i in range(4)])  4.24 us
    broadcast_in_dim x2, local copies, waits for them, and re-layouts, spread(): return exchange(jnp.broadcast_to(x[None], (n,) + x.shape), axis, groups)  3.65 us
  transfers between devices with their start and end apart: 11, of which 6 were waited for; matrix products, arithmetic and copies ran while one was open for 4% of the time, Pallas kernels for 0%

profile of v2, /device:TPU:14, one launch (start us, length us, event | category | flops | bytes accessed | tf_op | source)
XLA Modules:
  0.0 126.0 jit_solution(1965845727367786426)
XLA Ops:
  0.6 1.6 %broadcast_in_dim.4 = bf16[32,2,2304]{2,1,0:T(2,128)(2,1)} broadcast(bf16[2,2304]{1,0:T(2,128)(2,1)} %param.7), dimensions={1,2} | broadcast | bytes 304128 | tf_op jit(solution)/shard_map/broadcast_in_dim | solution.py:57
  2.2 27.1 %all-to-all-start = ((bf16[32,2,2304]{2,1,0:T(2,128)(2,1)}), bf16[32,2,2304]{2,1,0:T(2,128)(2,1)}, u32[]{:S(2)}, u32[]{:S(2)}) async-start(bf16[32,2,2304]{2,1,0:T(2,128)(2,1)} %broadcast_in_dim.4), calls=%async_computation | async-start | bytes 589824 | tf_op jit(solution)/shard_map/all_to_all | solution.py:53
  29.3 3.3 %collective-permute-start = (bf16[2,256,256]{2,1,0:T(8,128)(2,1)}, bf16[2,256,256]{2,1,0:T(8,128)(2,1)}, u32[]{:S(2)}, u32[]{:S(2)}) collective-permute-start(bf16[2,256,256]{2,1,0:T(8,128)(2,1)} %refs_3_.2), channel_id=1, source_target_pairs={{0,256},{256,0},{512,768},{768,512},{1,257},{257,1},{513,769},{769... | collective-permute-start | bytes 786440 | tf_op jit(solution)/shard_map/ppermute | solution.py:61
  32.6 1.9 %collective-permute-start.1 = (bf16[2,256,256]{2,1,0:T(8,128)(2,1)}, bf16[2,256,256]{2,1,0:T(8,128)(2,1)}, u32[]{:S(2)}, u32[]{:S(2)}) collective-permute-start(bf16[2,256,256]{2,1,0:T(8,128)(2,1)} %refs_3_.2), channel_id=1, source_target_pairs={{0,128},{128,0},{1,129},{129,1},{2,130},{130,2},{3,131},{131,3},{4... | collective-permute-start | bytes 786440 | tf_op jit(solution)/shard_map/ppermute | solution.py:69
  34.5 2.1 %pad_maximum_fusion.refs_1_ = bf16[672,2304]{1,0:T(8,128)(2,1)S(1)} fusion(bf16[96,2304]{1,0:T(8,128)(2,1)} %bitcast.24, bf16[576,2304]{1,0:T(8,128)(2,1)} %bitcast.23), kind=kLoop, calls=%fused_computation | loop fusion | flops 6193152 | bytes 6193152 | tf_op jit(solution)/shard_map/concatenate | solution.py:186
  36.6 0.0 copy-start.1
  36.7 7.4 %all-to-all-done = bf16[32,2,2304]{2,1,0:T(2,128)(2,1)} async-done(((bf16[32,2,2304]{2,1,0:T(2,128)(2,1)}), bf16[32,2,2304]{2,1,0:T(2,128)(2,1)}, u32[]{:S(2)}, u32[]{:S(2)}) %all-to-all-start) | async-done | bytes 294944 | tf_op jit(solution)/shard_map/all_to_all | solution.py:53
  44.0 1.8 %reshape.46 = bf16[64,2304]{1,0:T(8,128)(2,1)} reshape(bf16[32,2,2304]{2,1,0:T(2,128)(2,1)} %all-to-all-done) | data formatting | bytes 589824 | tf_op jit(solution)/shard_map/reshape | solution.py:187
  45.8 0.0 collective-permute-done.refs_4_
  45.8 0.0 collective-permute-done.1.refs_5_
  45.8 2.1 %broadcast_in_dim.5 = bf16[4,64,2304]{2,1,0:T(8,128)(2,1)} broadcast(bf16[64,2304]{1,0:T(8,128)(2,1)} %reshape.46), dimensions={1,2} | broadcast | bytes 1474560 | tf_op jit(solution)/shard_map/broadcast_in_dim | solution.py:57
  47.9 4.3 %all-to-all-start.1 = ((bf16[4,64,2304]{2,1,0:T(8,128)(2,1)}), bf16[4,64,2304]{2,1,0:T(8,128)(2,1)}, u32[]{:S(2)}, u32[]{:S(2)}) async-start(bf16[4,64,2304]{2,1,0:T(8,128)(2,1)} %broadcast_in_dim.5), calls=%async_computation.1 | async-start | bytes 2359296 | tf_op jit(solution)/shard_map/all_to_all | solution.py:53
  52.2 0.0 copy-done.1
  52.2 3.8 %collective-permute-start.2 = (bf16[2,256,256]{2,1,0:T(8,128)(2,1)S(1)}, bf16[2,256,256]{2,1,0:T(8,128)(2,1)}, u32[]{:S(2)}, u32[]{:S(2)}) collective-permute-start(bf16[2,256,256]{2,1,0:T(8,128)(2,1)S(1)} %copy-done.1), channel_id=1, source_target_pairs={{0,256},{256,0},{512,768},{768,512},{1,257},{257,1},{513,769},{769... | collective-permute-start | bytes 786440 | tf_op jit(solution)/shard_map/ppermute | solution.py:61
  56.0 5.9 %collective-permute-done.2.refs_8_ = bf16[2,256,256]{2,1,0:T(8,128)(2,1)} collective-permute-done((bf16[2,256,256]{2,1,0:T(8,128)(2,1)S(1)}, bf16[2,256,256]{2,1,0:T(8,128)(2,1)}, u32[]{:S(2)}, u32[]{:S(2)}) %collective-permute-start.2) | collective-permute-done | bytes 262176 | tf_op jit(solution)/shard_map/ppermute | solution.py:61
  61.9 0.8 all-to-all-done.1
  62.7 0.0 copy-start
  62.7 0.0 copy-start.4
  62.7 2.6 %shard_map.86 = bf16[8,32,768]{2,1,0:T(8,128)(2,1)S(1)} custom-call(bf16[256,2304]{1,0:T(8,128)(2,1)} %bitcast.3.refs_0_, bf16[672,2304]{1,0:T(8,128)(2,1)S(1)} %pad_maximum_fusion.refs_1_), custom_call_target="tpu_custom_call" | custom-call | tf_op jit(solution)/shard_map/pallas_call | solution.py:93
  65.3 0.0 copy-start.3
  65.3 15.3 %all_to_all.25 = bf16[8,32,768]{2,1,0:T(8,128)(2,1)S(1)} all-to-all(bf16[8,32,768]{2,1,0:T(8,128)(2,1)S(1)} %shard_map.86), channel_id=1, replica_groups=mesh['xl'=4,'core'=2,'xh'=2,'z'=8,'y'=8] {'xl','core'}, dimensions={0} | all-to-all | bytes 786432 | tf_op jit(solution)/shard_map/all_to_all | solution.py:53
  80.7 0.1 convert_reduce_fusion
  80.7 0.1 fusion.1
  80.8 0.6 copy.19
  81.4 10.7 %all-to-all-start.3 = ((bf16[16,4,96]{2,1,0:T(4,128)(2,1)}), bf16[16,4,96]{2,1,0:T(4,128)(2,1)S(1)}, u32[]{:S(2)}, u32[]{:S(2)}) async-start(bf16[16,4,96]{2,1,0:T(4,128)(2,1)} %copy.19), calls=%async_computation.3 | async-start | bytes 32768 | tf_op jit(solution)/shard_map/all_to_all | solution.py:53
  92.2 1.9 %collective-permute-start.4 = (bf16[2,256,256]{2,1,0:T(8,128)(2,1)}, bf16[2,256,256]{2,1,0:T(8,128)(2,1)S(1)}, u32[]{:S(2)}, u32[]{:S(2)}) collective-permute-start(bf16[2,256,256]{2,1,0:T(8,128)(2,1)} %refs_7_.1), channel_id=1, source_target_pairs={{0,128},{128,0},{1,129},{129,1},{2,130},{130,2},{3,131},{131,3},{4... | collective-permute-start | bytes 786440 | tf_op jit(solution)/shard_map/ppermute | solution.py:69
  94.1 2.4 %collective-permute-start.3 = (bf16[2,256,256]{2,1,0:T(8,128)(2,1)}, bf16[2,256,256]{2,1,0:T(8,128)(2,1)S(1)}, u32[]{:S(2)}, u32[]{:S(2)}) collective-permute-start(bf16[2,256,256]{2,1,0:T(8,128)(2,1)} %collective-permute-done.refs_4_), channel_id=1, source_target_pairs={{0,128},{128,0},{1,129},{129,1},{2,130},{130,2},{3,131},{131,3},{4... | collective-permute-start | bytes 786440 | tf_op jit(solution)/shard_map/ppermute | solution.py:69
  96.5 1.9 %collective-permute-start.5 = (bf16[2,256,256]{2,1,0:T(8,128)(2,1)}, bf16[2,256,256]{2,1,0:T(8,128)(2,1)S(1)}, u32[]{:S(2)}, u32[]{:S(2)}) collective-permute-start(bf16[2,256,256]{2,1,0:T(8,128)(2,1)} %collective-permute-done.2.refs_8_), channel_id=1, source_target_pairs={{0,128},{128,0},{1,129},{129,1},{2,130},{130,2},{3,131},{131,3},{4... | collective-permute-start | bytes 786440 | tf_op jit(solution)/shard_map/ppermute | solution.py:69
  98.5 0.8 all-to-all-done.3
  99.3 0.1 reshape.55
  99.4 0.6 pad_maximum_fusion.3
  100.0 12.0 %all-to-all-start.4 = ((bf16[4,2,768]{2,1,0:T(2,128)(2,1)}), bf16[4,2,768]{2,1,0:T(2,128)(2,1)S(1)}, u32[]{:S(2)}, u32[]{:S(2)}) async-start(bf16[4,2,768]{2,1,0:T(2,128)(2,1)} %pad_maximum_fusion.3), calls=%async_computation.4 | async-start | bytes 24576 | tf_op jit(solution)/shard_map/all_to_all | solution.py:53
  112.1 3.3 %all-to-all-done.4 = bf16[4,2,768]{2,1,0:T(2,128)(2,1)S(1)} async-done(((bf16[4,2,768]{2,1,0:T(2,128)(2,1)}), bf16[4,2,768]{2,1,0:T(2,128)(2,1)S(1)}, u32[]{:S(2)}, u32[]{:S(2)}) %all-to-all-start.4) | async-done | bytes 12320 | tf_op jit(solution)/shard_map/all_to_all | solution.py:53
  115.4 0.0 collective-permute-done.4.refs_9_
  115.4 0.0 collective-permute-done.3.refs_6_
  115.4 0.0 collective-permute-done.5.refs_10_
  115.4 0.0 copy-done
  115.4 0.0 copy-done.4
  115.5 0.0 copy-start.2
  115.5 0.9 copy-done.2
  116.4 2.1 %shard_map.87 = (f32[2,8,384]{2,1,0:T(8,128)S(1)}, f32[2,8,384]{2,1,0:T(8,128)S(1)}) custom-call(s32[1]{0:T(128)} %bitcast.5.refs_0_, s32[2]{0:T(128)S(1)} %copy-done.4, bf16[2,16,256]{2,1,0:T(8,128)(2,1)S(1)} %pad_maximum_fusion.2.refs_2_, bf16[2,256,256]{2,1,0:T(8,128)(2,1)S(1)} %copy-done, bf16[2,256,256]{2,1,0:T(8,128)(2,1)} %collective-permute-done.refs_4_, ...), custom_call_target="tpu_custom_call" | custom-call | tf_op jit(solution)/shard_map/pallas_call | solution.py:139
  118.5 4.2 %collective-permute-start.6 = (f32[2,8,384]{2,1,0:T(8,128)S(1)}, f32[2,8,384]{2,1,0:T(8,128)S(1)}, u32[]{:S(2)}, u32[]{:S(2)}) collective-permute-start(f32[2,8,384]{2,1,0:T(8,128)S(1)} %get-tuple-element.17), channel_id=1, source_target_pairs={{0,512},{256,768},{512,0},{768,256},{1,513},{257,769},{513,1},{769... | collective-permute-start | bytes 73736 | tf_op jit(solution)/shard_map/ppermute | solution.py:65
  122.8 0.1 fusion
  122.9 0.6 reshape.50
  123.5 1.6 %collective-permute-done.6.refs_1_ = f32[2,8,384]{2,1,0:T(8,128)S(1)} collective-permute-done((f32[2,8,384]{2,1,0:T(8,128)S(1)}, f32[2,8,384]{2,1,0:T(8,128)S(1)}, u32[]{:S(2)}, u32[]{:S(2)}) %collective-permute-start.6) | collective-permute-done | bytes 24608 | tf_op jit(solution)/shard_map/ppermute | solution.py:65
  125.1 0.0 copy-done.3
  125.1 0.9 shard_map.88
  (10 shorter events, 0.1 us)
Async XLA Ops:
  2.2 41.8 %all-to-all-start = ((bf16[32,2,2304]{2,1,0:T(2,128)(2,1)}), bf16[32,2,2304]{2,1,0:T(2,128)(2,1)}, u32[]{:S(2)}, u32[]{:S(2)}) async-start(bf16[32,2,2304]{2,1,0:T(2,128)(2,1)} %broadcast_in_dim.4), calls=%async_computation | async-start | bytes 589824 | tf_op jit(solution)/shard_map/all_to_all | solution.py:53
  29.3 16.6 %collective-permute-start = (bf16[2,256,256]{2,1,0:T(8,128)(2,1)}, bf16[2,256,256]{2,1,0:T(8,128)(2,1)}, u32[]{:S(2)}, u32[]{:S(2)}) collective-permute-start(bf16[2,256,256]{2,1,0:T(8,128)(2,1)} %refs_3_.2), channel_id=1, source_target_pairs={{0,256},{256,0},{512,768},{768,512},{1,257},{257,1},{513,769},{769... | collective-permute-start | bytes 786440 | tf_op jit(solution)/shard_map/ppermute | solution.py:61
  32.6 13.2 %collective-permute-start.1 = (bf16[2,256,256]{2,1,0:T(8,128)(2,1)}, bf16[2,256,256]{2,1,0:T(8,128)(2,1)}, u32[]{:S(2)}, u32[]{:S(2)}) collective-permute-start(bf16[2,256,256]{2,1,0:T(8,128)(2,1)} %refs_3_.2), channel_id=1, source_target_pairs={{0,128},{128,0},{1,129},{129,1},{2,130},{130,2},{3,131},{131,3},{4... | collective-permute-start | bytes 786440 | tf_op jit(solution)/shard_map/ppermute | solution.py:69
  36.6 15.5 %copy-start.1 = (bf16[2,256,256]{2,1,0:T(8,128)(2,1)S(1)}, bf16[2,256,256]{2,1,0:T(8,128)(2,1)}, u32[]{:S(2)}) copy-start(bf16[2,256,256]{2,1,0:T(8,128)(2,1)} %refs_7_.1) | copy-start | bytes 786436
  47.9 14.8 %all-to-all-start.1 = ((bf16[4,64,2304]{2,1,0:T(8,128)(2,1)}), bf16[4,64,2304]{2,1,0:T(8,128)(2,1)}, u32[]{:S(2)}, u32[]{:S(2)}) async-start(bf16[4,64,2304]{2,1,0:T(8,128)(2,1)} %broadcast_in_dim.5), calls=%async_computation.1 | async-start | bytes 2359296 | tf_op jit(solution)/shard_map/all_to_all | solution.py:53
  52.2 9.7 %collective-permute-start.2 = (bf16[2,256,256]{2,1,0:T(8,128)(2,1)S(1)}, bf16[2,256,256]{2,1,0:T(8,128)(2,1)}, u32[]{:S(2)}, u32[]{:S(2)}) collective-permute-start(bf16[2,256,256]{2,1,0:T(8,128)(2,1)S(1)} %copy-done.1), channel_id=1, source_target_pairs={{0,256},{256,0},{512,768},{768,512},{1,257},{257,1},{513,769},{769... | collective-permute-start | bytes 786440 | tf_op jit(solution)/shard_map/ppermute | solution.py:61
  62.7 52.7 %copy-start = (bf16[2,256,256]{2,1,0:T(8,128)(2,1)S(1)}, bf16[2,256,256]{2,1,0:T(8,128)(2,1)}, u32[]{:S(2)}) copy-start(bf16[2,256,256]{2,1,0:T(8,128)(2,1)} %refs_3_.2) | copy-start | bytes 786436
  62.7 52.7 %copy-start.4 = (s32[2]{0:T(128)S(1)}, s32[2]{0:T(128)}, u32[]{:S(2)}) copy-start(s32[2]{0:T(128)} %refs_1_.1) | copy-start | bytes 28
  65.3 59.8 %copy-start.3 = (bf16[2,2,256]{2,1,0:T(2,128)(2,1)S(1)}, bf16[2,2,256]{2,1,0:T(2,128)(2,1)}, u32[]{:S(2)}) copy-start(bf16[2,2,256]{2,1,0:T(2,128)(2,1)} %refs_3_.3) | copy-start | bytes 6148
  81.4 17.9 %all-to-all-start.3 = ((bf16[16,4,96]{2,1,0:T(4,128)(2,1)}), bf16[16,4,96]{2,1,0:T(4,128)(2,1)S(1)}, u32[]{:S(2)}, u32[]{:S(2)}) async-start(bf16[16,4,96]{2,1,0:T(4,128)(2,1)} %copy.19), calls=%async_computation.3 | async-start | bytes 32768 | tf_op jit(solution)/shard_map/all_to_all | solution.py:53
  92.2 23.2 %collective-permute-start.4 = (bf16[2,256,256]{2,1,0:T(8,128)(2,1)}, bf16[2,256,256]{2,1,0:T(8,128)(2,1)S(1)}, u32[]{:S(2)}, u32[]{:S(2)}) collective-permute-start(bf16[2,256,256]{2,1,0:T(8,128)(2,1)} %refs_7_.1), channel_id=1, source_target_pairs={{0,128},{128,0},{1,129},{129,1},{2,130},{130,2},{3,131},{131,3},{4... | collective-permute-start | bytes 786440 | tf_op jit(solution)/shard_map/ppermute | solution.py:69
  94.1 21.3 %collective-permute-start.3 = (bf16[2,256,256]{2,1,0:T(8,128)(2,1)}, bf16[2,256,256]{2,1,0:T(8,128)(2,1)S(1)}, u32[]{:S(2)}, u32[]{:S(2)}) collective-permute-start(bf16[2,256,256]{2,1,0:T(8,128)(2,1)} %collective-permute-done.refs_4_), channel_id=1, source_target_pairs={{0,128},{128,0},{1,129},{129,1},{2,130},{130,2},{3,131},{131,3},{4... | collective-permute-start | bytes 786440 | tf_op jit(solution)/shard_map/ppermute | solution.py:69
  96.5 18.9 %collective-permute-start.5 = (bf16[2,256,256]{2,1,0:T(8,128)(2,1)}, bf16[2,256,256]{2,1,0:T(8,128)(2,1)S(1)}, u32[]{:S(2)}, u32[]{:S(2)}) collective-permute-start(bf16[2,256,256]{2,1,0:T(8,128)(2,1)} %collective-permute-done.2.refs_8_), channel_id=1, source_target_pairs={{0,128},{128,0},{1,129},{129,1},{2,130},{130,2},{3,131},{131,3},{4... | collective-permute-start | bytes 786440 | tf_op jit(solution)/shard_map/ppermute | solution.py:69
  100.0 15.3 %all-to-all-start.4 = ((bf16[4,2,768]{2,1,0:T(2,128)(2,1)}), bf16[4,2,768]{2,1,0:T(2,128)(2,1)S(1)}, u32[]{:S(2)}, u32[]{:S(2)}) async-start(bf16[4,2,768]{2,1,0:T(2,128)(2,1)} %pad_maximum_fusion.3), calls=%async_computation.4 | async-start | bytes 24576 | tf_op jit(solution)/shard_map/all_to_all | solution.py:53
  115.5 1.0 copy-start.2
  118.5 6.6 %collective-permute-start.6 = (f32[2,8,384]{2,1,0:T(8,128)S(1)}, f32[2,8,384]{2,1,0:T(8,128)S(1)}, u32[]{:S(2)}, u32[]{:S(2)}) collective-permute-start(f32[2,8,384]{2,1,0:T(8,128)S(1)} %get-tuple-element.17), channel_id=1, source_target_pairs={{0,512},{256,768},{512,0},{768,256},{1,513},{257,769},{513,1},{769... | collective-permute-start | bytes 73736 | tf_op jit(solution)/shard_map/ppermute | solution.py:65

commit v3 on v2

--- a/solution.py
+++ b/solution.py
@@ -73,29 +73,55 @@
 LIMIT = pltpu.CompilerParams(vmem_limit_bytes=16 * 2**20)
 
 
-def project_kernel(qw, x_ref, w_ref, out_ref, acc_ref):
-    full = lax.dot_general(x_ref[...], w_ref[...], NT, preferred_element_type=jnp.float32)
-    width = full.shape[1]
-    query = full[:, width - qw :]
-    low = query - query.astype(jnp.bfloat16).astype(jnp.float32)
-    for p in range(4):
-        rows = slice(p * 64, p * 64 + 64)
-        acc_ref[:, p * 8 : p * 8 + 8, :width] = full[rows].reshape(8, 8, width)
-        acc_ref[:, p * 8 : p * 8 + 8, width:] = low[rows].reshape(8, 8, qw)
+PIECES = ((0, 256), (256, 512), (512, 576))
+
+
+def project_kernel(x_ref, wg_ref, wq_ref, out_ref, w_ref, acc_ref, sems):
+    width, qw = wg_ref.shape[0], wq_ref.shape[0]
+    total = width + qw
+    copies = [
+        pltpu.make_async_copy(wg_ref.at[pl.ds(lo, hi - lo)], w_ref.at[pl.ds(lo, hi - lo)], sems.at[i])
+        for i, (lo, hi) in enumerate(PIECES)
+    ]
+    copies.append(pltpu.make_async_copy(wq_ref, w_ref.at[pl.ds(width, qw)], sems.at[3]))
+    for c in copies:
+        c.start()
+
+    def put(part, lo, hi):
+        for p in range(4):
+            acc_ref[:, p * 8 : p * 8 + 8, lo:hi] = part[p * 64 : p * 64 + 64].reshape(8, 8, hi - lo)
+
+    for i, (lo, hi) in enumerate(PIECES):
+        copies[i].wait()
+        if i == 2:
+            copies[3].wait()
+            hi = total
+        part = lax.dot_general(x_ref[...], w_ref[lo:hi], NT, preferred_element_type=jnp.float32)
+        put(part, lo, hi)
+    query = part[:, PIECES[2][1] - PIECES[2][0] :]
+    put(query - query.astype(jnp.bfloat16).astype(jnp.float32), total, total + qw)
     out_ref[...] = acc_ref[...].astype(jnp.bfloat16)
 
 
-def project(rows, weights, qw):
-    def kernel(*refs):
-        project_kernel(qw, *refs)
-
-    shape = (8, rows.shape[0] // 8, weights.shape[0] + qw)
+def project(rows, w_query, w_gate_up):
+    d, _, width = w_gate_up.shape
+    wg = w_gate_up.transpose(1, 2, 0).reshape(2 * width, d)
+    wq = w_query.T
+    total = 2 * width + wq.shape[0]
+    shape = (8, rows.shape[0] // 8, total + wq.shape[0])
+    vmem, hbm = pl.BlockSpec(memory_space=pltpu.VMEM), pl.BlockSpec(memory_space=pltpu.HBM)
     return pl.pallas_call(
-        kernel,
+        project_kernel,
+        in_specs=[vmem, hbm, hbm],
+        out_specs=vmem,
         out_shape=jax.ShapeDtypeStruct(shape, jnp.bfloat16),
-        scratch_shapes=[pltpu.VMEM(shape, jnp.float32)],
-        compiler_params=LIMIT,
-    )(rows, weights)
+        scratch_shapes=[
+            pltpu.VMEM((total, d), jnp.bfloat16),
+            pltpu.VMEM(shape, jnp.float32),
+            pltpu.SemaphoreType.DMA((4,)),
+        ],
+        compiler_params=pltpu.CompilerParams(vmem_limit_bytes=52 * 2**20),
+    )(rows, wg, wq)
 
 
 def attend_kernel(order, place_ref, lengths_ref, q_ref, *refs):
@@ -182,16 +208,17 @@
     d, width, qw = tokens.shape[1], w_gate_up.shape[2], w_query.shape[1]
     seqs, _, head_dim = key_cache.shape
 
-    keys_b, keys_c = beside(key_cache), other_core(key_cache)
-    weights = jnp.concatenate([w_gate_up.transpose(1, 2, 0).reshape(2 * width, d), w_query.T], axis=0)
+    keys_b, values_b = beside(key_cache), beside(value_cache)
     rows = spread(tokens, LATTICE, 32, far_groups()).reshape(64, d)
-    rows, weights, keys_b, keys_c = lax.optimization_barrier((rows, weights, keys_b, keys_c))
-    values_b = beside(value_cache)
+    rows, keys_b, values_b = lax.optimization_barrier((rows, keys_b, values_b))
+    keys_c = other_core(key_cache)
     rows = spread(rows, PLANE, 4, near_groups()).reshape(256, d)
-    rows, values_b = lax.optimization_barrier((rows, values_b))
+    rows, keys_c = lax.optimization_barrier((rows, keys_c))
     values_c, keys_d, values_d = other_core(value_cache), other_core(keys_b), other_core(values_b)
 
-    got = exchange(project(rows, weights, qw), GX).astype(f32)
+    got = exchange(project(rows, w_query, w_gate_up), GX)
+    got, values_c, keys_d, values_d = lax.optimization_barrier((got, values_c, keys_d, values_d))
+    got = got.astype(f32)
     total = jnp.sum(got, axis=0)
     hidden = (jax.nn.silu(total[:, :width]) * total[:, width : 2 * width]).astype(bf16)
     hidden = hidden.reshape(2, 2, 4, 2, width).transpose(0, 2, 1, 3, 4).reshape(32, width)

time: 127 us -> 129 us (1.016)
  blocking collectives: 15.3 us -> 0 us
  waiting for transfers between devices: 19.8 us -> 34.4 us
  starting transfers between devices: 73.7 us -> 81.6 us
  local copies, waits for them, and re-layouts: 7.83 us -> 4.26 us
  other arithmetic: 2.95 us -> 0.85 us
    all_to_all x1 -> x0, blocking collectives: 15.3 us -> none  [exchange(): return lax.all_to_all(x, axis, 0, 0, axis_index_groups=groups, tiled=True)]
    all_to_all x4 -> x5, waiting for transfers between devices: 12.3 us -> 25.9 us  [exchange(): return lax.all_to_all(x, axis, 0, 0, axis_index_groups=groups, tiled=True)]
    all_to_all x4 -> x5, starting transfers between devices: 54.1 us -> 60.4 us  [exchange(): return lax.all_to_all(x, axis, 0, 0, axis_index_groups=groups, tiled=True)]
    ppermute x4, starting transfers between devices: 8.16 us -> 11.1 us  [other_core(): return lax.ppermute(x, 'core', [(0, 1), (1, 0)])]
    ppermute x4, waiting for transfers between devices: 0.01 us -> 2.49 us  [other_core(): return lax.ppermute(x, 'core', [(0, 1), (1, 0)])]
    concatenate x1 -> x0, other arithmetic: 2.1 us -> none  [body(): jnp.concatenate([w_gate_up.transpose(1, 2, 0).reshape(2 * width, d), w_qu...]
    pallas_call x1, Pallas kernels: 2.55 us -> 4.28 us  [project(): pl.pallas_call(project_kernel, in_specs=[vmem, hbm, hbm], out_specs=vmem,...]
    reshape x1, local copies, waits for them, and re-layouts: 1.78 us -> 0.11 us  [body(): rows = spread(tokens, LATTICE, 32, far_groups()).reshape(64, d)]
  transfers between devices with their start and end apart: 11 -> 12, of which waited for: 6 -> 10; matrix products, arithmetic and copies ran while one was open for 4% -> 1% of each run, Pallas kernels for 0% -> 0%
where the time goes in v3:
time: 129 us
  starting transfers between devices  81.6 us (63%)
  waiting for transfers between devices  34.4 us (27%)
  Pallas kernels  6.67 us (5%)
  local copies, waits for them, and re-layouts  4.26 us (3%)
    all_to_all x5, starting transfers between devices, exchange(): return lax.all_to_all(x, axis, 0, 0, axis_index_groups=groups, tiled=True)  60.4 us
    all_to_all x5, waiting for transfers between devices, exchange(): return lax.all_to_all(x, axis, 0, 0, axis_index_groups=groups, tiled=True)  25.9 us
    ppermute x4, starting transfers between devices, other_core(): return lax.ppermute(x, 'core', [(0, 1), (1, 0)])  11.1 us
    ppermute x2, starting transfers between devices, beside(): return lax.ppermute(x, 'xl', [(i, i ^ 1) for i in range(4)])  5.85 us
    ppermute x2, waiting for transfers between devices, beside(): return lax.ppermute(x, 'xl', [(i, i ^ 1) for i in range(4)])  4.38 us
    pallas_call x1, Pallas kernels, project(): pl.pallas_call(project_kernel, in_specs=[vmem, hbm, hbm], out_specs=vmem,...  4.28 us
    ppermute x1, starting transfers between devices, across(): return lax.ppermute(x, 'xl', [(i, i ^ 2) for i in range(4)])  4.24 us
    broadcast_in_dim x2, local copies, waits for them, and re-layouts, spread(): return exchange(jnp.broadcast_to(x[None], (n,) + x.shape), axis, groups)  2.69 us
  transfers between devices with their start and end apart: 12, of which 10 were waited for; matrix products, arithmetic and copies ran while one was open for 1% of the time, Pallas kernels for 0%

profile of v3, /device:TPU:14, one launch (start us, length us, event | category | flops | bytes accessed | tf_op | source)
XLA Modules:
  0.0 128.5 jit_solution(11865640092860422431)
XLA Ops:
  0.6 1.6 %broadcast_in_dim.4 = bf16[32,2,2304]{2,1,0:T(2,128)(2,1)} broadcast(bf16[2,2304]{1,0:T(2,128)(2,1)} %param.7), dimensions={1,2} | broadcast | bytes 304128 | tf_op jit(solution)/shard_map/broadcast_in_dim | solution.py:57
  2.2 27.0 %all-to-all-start = ((bf16[32,2,2304]{2,1,0:T(2,128)(2,1)}), bf16[32,2,2304]{2,1,0:T(2,128)(2,1)S(1)}, u32[]{:S(2)}, u32[]{:S(2)}) async-start(bf16[32,2,2304]{2,1,0:T(2,128)(2,1)} %broadcast_in_dim.4), calls=%async_computation | async-start | bytes 589824 | tf_op jit(solution)/shard_map/all_to_all | solution.py:53
  29.2 3.3 %collective-permute-start = (bf16[2,256,256]{2,1,0:T(8,128)(2,1)}, bf16[2,256,256]{2,1,0:T(8,128)(2,1)S(1)}, u32[]{:S(2)}, u32[]{:S(2)}) collective-permute-start(bf16[2,256,256]{2,1,0:T(8,128)(2,1)} %refs_3_.2), channel_id=1, source_target_pairs={{0,256},{256,0},{512,768},{768,512},{1,257},{257,1},{513,769},{769... | collective-permute-start | bytes 786440 | tf_op jit(solution)/shard_map/ppermute | solution.py:61
  32.6 2.5 %collective-permute-start.1 = (bf16[2,256,256]{2,1,0:T(8,128)(2,1)}, bf16[2,256,256]{2,1,0:T(8,128)(2,1)S(1)}, u32[]{:S(2)}, u32[]{:S(2)}) collective-permute-start(bf16[2,256,256]{2,1,0:T(8,128)(2,1)} %refs_7_.1), channel_id=1, source_target_pairs={{0,256},{256,0},{512,768},{768,512},{1,257},{257,1},{513,769},{769... | collective-permute-start | bytes 786440 | tf_op jit(solution)/shard_map/ppermute | solution.py:61
  35.1 8.9 %all-to-all-done = bf16[32,2,2304]{2,1,0:T(2,128)(2,1)S(1)} async-done(((bf16[32,2,2304]{2,1,0:T(2,128)(2,1)}), bf16[32,2,2304]{2,1,0:T(2,128)(2,1)S(1)}, u32[]{:S(2)}, u32[]{:S(2)}) %all-to-all-start) | async-done | bytes 294944 | tf_op jit(solution)/shard_map/all_to_all | solution.py:53
  43.9 0.1 reshape.46
  44.0 0.1 collective-permute-done.refs_4_
  44.1 4.3 %collective-permute-done.1.refs_8_ = bf16[2,256,256]{2,1,0:T(8,128)(2,1)S(1)} collective-permute-done((bf16[2,256,256]{2,1,0:T(8,128)(2,1)}, bf16[2,256,256]{2,1,0:T(8,128)(2,1)S(1)}, u32[]{:S(2)}, u32[]{:S(2)}) %collective-permute-start.1) | collective-permute-done | bytes 262176 | tf_op jit(solution)/shard_map/ppermute | solution.py:61
  48.4 1.1 broadcast_in_dim.5
  49.5 0.0 copy-start.1
  49.5 0.0 copy-start
  49.5 4.0 %all-to-all-start.1 = ((bf16[4,64,2304]{2,1,0:T(8,128)(2,1)}), bf16[4,64,2304]{2,1,0:T(8,128)(2,1)S(1)}, u32[]{:S(2)}, u32[]{:S(2)}) async-start(bf16[4,64,2304]{2,1,0:T(8,128)(2,1)} %broadcast_in_dim.5), calls=%async_computation.1 | async-start | bytes 2359296 | tf_op jit(solution)/shard_map/all_to_all | solution.py:53
  53.6 0.0 copy-done.1
  53.6 4.7 %collective-permute-start.2 = (bf16[2,256,256]{2,1,0:T(8,128)(2,1)S(1)}, bf16[2,256,256]{2,1,0:T(8,128)(2,1)S(1)}, u32[]{:S(2)}, u32[]{:S(2)}) collective-permute-start(bf16[2,256,256]{2,1,0:T(8,128)(2,1)S(1)} %copy-done.1), channel_id=1, source_target_pairs={{0,128},{128,0},{1,129},{129,1},{2,130},{130,2},{3,131},{131,3},{4... | collective-permute-start | bytes 786440 | tf_op jit(solution)/shard_map/ppermute | solution.py:69
  58.3 1.1 collective-permute-done.2.refs_5_
  59.4 4.2 %all-to-all-done.1 = bf16[4,64,2304]{2,1,0:T(8,128)(2,1)S(1)} async-done(((bf16[4,64,2304]{2,1,0:T(8,128)(2,1)}), bf16[4,64,2304]{2,1,0:T(8,128)(2,1)S(1)}, u32[]{:S(2)}, u32[]{:S(2)}) %all-to-all-start.1) | async-done | bytes 1179680 | tf_op jit(solution)/shard_map/all_to_all | solution.py:53
  63.7 0.0 copy-done
  63.7 0.0 copy-start.2
  63.7 4.3 %shard_map.86 = bf16[8,32,768]{2,1,0:T(8,128)(2,1)} custom-call(bf16[256,2304]{1,0:T(8,128)(2,1)S(1)} %bitcast.23, bf16[576,2304]{1,0:T(8,128)(2,1)} %bitcast.25, bf16[96,2304]{1,0:T(8,128)(2,1)S(1)} %bitcast.24), custom_call_target="tpu_custom_call" | custom-call | tf_op jit(solution)/shard_map/pallas_call | solution.py:113
  68.0 0.0 copy-start.4
  68.0 7.8 %all-to-all-start.2 = ((bf16[8,32,768]{2,1,0:T(8,128)(2,1)}), bf16[8,32,768]{2,1,0:T(8,128)(2,1)S(1)}, u32[]{:S(2)}, u32[]{:S(2)}) async-start(bf16[8,32,768]{2,1,0:T(8,128)(2,1)} %shard_map.86), calls=%async_computation.2 | async-start | bytes 786432 | tf_op jit(solution)/shard_map/all_to_all | solution.py:53
  75.8 0.0 copy-done.2
  75.8 2.0 %collective-permute-start.3 = (bf16[2,256,256]{2,1,0:T(8,128)(2,1)S(1)}, bf16[2,256,256]{2,1,0:T(8,128)(2,1)S(1)}, u32[]{:S(2)}, u32[]{:S(2)}) collective-permute-start(bf16[2,256,256]{2,1,0:T(8,128)(2,1)S(1)} %copy-done.2), channel_id=1, source_target_pairs={{0,128},{128,0},{1,129},{129,1},{2,130},{130,2},{3,131},{131,3},{4... | collective-permute-start | bytes 786440 | tf_op jit(solution)/shard_map/ppermute | solution.py:69
  77.9 2.3 %collective-permute-start.4 = (bf16[2,256,256]{2,1,0:T(8,128)(2,1)S(1)}, bf16[2,256,256]{2,1,0:T(8,128)(2,1)S(1)}, u32[]{:S(2)}, u32[]{:S(2)}) collective-permute-start(bf16[2,256,256]{2,1,0:T(8,128)(2,1)S(1)} %collective-permute-done.refs_4_), channel_id=1, source_target_pairs={{0,128},{128,0},{1,129},{129,1},{2,130},{130,2},{3,131},{131,3},{4... | collective-permute-start | bytes 786440 | tf_op jit(solution)/shard_map/ppermute | solution.py:69
  80.2 2.1 %collective-permute-start.5 = (bf16[2,256,256]{2,1,0:T(8,128)(2,1)S(1)}, bf16[2,256,256]{2,1,0:T(8,128)(2,1)S(1)}, u32[]{:S(2)}, u32[]{:S(2)}) collective-permute-start(bf16[2,256,256]{2,1,0:T(8,128)(2,1)S(1)} %collective-permute-done.1.refs_8_), channel_id=1, source_target_pairs={{0,128},{128,0},{1,129},{129,1},{2,130},{130,2},{3,131},{131,3},{4... | collective-permute-start | bytes 786440 | tf_op jit(solution)/shard_map/ppermute | solution.py:69
  82.2 0.0 collective-permute-done.3.refs_9_
  82.2 0.0 collective-permute-done.4.refs_6_
  82.2 1.3 %collective-permute-done.5.refs_10_ = bf16[2,256,256]{2,1,0:T(8,128)(2,1)S(1)} collective-permute-done((bf16[2,256,256]{2,1,0:T(8,128)(2,1)S(1)}, bf16[2,256,256]{2,1,0:T(8,128)(2,1)S(1)}, u32[]{:S(2)}, u32[]{:S(2)}) %collective-permute-start.5) | collective-permute-done | bytes 262176 | tf_op jit(solution)/shard_map/ppermute | solution.py:69
  83.6 2.4 %all-to-all-done.2 = bf16[8,32,768]{2,1,0:T(8,128)(2,1)S(1)} async-done(((bf16[8,32,768]{2,1,0:T(8,128)(2,1)}), bf16[8,32,768]{2,1,0:T(8,128)(2,1)S(1)}, u32[]{:S(2)}, u32[]{:S(2)}) %all-to-all-start.2) | async-done | bytes 393248 | tf_op jit(solution)/shard_map/all_to_all | solution.py:53
  86.0 0.1 convert_reduce_fusion
  86.0 0.1 fusion.1
  86.2 0.6 copy.19
  86.8 10.8 %all-to-all-start.3 = ((bf16[16,4,96]{2,1,0:T(4,128)(2,1)}), bf16[16,4,96]{2,1,0:T(4,128)(2,1)S(1)}, u32[]{:S(2)}, u32[]{:S(2)}) async-start(bf16[16,4,96]{2,1,0:T(4,128)(2,1)} %copy.19), calls=%async_computation.3 | async-start | bytes 32768 | tf_op jit(solution)/shard_map/all_to_all | solution.py:53
  97.6 7.1 %all-to-all-done.3 = bf16[16,4,96]{2,1,0:T(4,128)(2,1)S(1)} async-done(((bf16[16,4,96]{2,1,0:T(4,128)(2,1)}), bf16[16,4,96]{2,1,0:T(4,128)(2,1)S(1)}, u32[]{:S(2)}, u32[]{:S(2)}) %all-to-all-start.3) | async-done | bytes 12320 | tf_op jit(solution)/shard_map/all_to_all | solution.py:53
  104.7 0.1 reshape.55
  104.8 0.6 pad_maximum_fusion.2
  105.5 10.7 %all-to-all-start.4 = ((bf16[4,2,768]{2,1,0:T(2,128)(2,1)}), bf16[4,2,768]{2,1,0:T(2,128)(2,1)S(1)}, u32[]{:S(2)}, u32[]{:S(2)}) async-start(bf16[4,2,768]{2,1,0:T(2,128)(2,1)} %pad_maximum_fusion.2), calls=%async_computation.4 | async-start | bytes 24576 | tf_op jit(solution)/shard_map/all_to_all | solution.py:53
  116.1 3.3 %all-to-all-done.4 = bf16[4,2,768]{2,1,0:T(2,128)(2,1)S(1)} async-done(((bf16[4,2,768]{2,1,0:T(2,128)(2,1)}), bf16[4,2,768]{2,1,0:T(2,128)(2,1)S(1)}, u32[]{:S(2)}, u32[]{:S(2)}) %all-to-all-start.4) | async-done | bytes 12320 | tf_op jit(solution)/shard_map/all_to_all | solution.py:53
  119.5 0.0 copy-done.4
  119.5 0.0 copy-start.3
  119.5 1.5 %shard_map.87 = (f32[2,8,384]{2,1,0:T(8,128)S(1)}, f32[2,8,384]{2,1,0:T(8,128)S(1)}) custom-call(s32[1]{0:T(128)} %bitcast.5.refs_0_, s32[2]{0:T(128)S(1)} %copy-done.4, bf16[2,16,256]{2,1,0:T(8,128)(2,1)S(1)} %pad_maximum_fusion.1.refs_2_, bf16[2,256,256]{2,1,0:T(8,128)(2,1)S(1)} %copy-done.1, bf16[2,256,256]{2,1,0:T(8,128)(2,1)S(1)} %collective-permute-done.refs_4_, ...), custom_call_target="tpu_custom_call" | custom-call | tf_op jit(solution)/shard_map/pallas_call | solution.py:165
  121.0 4.2 %collective-permute-start.6 = (f32[2,8,384]{2,1,0:T(8,128)S(1)}, f32[2,8,384]{2,1,0:T(8,128)S(1)}, u32[]{:S(2)}, u32[]{:S(2)}) collective-permute-start(f32[2,8,384]{2,1,0:T(8,128)S(1)} %get-tuple-element.23), channel_id=1, source_target_pairs={{0,512},{256,768},{512,0},{768,256},{1,513},{257,769},{513,1},{769... | collective-permute-start | bytes 73736 | tf_op jit(solution)/shard_map/ppermute | solution.py:65
  125.3 0.1 fusion
  125.4 0.6 reshape.50
  126.1 1.6 %collective-permute-done.6.refs_1_ = f32[2,8,384]{2,1,0:T(8,128)S(1)} collective-permute-done((f32[2,8,384]{2,1,0:T(8,128)S(1)}, f32[2,8,384]{2,1,0:T(8,128)S(1)}, u32[]{:S(2)}, u32[]{:S(2)}) %collective-permute-start.6) | collective-permute-done | bytes 24608 | tf_op jit(solution)/shard_map/ppermute | solution.py:65
  127.7 0.0 copy-done.3
  127.7 0.9 shard_map.88
  (10 shorter events, 0.1 us)
Async XLA Ops:
  2.2 41.7 %all-to-all-start = ((bf16[32,2,2304]{2,1,0:T(2,128)(2,1)}), bf16[32,2,2304]{2,1,0:T(2,128)(2,1)S(1)}, u32[]{:S(2)}, u32[]{:S(2)}) async-start(bf16[32,2,2304]{2,1,0:T(2,128)(2,1)} %broadcast_in_dim.4), calls=%async_computation | async-start | bytes 589824 | tf_op jit(solution)/shard_map/all_to_all | solution.py:53
  29.2 14.9 %collective-permute-start = (bf16[2,256,256]{2,1,0:T(8,128)(2,1)}, bf16[2,256,256]{2,1,0:T(8,128)(2,1)S(1)}, u32[]{:S(2)}, u32[]{:S(2)}) collective-permute-start(bf16[2,256,256]{2,1,0:T(8,128)(2,1)} %refs_3_.2), channel_id=1, source_target_pairs={{0,256},{256,0},{512,768},{768,512},{1,257},{257,1},{513,769},{769... | collective-permute-start | bytes 786440 | tf_op jit(solution)/shard_map/ppermute | solution.py:61
  32.6 15.9 %collective-permute-start.1 = (bf16[2,256,256]{2,1,0:T(8,128)(2,1)}, bf16[2,256,256]{2,1,0:T(8,128)(2,1)S(1)}, u32[]{:S(2)}, u32[]{:S(2)}) collective-permute-start(bf16[2,256,256]{2,1,0:T(8,128)(2,1)} %refs_7_.1), channel_id=1, source_target_pairs={{0,256},{256,0},{512,768},{768,512},{1,257},{257,1},{513,769},{769... | collective-permute-start | bytes 786440 | tf_op jit(solution)/shard_map/ppermute | solution.py:61
  49.5 4.0 %copy-start.1 = (bf16[2,256,256]{2,1,0:T(8,128)(2,1)S(1)}, bf16[2,256,256]{2,1,0:T(8,128)(2,1)}, u32[]{:S(2)}) copy-start(bf16[2,256,256]{2,1,0:T(8,128)(2,1)} %refs_3_.2) | copy-start | bytes 786436
  49.5 14.1 %copy-start = (bf16[2304,96]{0,1:T(8,128)(2,1)S(1)}, bf16[2304,96]{0,1:T(8,128)(2,1)}, u32[]{:S(2)}) copy-start(bf16[2304,96]{0,1:T(8,128)(2,1)} %param.8) | copy-start | bytes 1327108
  49.5 14.1 %all-to-all-start.1 = ((bf16[4,64,2304]{2,1,0:T(8,128)(2,1)}), bf16[4,64,2304]{2,1,0:T(8,128)(2,1)S(1)}, u32[]{:S(2)}, u32[]{:S(2)}) async-start(bf16[4,64,2304]{2,1,0:T(8,128)(2,1)} %broadcast_in_dim.5), calls=%async_computation.1 | async-start | bytes 2359296 | tf_op jit(solution)/shard_map/all_to_all | solution.py:53
  53.6 5.9 %collective-permute-start.2 = (bf16[2,256,256]{2,1,0:T(8,128)(2,1)S(1)}, bf16[2,256,256]{2,1,0:T(8,128)(2,1)S(1)}, u32[]{:S(2)}, u32[]{:S(2)}) collective-permute-start(bf16[2,256,256]{2,1,0:T(8,128)(2,1)S(1)} %copy-done.1), channel_id=1, source_target_pairs={{0,128},{128,0},{1,129},{129,1},{2,130},{130,2},{3,131},{131,3},{4... | collective-permute-start | bytes 786440 | tf_op jit(solution)/shard_map/ppermute | solution.py:69
  63.7 12.1 %copy-start.2 = (bf16[2,256,256]{2,1,0:T(8,128)(2,1)S(1)}, bf16[2,256,256]{2,1,0:T(8,128)(2,1)}, u32[]{:S(2)}) copy-start(bf16[2,256,256]{2,1,0:T(8,128)(2,1)} %refs_7_.1) | copy-start | bytes 786436
  68.0 51.5 %copy-start.4 = (s32[2]{0:T(128)S(1)}, s32[2]{0:T(128)}, u32[]{:S(2)}) copy-start(s32[2]{0:T(128)} %refs_1_.1) | copy-start | bytes 28
  68.0 18.0 %all-to-all-start.2 = ((bf16[8,32,768]{2,1,0:T(8,128)(2,1)}), bf16[8,32,768]{2,1,0:T(8,128)(2,1)S(1)}, u32[]{:S(2)}, u32[]{:S(2)}) async-start(bf16[8,32,768]{2,1,0:T(8,128)(2,1)} %shard_map.86), calls=%async_computation.2 | async-start | bytes 786432 | tf_op jit(solution)/shard_map/all_to_all | solution.py:53
  75.8 6.4 %collective-permute-start.3 = (bf16[2,256,256]{2,1,0:T(8,128)(2,1)S(1)}, bf16[2,256,256]{2,1,0:T(8,128)(2,1)S(1)}, u32[]{:S(2)}, u32[]{:S(2)}) collective-permute-start(bf16[2,256,256]{2,1,0:T(8,128)(2,1)S(1)} %copy-done.2), channel_id=1, source_target_pairs={{0,128},{128,0},{1,129},{129,1},{2,130},{130,2},{3,131},{131,3},{4... | collective-permute-start | bytes 786440 | tf_op jit(solution)/shard_map/ppermute | solution.py:69
  77.9 4.4 %collective-permute-start.4 = (bf16[2,256,256]{2,1,0:T(8,128)(2,1)S(1)}, bf16[2,256,256]{2,1,0:T(8,128)(2,1)S(1)}, u32[]{:S(2)}, u32[]{:S(2)}) collective-permute-start(bf16[2,256,256]{2,1,0:T(8,128)(2,1)S(1)} %collective-permute-done.refs_4_), channel_id=1, source_target_pairs={{0,128},{128,0},{1,129},{129,1},{2,130},{130,2},{3,131},{131,3},{4... | collective-permute-start | bytes 786440 | tf_op jit(solution)/shard_map/ppermute | solution.py:69
  80.2 3.4 %collective-permute-start.5 = (bf16[2,256,256]{2,1,0:T(8,128)(2,1)S(1)}, bf16[2,256,256]{2,1,0:T(8,128)(2,1)S(1)}, u32[]{:S(2)}, u32[]{:S(2)}) collective-permute-start(bf16[2,256,256]{2,1,0:T(8,128)(2,1)S(1)} %collective-permute-done.1.refs_8_), channel_id=1, source_target_pairs={{0,128},{128,0},{1,129},{129,1},{2,130},{130,2},{3,131},{131,3},{4... | collective-permute-start | bytes 786440 | tf_op jit(solution)/shard_map/ppermute | solution.py:69
  86.8 18.0 %all-to-all-start.3 = ((bf16[16,4,96]{2,1,0:T(4,128)(2,1)}), bf16[16,4,96]{2,1,0:T(4,128)(2,1)S(1)}, u32[]{:S(2)}, u32[]{:S(2)}) async-start(bf16[16,4,96]{2,1,0:T(4,128)(2,1)} %copy.19), calls=%async_computation.3 | async-start | bytes 32768 | tf_op jit(solution)/shard_map/all_to_all | solution.py:53
  105.5 14.0 %all-to-all-start.4 = ((bf16[4,2,768]{2,1,0:T(2,128)(2,1)}), bf16[4,2,768]{2,1,0:T(2,128)(2,1)S(1)}, u32[]{:S(2)}, u32[]{:S(2)}) async-start(bf16[4,2,768]{2,1,0:T(2,128)(2,1)} %pad_maximum_fusion.2), calls=%async_computation.4 | async-start | bytes 24576 | tf_op jit(solution)/shard_map/all_to_all | solution.py:53
  119.5 8.2 %copy-start.3 = (bf16[2,2,256]{2,1,0:T(2,128)(2,1)S(1)}, bf16[2,2,256]{2,1,0:T(2,128)(2,1)}, u32[]{:S(2)}) copy-start(bf16[2,2,256]{2,1,0:T(2,128)(2,1)} %refs_3_.3) | copy-start | bytes 6148
  121.0 6.6 %collective-permute-start.6 = (f32[2,8,384]{2,1,0:T(8,128)S(1)}, f32[2,8,384]{2,1,0:T(8,128)S(1)}, u32[]{:S(2)}, u32[]{:S(2)}) collective-permute-start(f32[2,8,384]{2,1,0:T(8,128)S(1)} %get-tuple-element.23), channel_id=1, source_target_pairs={{0,512},{256,768},{512,0},{768,256},{1,513},{257,769},{513,1},{769... | collective-permute-start | bytes 73736 | tf_op jit(solution)/shard_map/ppermute | solution.py:65

commit v4 on v1

--- a/solution.py
+++ b/solution.py
@@ -9,15 +9,12 @@
 GX = ("xl", "core")
 GY = ("xh", "z", "y")
 ALL = GX + GY
-LATTICE = ("xh", "z", "y")
 PLANE = ("core", "z", "y")
 
 
 def far_groups():
     return [
-        [xh * 64 + (zh * 2 + zlo) * 8 + yh * 2 + ylo for xh in range(2) for zh in range(4) for yh in range(4)]
-        for zlo in range(2)
-        for ylo in range(2)
+        [(zh * 2 + zlo) * 8 + yh * 2 + ylo for zh in range(4) for yh in range(4)] for zlo in range(2) for ylo in range(2)
     ]
 
 
@@ -65,7 +62,11 @@
 
 
 def project_kernel(x_ref, wg_ref, wq_ref, out_ref, acc_ref):
-    x = x_ref[...]
+    n = x_ref.shape[0]
+    i = lax.broadcasted_iota(jnp.int32, (n, n), 0)
+    source = (i & ~63) | ((i >> 3 & 3) << 4) | ((i >> 1 & 3) << 2) | ((i >> 5 & 1) << 1) | (i & 1)
+    order = (source == lax.broadcasted_iota(jnp.int32, (n, n), 1)).astype(jnp.float32).astype(jnp.bfloat16)
+    x = jnp.dot(order, x_ref[...], preferred_element_type=jnp.float32).astype(jnp.bfloat16)
     width, qw = wg_ref.shape[0], wq_ref.shape[0]
     gate_up = lax.dot_general(x, wg_ref[...], NT, preferred_element_type=jnp.float32)
     query = lax.dot_general(x, wq_ref[...], NT, preferred_element_type=jnp.float32)
@@ -175,12 +176,16 @@
     d, width, qw = tokens.shape[1], w_gate_up.shape[2], w_query.shape[1]
     seqs, _, head_dim = key_cache.shape
 
-    keys_b = beside(key_cache)
-    rows = spread(tokens, LATTICE, 32, far_groups()).reshape(64, d)
-    rows, keys_b = lax.optimization_barrier((rows, keys_b))
-    values_b, keys_c = beside(value_cache), other_core(key_cache)
+    partner = lax.ppermute(tokens, "xh", [(0, 1), (1, 0)])
+    first = lax.axis_index("xh") == 0
+    rows = jnp.stack([jnp.where(first, tokens, partner), jnp.where(first, partner, tokens)])
+    keys_b, values_b = beside(key_cache), beside(value_cache)
+    rows = spread(rows.reshape(2 * seqs, d), ("z", "y"), 16, far_groups())
+    rows = rows.reshape(64, d)
+    rows, keys_b, values_b = lax.optimization_barrier((rows, keys_b, values_b))
+    keys_c = other_core(key_cache)
     rows = spread(rows, PLANE, 4, near_groups()).reshape(256, d)
-    rows, values_b, keys_c = lax.optimization_barrier((rows, values_b, keys_c))
+    rows, keys_c = lax.optimization_barrier((rows, keys_c))
     values_c, keys_d, values_d = other_core(value_cache), other_core(keys_b), other_core(values_b)
 
     got = exchange(project(rows, w_query, w_gate_up), GX).astype(f32)

time: 121 us -> 128 us (1.058)
  waiting for transfers between devices: 28 us -> 33 us
  starting transfers between devices: 80.1 us -> 81.6 us
    ppermute x0 -> x1, starting transfers between devices: none -> 5.05 us  [body(): partner = lax.ppermute(tokens, 'xh', [(0, 1), (1, 0)])]
    ppermute x0 -> x1, waiting for transfers between devices: none -> 4.65 us  [body(): partner = lax.ppermute(tokens, 'xh', [(0, 1), (1, 0)])]
    all_to_all x4, starting transfers between devices: 49.5 us -> 45.3 us  [exchange(): return lax.all_to_all(x, axis, 0, 0, axis_index_groups=groups, tiled=True)]
    ppermute x2, waiting for transfers between devices: 3.18 us -> 0.67 us  [beside(): return lax.ppermute(x, 'xl', [(i, i ^ 1) for i in range(4)])]
    all_to_all x4, waiting for transfers between devices: 22.2 us -> 23.9 us  [exchange(): return lax.all_to_all(x, axis, 0, 0, axis_index_groups=groups, tiled=True)]
    ppermute x2, starting transfers between devices: 13.9 us -> 15.4 us  [across(): return lax.ppermute(x, 'xl', [(i, i ^ 2) for i in range(4)])]
    ppermute x2, starting transfers between devices: 7.24 us -> 5.85 us  [beside(): return lax.ppermute(x, 'xl', [(i, i ^ 1) for i in range(4)])]
    broadcast_in_dim x2 -> x3, local copies, waits for them, and re-layouts: 2.69 us -> 1.93 us  [spread(): return exchange(jnp.broadcast_to(x[None], (n,) + x.shape), axis, groups)]
  transfers between devices with their start and end apart: 12 -> 13, of which waited for: 7 -> 9; matrix products, arithmetic and copies ran while one was open for 1% -> 1% of each run, Pallas kernels for 0% -> 0%
where the time goes in v4:
time: 128 us; the launch traced here: 127 us
  starting transfers between devices  81.6 us (64%)
  waiting for transfers between devices  33 us (26%)
  local copies, waits for them, and re-layouts  5.19 us (4%)
  Pallas kernels  4.96 us (4%)
    all_to_all x4, starting transfers between devices, exchange(): return lax.all_to_all(x, axis, 0, 0, axis_index_groups=groups, tiled=True)  45.3 us
    all_to_all x4, waiting for transfers between devices, exchange(): return lax.all_to_all(x, axis, 0, 0, axis_index_groups=groups, tiled=True)  23.9 us
    ppermute x2, starting transfers between devices, across(): return lax.ppermute(x, 'xl', [(i, i ^ 2) for i in range(4)])  15.4 us
    ppermute x4, starting transfers between devices, other_core(): return lax.ppermute(x, 'core', [(0, 1), (1, 0)])  9.91 us
    ppermute x2, starting transfers between devices, beside(): return lax.ppermute(x, 'xl', [(i, i ^ 1) for i in range(4)])  5.85 us
    ppermute x1, starting transfers between devices, body(): partner = lax.ppermute(tokens, 'xh', [(0, 1), (1, 0)])  5.05 us
    ppermute x1, waiting for transfers between devices, body(): partner = lax.ppermute(tokens, 'xh', [(0, 1), (1, 0)])  4.65 us
    ppermute x2, waiting for transfers between devices, across(): return lax.ppermute(x, 'xl', [(i, i ^ 2) for i in range(4)])  2.63 us
  transfers between devices with their start and end apart: 13, of which 9 were waited for; matrix products, arithmetic and copies ran while one was open for 1% of the time, Pallas kernels for 0%

profile of v4, /device:TPU:14, one launch (start us, length us, event | category | flops | bytes accessed | tf_op | source)
XLA Modules:
  0.0 126.6 jit_solution(11674676870098899467)
XLA Ops:
  0.6 5.1 %collective-permute-start = (bf16[2,2304]{1,0:T(2,128)(2,1)}, bf16[2,2304]{1,0:T(2,128)(2,1)S(1)}, u32[]{:S(2)}, u32[]{:S(2)}) collective-permute-start(bf16[2,2304]{1,0:T(2,128)(2,1)} %param.7), channel_id=1, source_target_pairs={{0,64},{64,0},{1,65},{65,1},{2,66},{66,2},{3,67},{67,3},{4,68},{68... | collective-permute-start | bytes 27656 | tf_op jit(solution)/shard_map/ppermute | solution.py:179
  5.7 4.6 %collective-permute-done = bf16[2,2304]{1,0:T(2,128)(2,1)S(1)} collective-permute-done((bf16[2,2304]{1,0:T(2,128)(2,1)}, bf16[2,2304]{1,0:T(2,128)(2,1)S(1)}, u32[]{:S(2)}, u32[]{:S(2)}) %collective-permute-start) | collective-permute-done | bytes 9248 | tf_op jit(solution)/shard_map/ppermute | solution.py:179
  10.3 0.7 fusion.2
  11.1 0.8 broadcast_in_dim.14
  11.9 21.6 %all-to-all-start = ((bf16[16,4,2304]{2,1,0:T(4,128)(2,1)}), bf16[16,4,2304]{2,1,0:T(4,128)(2,1)S(1)}, u32[]{:S(2)}, u32[]{:S(2)}) async-start(bf16[16,4,2304]{2,1,0:T(4,128)(2,1)} %broadcast_in_dim.14), calls=%async_computation | async-start | bytes 589824 | tf_op jit(solution)/shard_map/all_to_all | solution.py:41
  33.5 3.3 %collective-permute-start.1 = (bf16[2,256,256]{2,1,0:T(8,128)(2,1)}, bf16[2,256,256]{2,1,0:T(8,128)(2,1)S(1)}, u32[]{:S(2)}, u32[]{:S(2)}) collective-permute-start(bf16[2,256,256]{2,1,0:T(8,128)(2,1)} %refs_3_.2), channel_id=1, source_target_pairs={{0,256},{256,0},{512,768},{768,512},{1,257},{257,1},{513,769},{769... | collective-permute-start | bytes 786440 | tf_op jit(solution)/shard_map/ppermute | solution.py:49
  36.8 2.5 %collective-permute-start.2 = (bf16[2,256,256]{2,1,0:T(8,128)(2,1)}, bf16[2,256,256]{2,1,0:T(8,128)(2,1)S(1)}, u32[]{:S(2)}, u32[]{:S(2)}) collective-permute-start(bf16[2,256,256]{2,1,0:T(8,128)(2,1)} %refs_7_.1), channel_id=1, source_target_pairs={{0,256},{256,0},{512,768},{768,512},{1,257},{257,1},{513,769},{769... | collective-permute-start | bytes 786440 | tf_op jit(solution)/shard_map/ppermute | solution.py:49
  39.4 7.7 %all-to-all-done = bf16[16,4,2304]{2,1,0:T(4,128)(2,1)S(1)} async-done(((bf16[16,4,2304]{2,1,0:T(4,128)(2,1)}), bf16[16,4,2304]{2,1,0:T(4,128)(2,1)S(1)}, u32[]{:S(2)}, u32[]{:S(2)}) %all-to-all-start) | async-done | bytes 294944 | tf_op jit(solution)/shard_map/all_to_all | solution.py:41
  47.1 0.1 reshape.33
  47.2 0.0 collective-permute-done.1.refs_4_
  47.2 0.7 collective-permute-done.2.refs_8_
  47.9 1.1 broadcast_in_dim.15
  49.0 0.0 copy-start.2
  49.0 0.0 copy-start.1
  49.0 4.0 %all-to-all-start.1 = ((bf16[4,64,2304]{2,1,0:T(8,128)(2,1)}), bf16[4,64,2304]{2,1,0:T(8,128)(2,1)S(1)}, u32[]{:S(2)}, u32[]{:S(2)}) async-start(bf16[4,64,2304]{2,1,0:T(8,128)(2,1)} %broadcast_in_dim.15), calls=%async_computation.1 | async-start | bytes 2359296 | tf_op jit(solution)/shard_map/all_to_all | solution.py:41
  53.0 0.0 copy-done.2
  53.0 3.5 %collective-permute-start.3 = (bf16[2,256,256]{2,1,0:T(8,128)(2,1)S(1)}, bf16[2,256,256]{2,1,0:T(8,128)(2,1)S(1)}, u32[]{:S(2)}, u32[]{:S(2)}) collective-permute-start(bf16[2,256,256]{2,1,0:T(8,128)(2,1)S(1)} %copy-done.2), channel_id=1, source_target_pairs={{0,128},{128,0},{1,129},{129,1},{2,130},{130,2},{3,131},{131,3},{4... | collective-permute-start | bytes 786440 | tf_op jit(solution)/shard_map/ppermute | solution.py:57
  56.5 1.1 collective-permute-done.3.refs_5_
  57.7 5.4 %all-to-all-done.1 = bf16[4,64,2304]{2,1,0:T(8,128)(2,1)S(1)} async-done(((bf16[4,64,2304]{2,1,0:T(8,128)(2,1)}), bf16[4,64,2304]{2,1,0:T(8,128)(2,1)S(1)}, u32[]{:S(2)}, u32[]{:S(2)}) %all-to-all-start.1) | async-done | bytes 1179680 | tf_op jit(solution)/shard_map/all_to_all | solution.py:41
  63.1 0.0 copy-done.1
  63.1 0.0 copy-start
  63.1 1.7 %copy-done = bf16[2304,2,288]{0,2,1:T(8,128)(2,1)S(1)} copy-done((bf16[2304,2,288]{0,2,1:T(8,128)(2,1)S(1)}, bf16[2304,2,288]{0,2,1:T(8,128)(2,1)}, u32[]{:S(2)}) %copy-start) | copy-done | bytes 2654232
  64.9 0.0 copy-start.3
  64.9 2.6 %shard_map.86 = bf16[8,32,768]{2,1,0:T(8,128)(2,1)} custom-call(bf16[256,2304]{1,0:T(8,128)(2,1)S(1)} %bitcast.17, bf16[576,2304]{1,0:T(8,128)(2,1)S(1)} %bitcast.18, bf16[96,2304]{1,0:T(8,128)(2,1)S(1)} %bitcast.19), custom_call_target="tpu_custom_call" | custom-call | tf_op jit(solution)/shard_map/pallas_call | solution.py:87
  67.4 0.0 copy-start.5
  67.4 6.7 %all-to-all-start.2 = ((bf16[8,32,768]{2,1,0:T(8,128)(2,1)}), bf16[8,32,768]{2,1,0:T(8,128)(2,1)S(1)}, u32[]{:S(2)}, u32[]{:S(2)}) async-start(bf16[8,32,768]{2,1,0:T(8,128)(2,1)} %shard_map.86), calls=%async_computation.2 | async-start | bytes 786432 | tf_op jit(solution)/shard_map/all_to_all | solution.py:41
  74.2 0.0 copy-done.3
  74.2 2.0 %collective-permute-start.6 = (bf16[2,256,256]{2,1,0:T(8,128)(2,1)S(1)}, bf16[2,256,256]{2,1,0:T(8,128)(2,1)S(1)}, u32[]{:S(2)}, u32[]{:S(2)}) collective-permute-start(bf16[2,256,256]{2,1,0:T(8,128)(2,1)S(1)} %copy-done.3), channel_id=1, source_target_pairs={{0,128},{128,0},{1,129},{129,1},{2,130},{130,2},{3,131},{131,3},{4... | collective-permute-start | bytes 786440 | tf_op jit(solution)/shard_map/ppermute | solution.py:57
  76.2 2.3 %collective-permute-start.5 = (bf16[2,256,256]{2,1,0:T(8,128)(2,1)S(1)}, bf16[2,256,256]{2,1,0:T(8,128)(2,1)S(1)}, u32[]{:S(2)}, u32[]{:S(2)}) collective-permute-start(bf16[2,256,256]{2,1,0:T(8,128)(2,1)S(1)} %collective-permute-done.1.refs_4_), channel_id=1, source_target_pairs={{0,128},{128,0},{1,129},{129,1},{2,130},{130,2},{3,131},{131,3},{4... | collective-permute-start | bytes 786440 | tf_op jit(solution)/shard_map/ppermute | solution.py:57
  78.5 2.1 %collective-permute-start.7 = (bf16[2,256,256]{2,1,0:T(8,128)(2,1)S(1)}, bf16[2,256,256]{2,1,0:T(8,128)(2,1)S(1)}, u32[]{:S(2)}, u32[]{:S(2)}) collective-permute-start(bf16[2,256,256]{2,1,0:T(8,128)(2,1)S(1)} %collective-permute-done.2.refs_8_), channel_id=1, source_target_pairs={{0,128},{128,0},{1,129},{129,1},{2,130},{130,2},{3,131},{131,3},{4... | collective-permute-start | bytes 786440 | tf_op jit(solution)/shard_map/ppermute | solution.py:57
  80.6 3.8 %all-to-all-done.2 = bf16[8,32,768]{2,1,0:T(8,128)(2,1)S(1)} async-done(((bf16[8,32,768]{2,1,0:T(8,128)(2,1)}), bf16[8,32,768]{2,1,0:T(8,128)(2,1)S(1)}, u32[]{:S(2)}, u32[]{:S(2)}) %all-to-all-start.2) | async-done | bytes 393248 | tf_op jit(solution)/shard_map/all_to_all | solution.py:41
  84.4 0.1 convert_reduce_fusion
  84.4 0.1 fusion.1
  84.5 0.6 copy.13
  85.2 13.0 %all-to-all-start.3 = ((bf16[32,2,96]{2,1,0:T(2,128)(2,1)}), bf16[32,2,96]{2,1,0:T(2,128)(2,1)S(1)}, u32[]{:S(2)}, u32[]{:S(2)}) async-start(bf16[32,2,96]{2,1,0:T(2,128)(2,1)} %copy.13), calls=%async_computation.3 | async-start | bytes 32768 | tf_op jit(solution)/shard_map/all_to_all | solution.py:41
  98.2 7.0 %all-to-all-done.3 = bf16[32,2,96]{2,1,0:T(2,128)(2,1)S(1)} async-done(((bf16[32,2,96]{2,1,0:T(2,128)(2,1)}), bf16[32,2,96]{2,1,0:T(2,128)(2,1)S(1)}, u32[]{:S(2)}, u32[]{:S(2)}) %all-to-all-start.3) | async-done | bytes 12320 | tf_op jit(solution)/shard_map/all_to_all | solution.py:41
  105.2 0.1 reshape.41
  105.3 10.6 %collective-permute-start.4 = (bf16[2,8,256]{2,1,0:T(8,128)(2,1)S(1)}, bf16[2,8,256]{2,1,0:T(8,128)(2,1)S(1)}, u32[]{:S(2)}, u32[]{:S(2)}) collective-permute-start(bf16[2,8,256]{2,1,0:T(8,128)(2,1)S(1)} %pad.4), channel_id=1, source_target_pairs={{0,512},{256,768},{512,0},{768,256},{1,513},{257,769},{513,1},{769... | collective-permute-start | bytes 24584 | tf_op jit(solution)/shard_map/ppermute | solution.py:53
  115.9 1.6 %collective-permute-done.4 = bf16[2,8,256]{2,1,0:T(8,128)(2,1)S(1)} collective-permute-done((bf16[2,8,256]{2,1,0:T(8,128)(2,1)S(1)}, bf16[2,8,256]{2,1,0:T(8,128)(2,1)S(1)}, u32[]{:S(2)}, u32[]{:S(2)}) %collective-permute-start.4) | collective-permute-done | bytes 8224 | tf_op jit(solution)/shard_map/ppermute | solution.py:53
  117.5 0.0 collective-permute-done.6.refs_9_
  117.5 0.0 collective-permute-done.5.refs_6_
  117.5 0.0 collective-permute-done.7.refs_10_
  117.5 0.0 copy-done.5
  117.6 0.0 copy-start.4
  117.6 1.5 %shard_map.87 = (f32[2,8,384]{2,1,0:T(8,128)S(1)}, f32[2,8,384]{2,1,0:T(8,128)S(1)}) custom-call(s32[1]{0:T(128)} %bitcast.7.refs_0_, s32[2]{0:T(128)S(1)} %copy-done.5, bf16[2,16,256]{2,1,0:T(8,128)(2,1)S(1)} %pad_maximum_fusion.2.refs_2_, bf16[2,256,256]{2,1,0:T(8,128)(2,1)S(1)} %copy-done.2, bf16[2,256,256]{2,1,0:T(8,128)(2,1)S(1)} %collective-permute-done.1.refs_4_, ...), custom_call_target="tpu_custom_call" | custom-call | tf_op jit(solution)/shard_map/pallas_call | solution.py:133
  119.1 4.8 %collective-permute-start.8 = (f32[2,8,384]{2,1,0:T(8,128)S(1)}, f32[2,8,384]{2,1,0:T(8,128)S(1)}, u32[]{:S(2)}, u32[]{:S(2)}) collective-permute-start(f32[2,8,384]{2,1,0:T(8,128)S(1)} %get-tuple-element.15), channel_id=1, source_target_pairs={{0,512},{256,768},{512,0},{768,256},{1,513},{257,769},{513,1},{769... | collective-permute-start | bytes 73736 | tf_op jit(solution)/shard_map/ppermute | solution.py:53
  123.9 0.1 fusion
  124.1 0.6 reshape.37
  124.7 1.0 collective-permute-done.8.refs_1_
  125.7 0.0 copy-done.4
  125.7 0.9 shard_map.88
  (10 shorter events, 0.1 us)
Async XLA Ops:
  0.6 9.7 %collective-permute-start = (bf16[2,2304]{1,0:T(2,128)(2,1)}, bf16[2,2304]{1,0:T(2,128)(2,1)S(1)}, u32[]{:S(2)}, u32[]{:S(2)}) collective-permute-start(bf16[2,2304]{1,0:T(2,128)(2,1)} %param.7), channel_id=1, source_target_pairs={{0,64},{64,0},{1,65},{65,1},{2,66},{66,2},{3,67},{67,3},{4,68},{68... | collective-permute-start | bytes 27656 | tf_op jit(solution)/shard_map/ppermute | solution.py:179
  11.9 35.2 %all-to-all-start = ((bf16[16,4,2304]{2,1,0:T(4,128)(2,1)}), bf16[16,4,2304]{2,1,0:T(4,128)(2,1)S(1)}, u32[]{:S(2)}, u32[]{:S(2)}) async-start(bf16[16,4,2304]{2,1,0:T(4,128)(2,1)} %broadcast_in_dim.14), calls=%async_computation | async-start | bytes 589824 | tf_op jit(solution)/shard_map/all_to_all | solution.py:41
  33.5 13.7 %collective-permute-start.1 = (bf16[2,256,256]{2,1,0:T(8,128)(2,1)}, bf16[2,256,256]{2,1,0:T(8,128)(2,1)S(1)}, u32[]{:S(2)}, u32[]{:S(2)}) collective-permute-start(bf16[2,256,256]{2,1,0:T(8,128)(2,1)} %refs_3_.2), channel_id=1, source_target_pairs={{0,256},{256,0},{512,768},{768,512},{1,257},{257,1},{513,769},{769... | collective-permute-start | bytes 786440 | tf_op jit(solution)/shard_map/ppermute | solution.py:49
  36.8 11.0 %collective-permute-start.2 = (bf16[2,256,256]{2,1,0:T(8,128)(2,1)}, bf16[2,256,256]{2,1,0:T(8,128)(2,1)S(1)}, u32[]{:S(2)}, u32[]{:S(2)}) collective-permute-start(bf16[2,256,256]{2,1,0:T(8,128)(2,1)} %refs_7_.1), channel_id=1, source_target_pairs={{0,256},{256,0},{512,768},{768,512},{1,257},{257,1},{513,769},{769... | collective-permute-start | bytes 786440 | tf_op jit(solution)/shard_map/ppermute | solution.py:49
  49.0 4.0 %copy-start.2 = (bf16[2,256,256]{2,1,0:T(8,128)(2,1)S(1)}, bf16[2,256,256]{2,1,0:T(8,128)(2,1)}, u32[]{:S(2)}) copy-start(bf16[2,256,256]{2,1,0:T(8,128)(2,1)} %refs_3_.2) | copy-start | bytes 786436
  49.0 14.1 %copy-start.1 = (bf16[2304,96]{0,1:T(8,128)(2,1)S(1)}, bf16[2304,96]{0,1:T(8,128)(2,1)}, u32[]{:S(2)}) copy-start(bf16[2304,96]{0,1:T(8,128)(2,1)} %param.8) | copy-start | bytes 1327108
  49.0 14.1 %all-to-all-start.1 = ((bf16[4,64,2304]{2,1,0:T(8,128)(2,1)}), bf16[4,64,2304]{2,1,0:T(8,128)(2,1)S(1)}, u32[]{:S(2)}, u32[]{:S(2)}) async-start(bf16[4,64,2304]{2,1,0:T(8,128)(2,1)} %broadcast_in_dim.15), calls=%async_computation.1 | async-start | bytes 2359296 | tf_op jit(solution)/shard_map/all_to_all | solution.py:41
  53.0 4.7 %collective-permute-start.3 = (bf16[2,256,256]{2,1,0:T(8,128)(2,1)S(1)}, bf16[2,256,256]{2,1,0:T(8,128)(2,1)S(1)}, u32[]{:S(2)}, u32[]{:S(2)}) collective-permute-start(bf16[2,256,256]{2,1,0:T(8,128)(2,1)S(1)} %copy-done.2), channel_id=1, source_target_pairs={{0,128},{128,0},{1,129},{129,1},{2,130},{130,2},{3,131},{131,3},{4... | collective-permute-start | bytes 786440 | tf_op jit(solution)/shard_map/ppermute | solution.py:57
  63.1 1.8 %copy-start = (bf16[2304,2,288]{0,2,1:T(8,128)(2,1)S(1)}, bf16[2304,2,288]{0,2,1:T(8,128)(2,1)}, u32[]{:S(2)}) copy-start(bf16[2304,2,288]{0,2,1:T(8,128)(2,1)} %param.9) | copy-start | bytes 7962628
  64.9 9.3 %copy-start.3 = (bf16[2,256,256]{2,1,0:T(8,128)(2,1)S(1)}, bf16[2,256,256]{2,1,0:T(8,128)(2,1)}, u32[]{:S(2)}) copy-start(bf16[2,256,256]{2,1,0:T(8,128)(2,1)} %refs_7_.1) | copy-start | bytes 786436
  67.4 50.1 %copy-start.5 = (s32[2]{0:T(128)S(1)}, s32[2]{0:T(128)}, u32[]{:S(2)}) copy-start(s32[2]{0:T(128)} %refs_1_.1) | copy-start | bytes 28
  67.4 16.9 %all-to-all-start.2 = ((bf16[8,32,768]{2,1,0:T(8,128)(2,1)}), bf16[8,32,768]{2,1,0:T(8,128)(2,1)S(1)}, u32[]{:S(2)}, u32[]{:S(2)}) async-start(bf16[8,32,768]{2,1,0:T(8,128)(2,1)} %shard_map.86), calls=%async_computation.2 | async-start | bytes 786432 | tf_op jit(solution)/shard_map/all_to_all | solution.py:41
  74.2 43.3 %collective-permute-start.6 = (bf16[2,256,256]{2,1,0:T(8,128)(2,1)S(1)}, bf16[2,256,256]{2,1,0:T(8,128)(2,1)S(1)}, u32[]{:S(2)}, u32[]{:S(2)}) collective-permute-start(bf16[2,256,256]{2,1,0:T(8,128)(2,1)S(1)} %copy-done.3), channel_id=1, source_target_pairs={{0,128},{128,0},{1,129},{129,1},{2,130},{130,2},{3,131},{131,3},{4... | collective-permute-start | bytes 786440 | tf_op jit(solution)/shard_map/ppermute | solution.py:57
  76.2 41.3 %collective-permute-start.5 = (bf16[2,256,256]{2,1,0:T(8,128)(2,1)S(1)}, bf16[2,256,256]{2,1,0:T(8,128)(2,1)S(1)}, u32[]{:S(2)}, u32[]{:S(2)}) collective-permute-start(bf16[2,256,256]{2,1,0:T(8,128)(2,1)S(1)} %collective-permute-done.1.refs_4_), channel_id=1, source_target_pairs={{0,128},{128,0},{1,129},{129,1},{2,130},{130,2},{3,131},{131,3},{4... | collective-permute-start | bytes 786440 | tf_op jit(solution)/shard_map/ppermute | solution.py:57
  78.5 39.0 %collective-permute-start.7 = (bf16[2,256,256]{2,1,0:T(8,128)(2,1)S(1)}, bf16[2,256,256]{2,1,0:T(8,128)(2,1)S(1)}, u32[]{:S(2)}, u32[]{:S(2)}) collective-permute-start(bf16[2,256,256]{2,1,0:T(8,128)(2,1)S(1)} %collective-permute-done.2.refs_8_), channel_id=1, source_target_pairs={{0,128},{128,0},{1,129},{129,1},{2,130},{130,2},{3,131},{131,3},{4... | collective-permute-start | bytes 786440 | tf_op jit(solution)/shard_map/ppermute | solution.py:57
  85.2 20.0 %all-to-all-start.3 = ((bf16[32,2,96]{2,1,0:T(2,128)(2,1)}), bf16[32,2,96]{2,1,0:T(2,128)(2,1)S(1)}, u32[]{:S(2)}, u32[]{:S(2)}) async-start(bf16[32,2,96]{2,1,0:T(2,128)(2,1)} %copy.13), calls=%async_computation.3 | async-start | bytes 32768 | tf_op jit(solution)/shard_map/all_to_all | solution.py:41
  105.3 12.2 %collective-permute-start.4 = (bf16[2,8,256]{2,1,0:T(8,128)(2,1)S(1)}, bf16[2,8,256]{2,1,0:T(8,128)(2,1)S(1)}, u32[]{:S(2)}, u32[]{:S(2)}) collective-permute-start(bf16[2,8,256]{2,1,0:T(8,128)(2,1)S(1)} %pad.4), channel_id=1, source_target_pairs={{0,512},{256,768},{512,0},{768,256},{1,513},{257,769},{513,1},{769... | collective-permute-start | bytes 24584 | tf_op jit(solution)/shard_map/ppermute | solution.py:53
  117.6 8.2 %copy-start.4 = (bf16[2,2,256]{2,1,0:T(2,128)(2,1)S(1)}, bf16[2,2,256]{2,1,0:T(2,128)(2,1)}, u32[]{:S(2)}) copy-start(bf16[2,2,256]{2,1,0:T(2,128)(2,1)} %refs_3_.3) | copy-start | bytes 6148
  119.1 6.6 %collective-permute-start.8 = (f32[2,8,384]{2,1,0:T(8,128)S(1)}, f32[2,8,384]{2,1,0:T(8,128)S(1)}, u32[]{:S(2)}, u32[]{:S(2)}) collective-permute-start(f32[2,8,384]{2,1,0:T(8,128)S(1)} %get-tuple-element.15), channel_id=1, source_target_pairs={{0,512},{256,768},{512,0},{768,256},{1,513},{257,769},{513,1},{769... | collective-permute-start | bytes 73736 | tf_op jit(solution)/shard_map/ppermute | solution.py:53

commit v5 on v1

--- a/solution.py
+++ b/solution.py
@@ -8,7 +8,6 @@
 NEG = -1e30
 GX = ("xl", "core")
 GY = ("xh", "z", "y")
-ALL = GX + GY
 LATTICE = ("xh", "z", "y")
 PLANE = ("core", "z", "y")
 
@@ -32,12 +31,12 @@
     return groups
 
 
-def query_groups():
-    def half(g, h):
-        return [g * 128 + h * 16 + i for i in range(16)]
-
-    pairs = [(g, h) for g in range(8) for h in range(g + 1, 8)]
-    return [half(g, h) + half(h, g) for g, h in pairs] + [half(g, g) + half(g + 1, g + 1) for g in range(0, 8, 2)]
+def column_groups():
+    return [[zh * 16 + i for i in range(16)] for zh in range(4)]
+
+
+def transposition(flip):
+    return [(g * 16 + h * 2 + lo, (h ^ flip) * 16 + g * 2 + lo) for g in range(8) for h in range(8) for lo in range(2)]
 
 
 def exchange(x, axis, groups=None):
@@ -189,16 +188,14 @@
     hidden = hidden.reshape(2, 2, 4, 2, width).transpose(0, 2, 1, 3, 4).reshape(32, width)
     query = (total[:, 2 * width : 2 * width + qw] + total[:, 2 * width + qw :]).astype(bf16)
 
-    query = query.reshape(2, 2, 4, 2, qw).transpose(0, 2, 1, 3, 4).reshape(16, 2, qw)
-    query = exchange(jnp.concatenate([query, query], axis=0), ALL, query_groups())
-    place = lax.axis_index(GX)
-    block = lax.axis_index("xh") * 4 + lax.axis_index("z") // 2
-    sender = jnp.where(place == block, place % 2, (place < block).astype(place.dtype))
-    query = lax.dynamic_slice_in_dim(query, sender * 16, 16, 0)
+    query = query.reshape(2, 2, 4, 2, qw).transpose(0, 2, 1, 3, 4).reshape(16, seqs, qw)
+    query = exchange(query, ("z", "y"), column_groups())
     per_dev = 16 * qw // head_dim
     query = query.transpose(1, 0, 2).reshape(seqs, per_dev, head_dim)
     query = jnp.pad(query, ((0, 0), (0, 8 - per_dev), (0, 0)))
-    queries = jnp.concatenate([query, across(query)], axis=1)
+    queries = [lax.ppermute(query, ("xl", "core", "xh", "z"), transposition(flip)) for flip in (0, 4)]
+    queries = jnp.concatenate(queries, axis=1)
+    place = lax.axis_index(GX)
 
     keys = (key_cache, keys_b, keys_c, keys_d)
     values = (value_cache, values_b, values_c, values_d)

time: 121 us -> 125 us (1.033)
  blocking collectives: 0 us -> 14.3 us
  starting transfers between devices: 80.1 us -> 68.8 us
  waiting for transfers between devices: 28 us -> 29.5 us
    all_to_all x0 -> x1, blocking collectives: none -> 14.3 us  [exchange(): return lax.all_to_all(x, axis, 0, 0, axis_index_groups=groups, tiled=True)]
    ppermute x0 -> x2, starting transfers between devices: none -> 12.6 us  [body(): lax.ppermute(query, ('xl', 'core', 'xh', 'z'), transposition(flip))]
    ppermute x2 -> x1, starting transfers between devices: 13.9 us -> 1.92 us  [across(): return lax.ppermute(x, 'xl', [(i, i ^ 2) for i in range(4)])]
    all_to_all x4 -> x3, starting transfers between devices: 49.5 us -> 37.5 us  [exchange(): return lax.all_to_all(x, axis, 0, 0, axis_index_groups=groups, tiled=True)]
    ppermute x0 -> x2, waiting for transfers between devices: none -> 7.13 us  [body(): lax.ppermute(query, ('xl', 'core', 'xh', 'z'), transposition(flip))]
    all_to_all x4 -> x3, waiting for transfers between devices: 22.2 us -> 15.2 us  [exchange(): return lax.all_to_all(x, axis, 0, 0, axis_index_groups=groups, tiled=True)]
    ppermute x2 -> x1, waiting for transfers between devices: 2.63 us -> 3.92 us  [across(): return lax.ppermute(x, 'xl', [(i, i ^ 2) for i in range(4)])]
  transfers between devices with their start and end apart: 12 -> 12, of which waited for: 7 -> 6; matrix products, arithmetic and copies ran while one was open for 1% -> 1% of each run, Pallas kernels for 0% -> 0%
where the time goes in v5:
time: 125 us; the launch traced here: 124 us
  starting transfers between devices  68.8 us (55%)
  waiting for transfers between devices  29.5 us (24%)
  blocking collectives  14.3 us (11%)
  local copies, waits for them, and re-layouts  5.38 us (4%)
  Pallas kernels  4.65 us (4%)
    all_to_all x3, starting transfers between devices, exchange(): return lax.all_to_all(x, axis, 0, 0, axis_index_groups=groups, tiled=True)  37.5 us
    all_to_all x3, waiting for transfers between devices, exchange(): return lax.all_to_all(x, axis, 0, 0, axis_index_groups=groups, tiled=True)  15.2 us
    all_to_all x1, blocking collectives, exchange(): return lax.all_to_all(x, axis, 0, 0, axis_index_groups=groups, tiled=True)  14.3 us
    ppermute x2, starting transfers between devices, body(): lax.ppermute(query, ('xl', 'core', 'xh', 'z'), transposition(flip))  12.6 us
    ppermute x4, starting transfers between devices, other_core(): return lax.ppermute(x, 'core', [(0, 1), (1, 0)])  9.5 us
    ppermute x2, starting transfers between devices, beside(): return lax.ppermute(x, 'xl', [(i, i ^ 1) for i in range(4)])  7.24 us
    ppermute x2, waiting for transfers between devices, body(): lax.ppermute(query, ('xl', 'core', 'xh', 'z'), transposition(flip))  7.13 us
    ppermute x1, waiting for transfers between devices, across(): return lax.ppermute(x, 'xl', [(i, i ^ 2) for i in range(4)])  3.92 us
  transfers between devices with their start and end apart: 12, of which 6 were waited for; matrix products, arithmetic and copies ran while one was open for 1% of the time, Pallas kernels for 0%

profile of v5, /device:TPU:14, one launch (start us, length us, event | category | flops | bytes accessed | tf_op | source)
XLA Modules:
  0.0 123.6 jit_solution(9352801291794746347)
XLA Ops:
  0.6 1.6 %broadcast_in_dim.4 = bf16[32,2,2304]{2,1,0:T(2,128)(2,1)} broadcast(bf16[2,2304]{1,0:T(2,128)(2,1)} %param.7), dimensions={1,2} | broadcast | bytes 304128 | tf_op jit(solution)/shard_map/broadcast_in_dim | solution.py:47
  2.2 27.0 %all-to-all-start = ((bf16[32,2,2304]{2,1,0:T(2,128)(2,1)}), bf16[32,2,2304]{2,1,0:T(2,128)(2,1)S(1)}, u32[]{:S(2)}, u32[]{:S(2)}) async-start(bf16[32,2,2304]{2,1,0:T(2,128)(2,1)} %broadcast_in_dim.4), calls=%async_computation | async-start | bytes 589824 | tf_op jit(solution)/shard_map/all_to_all | solution.py:43
  29.2 3.3 %collective-permute-start = (bf16[2,256,256]{2,1,0:T(8,128)(2,1)}, bf16[2,256,256]{2,1,0:T(8,128)(2,1)S(1)}, u32[]{:S(2)}, u32[]{:S(2)}) collective-permute-start(bf16[2,256,256]{2,1,0:T(8,128)(2,1)} %refs_3_.2), channel_id=1, source_target_pairs={{0,256},{256,0},{512,768},{768,512},{1,257},{257,1},{513,769},{769... | collective-permute-start | bytes 786440 | tf_op jit(solution)/shard_map/ppermute | solution.py:51
  32.6 11.4 %all-to-all-done = bf16[32,2,2304]{2,1,0:T(2,128)(2,1)S(1)} async-done(((bf16[32,2,2304]{2,1,0:T(2,128)(2,1)}), bf16[32,2,2304]{2,1,0:T(2,128)(2,1)S(1)}, u32[]{:S(2)}, u32[]{:S(2)}) %all-to-all-start) | async-done | bytes 294944 | tf_op jit(solution)/shard_map/all_to_all | solution.py:43
  43.9 0.1 reshape.33
  44.0 0.0 collective-permute-done.refs_4_
  44.0 1.1 broadcast_in_dim.5
  45.2 0.0 copy-start.3
  45.2 0.0 copy-start.2
  45.2 0.0 copy-start.1
  45.2 3.8 %all-to-all-start.1 = ((bf16[4,64,2304]{2,1,0:T(8,128)(2,1)}), bf16[4,64,2304]{2,1,0:T(8,128)(2,1)S(1)}, u32[]{:S(2)}, u32[]{:S(2)}) async-start(bf16[4,64,2304]{2,1,0:T(8,128)(2,1)} %broadcast_in_dim.5), calls=%async_computation.1 | async-start | bytes 2359296 | tf_op jit(solution)/shard_map/all_to_all | solution.py:43
  49.0 0.0 copy-done.3
  49.0 3.9 %collective-permute-start.1 = (bf16[2,256,256]{2,1,0:T(8,128)(2,1)S(1)}, bf16[2,256,256]{2,1,0:T(8,128)(2,1)S(1)}, u32[]{:S(2)}, u32[]{:S(2)}) collective-permute-start(bf16[2,256,256]{2,1,0:T(8,128)(2,1)S(1)} %copy-done.3), channel_id=1, source_target_pairs={{0,256},{256,0},{512,768},{768,512},{1,257},{257,1},{513,769},{769... | collective-permute-start | bytes 786440 | tf_op jit(solution)/shard_map/ppermute | solution.py:51
  52.9 0.0 copy-done.2
  52.9 3.1 %collective-permute-start.2 = (bf16[2,256,256]{2,1,0:T(8,128)(2,1)S(1)}, bf16[2,256,256]{2,1,0:T(8,128)(2,1)S(1)}, u32[]{:S(2)}, u32[]{:S(2)}) collective-permute-start(bf16[2,256,256]{2,1,0:T(8,128)(2,1)S(1)} %copy-done.2), channel_id=1, source_target_pairs={{0,128},{128,0},{1,129},{129,1},{2,130},{130,2},{3,131},{131,3},{4... | collective-permute-start | bytes 786440 | tf_op jit(solution)/shard_map/ppermute | solution.py:59
  56.0 3.2 %collective-permute-done.1.refs_8_ = bf16[2,256,256]{2,1,0:T(8,128)(2,1)S(1)} collective-permute-done((bf16[2,256,256]{2,1,0:T(8,128)(2,1)S(1)}, bf16[2,256,256]{2,1,0:T(8,128)(2,1)S(1)}, u32[]{:S(2)}, u32[]{:S(2)}) %collective-permute-start.1) | collective-permute-done | bytes 262176 | tf_op jit(solution)/shard_map/ppermute | solution.py:51
  59.2 0.0 collective-permute-done.2.refs_5_
  59.2 0.1 all-to-all-done.1
  59.3 0.0 copy-done.1
  59.3 0.0 copy-start
  59.3 1.7 %copy-done = bf16[2304,2,288]{0,2,1:T(8,128)(2,1)S(1)} copy-done((bf16[2304,2,288]{0,2,1:T(8,128)(2,1)S(1)}, bf16[2304,2,288]{0,2,1:T(8,128)(2,1)}, u32[]{:S(2)}) %copy-start) | copy-done | bytes 2654232
  61.0 2.3 %shard_map.86 = bf16[8,32,768]{2,1,0:T(8,128)(2,1)} custom-call(bf16[256,2304]{1,0:T(8,128)(2,1)S(1)} %bitcast.12, bf16[576,2304]{1,0:T(8,128)(2,1)S(1)} %bitcast.13, bf16[96,2304]{1,0:T(8,128)(2,1)S(1)} %bitcast.14), custom_call_target="tpu_custom_call" | custom-call | tf_op jit(solution)/shard_map/pallas_call | solution.py:85
  63.3 0.0 copy-start.5
  63.3 6.7 %all-to-all-start.2 = ((bf16[8,32,768]{2,1,0:T(8,128)(2,1)}), bf16[8,32,768]{2,1,0:T(8,128)(2,1)S(1)}, u32[]{:S(2)}, u32[]{:S(2)}) async-start(bf16[8,32,768]{2,1,0:T(8,128)(2,1)} %shard_map.86), calls=%async_computation.2 | async-start | bytes 786432 | tf_op jit(solution)/shard_map/all_to_all | solution.py:43
  70.0 2.0 %collective-permute-start.6 = (bf16[2,256,256]{2,1,0:T(8,128)(2,1)S(1)}, bf16[2,256,256]{2,1,0:T(8,128)(2,1)S(1)}, u32[]{:S(2)}, u32[]{:S(2)}) collective-permute-start(bf16[2,256,256]{2,1,0:T(8,128)(2,1)S(1)} %copy-done.3), channel_id=1, source_target_pairs={{0,128},{128,0},{1,129},{129,1},{2,130},{130,2},{3,131},{131,3},{4... | collective-permute-start | bytes 786440 | tf_op jit(solution)/shard_map/ppermute | solution.py:59
  72.1 2.3 %collective-permute-start.5 = (bf16[2,256,256]{2,1,0:T(8,128)(2,1)S(1)}, bf16[2,256,256]{2,1,0:T(8,128)(2,1)S(1)}, u32[]{:S(2)}, u32[]{:S(2)}) collective-permute-start(bf16[2,256,256]{2,1,0:T(8,128)(2,1)S(1)} %collective-permute-done.refs_4_), channel_id=1, source_target_pairs={{0,128},{128,0},{1,129},{129,1},{2,130},{130,2},{3,131},{131,3},{4... | collective-permute-start | bytes 786440 | tf_op jit(solution)/shard_map/ppermute | solution.py:59
  74.4 2.1 %collective-permute-start.7 = (bf16[2,256,256]{2,1,0:T(8,128)(2,1)S(1)}, bf16[2,256,256]{2,1,0:T(8,128)(2,1)S(1)}, u32[]{:S(2)}, u32[]{:S(2)}) collective-permute-start(bf16[2,256,256]{2,1,0:T(8,128)(2,1)S(1)} %collective-permute-done.1.refs_8_), channel_id=1, source_target_pairs={{0,128},{128,0},{1,129},{129,1},{2,130},{130,2},{3,131},{131,3},{4... | collective-permute-start | bytes 786440 | tf_op jit(solution)/shard_map/ppermute | solution.py:59
  76.4 3.8 %all-to-all-done.2 = bf16[8,32,768]{2,1,0:T(8,128)(2,1)S(1)} async-done(((bf16[8,32,768]{2,1,0:T(8,128)(2,1)}), bf16[8,32,768]{2,1,0:T(8,128)(2,1)S(1)}, u32[]{:S(2)}, u32[]{:S(2)}) %all-to-all-start.2) | async-done | bytes 393248 | tf_op jit(solution)/shard_map/all_to_all | solution.py:43
  80.2 0.1 convert_reduce_fusion
  80.3 0.1 fusion.1
  80.4 14.3 %all_to_all.20 = bf16[16,2,96]{2,1,0:T(2,128)(2,1)S(1)} all-to-all(bf16[16,2,96]{2,1,0:T(2,128)(2,1)S(1)} %copy.13), channel_id=1, replica_groups={{0,1,2,3,4,5,6,7,8,9,10,11,12,13,14,15},{16,17,18,19,20,21,22,23,24,25,..., dimensions={0} | all-to-all | bytes 12288 | tf_op jit(solution)/shard_map/all_to_all | solution.py:43
  94.7 0.1 reshape.41
  94.8 6.4 %collective-permute-start.3 = (bf16[2,8,256]{2,1,0:T(8,128)(2,1)S(1)}, bf16[2,8,256]{2,1,0:T(8,128)(2,1)S(1)}, u32[]{:S(2)}, u32[]{:S(2)}) collective-permute-start(bf16[2,8,256]{2,1,0:T(8,128)(2,1)S(1)} %pad.4), channel_id=1, source_target_pairs={{0,0},{8,8},{16,128},{24,136},{32,256},{40,264},{48,384},{56,392},... | collective-permute-start | bytes 24584 | tf_op jit(solution)/shard_map/ppermute | solution.py:196
  101.2 6.2 %collective-permute-start.4 = (bf16[2,8,256]{2,1,0:T(8,128)(2,1)S(1)}, bf16[2,8,256]{2,1,0:T(8,128)(2,1)S(1)}, u32[]{:S(2)}, u32[]{:S(2)}) collective-permute-start(bf16[2,8,256]{2,1,0:T(8,128)(2,1)S(1)} %pad.4), channel_id=1, source_target_pairs={{0,512},{8,520},{16,640},{24,648},{32,768},{40,776},{48,896},{56,9... | collective-permute-start | bytes 24584 | tf_op jit(solution)/shard_map/ppermute | solution.py:196
  107.4 0.0 collective-permute-done.3
  107.4 7.1 %collective-permute-done.4 = bf16[2,8,256]{2,1,0:T(8,128)(2,1)S(1)} collective-permute-done((bf16[2,8,256]{2,1,0:T(8,128)(2,1)S(1)}, bf16[2,8,256]{2,1,0:T(8,128)(2,1)S(1)}, u32[]{:S(2)}, u32[]{:S(2)}) %collective-permute-start.4) | collective-permute-done | bytes 8224 | tf_op jit(solution)/shard_map/ppermute | solution.py:196
  114.5 0.0 collective-permute-done.6.refs_9_
  114.5 0.0 collective-permute-done.5.refs_6_
  114.6 0.0 collective-permute-done.7.refs_10_
  114.6 0.0 copy-done.5
  114.6 0.0 copy-start.4
  114.6 1.5 %shard_map.87 = (f32[2,8,384]{2,1,0:T(8,128)S(1)}, f32[2,8,384]{2,1,0:T(8,128)S(1)}) custom-call(s32[1]{0:T(128)} %bitcast.5.refs_0_, s32[2]{0:T(128)S(1)} %copy-done.5, bf16[2,16,256]{2,1,0:T(8,128)(2,1)S(1)} %constant_dynamic-update-slice_fusion.refs_2_, bf16[2,256,256]{2,1,0:T(8,128)(2,1)S(1)} %copy-done.2, ...), custom_call_target="tpu_custom_call" | custom-call | tf_op jit(solution)/shard_map/pallas_call | solution.py:131
  116.1 1.9 %collective-permute-start.8 = (f32[2,8,384]{2,1,0:T(8,128)S(1)}, f32[2,8,384]{2,1,0:T(8,128)S(1)}, u32[]{:S(2)}, u32[]{:S(2)}) collective-permute-start(f32[2,8,384]{2,1,0:T(8,128)S(1)} %get-tuple-element.15), channel_id=1, source_target_pairs={{0,512},{256,768},{512,0},{768,256},{1,513},{257,769},{513,1},{769... | collective-permute-start | bytes 73736 | tf_op jit(solution)/shard_map/ppermute | solution.py:55
  118.0 0.1 fusion
  118.2 0.6 reshape.37
  118.8 3.9 %collective-permute-done.8.refs_1_ = f32[2,8,384]{2,1,0:T(8,128)S(1)} collective-permute-done((f32[2,8,384]{2,1,0:T(8,128)S(1)}, f32[2,8,384]{2,1,0:T(8,128)S(1)}, u32[]{:S(2)}, u32[]{:S(2)}) %collective-permute-start.8) | collective-permute-done | bytes 24608 | tf_op jit(solution)/shard_map/ppermute | solution.py:55
  122.7 0.0 copy-done.4
  122.7 0.9 shard_map.88
  (8 shorter events, 0.1 us)
Async XLA Ops:
  2.2 41.7 %all-to-all-start = ((bf16[32,2,2304]{2,1,0:T(2,128)(2,1)}), bf16[32,2,2304]{2,1,0:T(2,128)(2,1)S(1)}, u32[]{:S(2)}, u32[]{:S(2)}) async-start(bf16[32,2,2304]{2,1,0:T(2,128)(2,1)} %broadcast_in_dim.4), calls=%async_computation | async-start | bytes 589824 | tf_op jit(solution)/shard_map/all_to_all | solution.py:43
  29.2 14.8 %collective-permute-start = (bf16[2,256,256]{2,1,0:T(8,128)(2,1)}, bf16[2,256,256]{2,1,0:T(8,128)(2,1)S(1)}, u32[]{:S(2)}, u32[]{:S(2)}) collective-permute-start(bf16[2,256,256]{2,1,0:T(8,128)(2,1)} %refs_3_.2), channel_id=1, source_target_pairs={{0,256},{256,0},{512,768},{768,512},{1,257},{257,1},{513,769},{769... | collective-permute-start | bytes 786440 | tf_op jit(solution)/shard_map/ppermute | solution.py:51
  45.2 3.8 %copy-start.3 = (bf16[2,256,256]{2,1,0:T(8,128)(2,1)S(1)}, bf16[2,256,256]{2,1,0:T(8,128)(2,1)}, u32[]{:S(2)}) copy-start(bf16[2,256,256]{2,1,0:T(8,128)(2,1)} %refs_7_.1) | copy-start | bytes 786436
  45.2 7.7 %copy-start.2 = (bf16[2,256,256]{2,1,0:T(8,128)(2,1)S(1)}, bf16[2,256,256]{2,1,0:T(8,128)(2,1)}, u32[]{:S(2)}) copy-start(bf16[2,256,256]{2,1,0:T(8,128)(2,1)} %refs_3_.2) | copy-start | bytes 786436
  45.2 14.1 %copy-start.1 = (bf16[2304,96]{0,1:T(8,128)(2,1)S(1)}, bf16[2304,96]{0,1:T(8,128)(2,1)}, u32[]{:S(2)}) copy-start(bf16[2304,96]{0,1:T(8,128)(2,1)} %param.8) | copy-start | bytes 1327108
  45.2 14.1 %all-to-all-start.1 = ((bf16[4,64,2304]{2,1,0:T(8,128)(2,1)}), bf16[4,64,2304]{2,1,0:T(8,128)(2,1)S(1)}, u32[]{:S(2)}, u32[]{:S(2)}) async-start(bf16[4,64,2304]{2,1,0:T(8,128)(2,1)} %broadcast_in_dim.5), calls=%async_computation.1 | async-start | bytes 2359296 | tf_op jit(solution)/shard_map/all_to_all | solution.py:43
  49.0 10.2 %collective-permute-start.1 = (bf16[2,256,256]{2,1,0:T(8,128)(2,1)S(1)}, bf16[2,256,256]{2,1,0:T(8,128)(2,1)S(1)}, u32[]{:S(2)}, u32[]{:S(2)}) collective-permute-start(bf16[2,256,256]{2,1,0:T(8,128)(2,1)S(1)} %copy-done.3), channel_id=1, source_target_pairs={{0,256},{256,0},{512,768},{768,512},{1,257},{257,1},{513,769},{769... | collective-permute-start | bytes 786440 | tf_op jit(solution)/shard_map/ppermute | solution.py:51
  52.9 6.3 %collective-permute-start.2 = (bf16[2,256,256]{2,1,0:T(8,128)(2,1)S(1)}, bf16[2,256,256]{2,1,0:T(8,128)(2,1)S(1)}, u32[]{:S(2)}, u32[]{:S(2)}) collective-permute-start(bf16[2,256,256]{2,1,0:T(8,128)(2,1)S(1)} %copy-done.2), channel_id=1, source_target_pairs={{0,128},{128,0},{1,129},{129,1},{2,130},{130,2},{3,131},{131,3},{4... | collective-permute-start | bytes 786440 | tf_op jit(solution)/shard_map/ppermute | solution.py:59
  59.3 1.8 %copy-start = (bf16[2304,2,288]{0,2,1:T(8,128)(2,1)S(1)}, bf16[2304,2,288]{0,2,1:T(8,128)(2,1)}, u32[]{:S(2)}) copy-start(bf16[2304,2,288]{0,2,1:T(8,128)(2,1)} %param.9) | copy-start | bytes 7962628
  63.3 51.3 %copy-start.5 = (s32[2]{0:T(128)S(1)}, s32[2]{0:T(128)}, u32[]{:S(2)}) copy-start(s32[2]{0:T(128)} %refs_1_.1) | copy-start | bytes 28
  63.3 16.9 %all-to-all-start.2 = ((bf16[8,32,768]{2,1,0:T(8,128)(2,1)}), bf16[8,32,768]{2,1,0:T(8,128)(2,1)S(1)}, u32[]{:S(2)}, u32[]{:S(2)}) async-start(bf16[8,32,768]{2,1,0:T(8,128)(2,1)} %shard_map.86), calls=%async_computation.2 | async-start | bytes 786432 | tf_op jit(solution)/shard_map/all_to_all | solution.py:43
  70.0 44.5 %collective-permute-start.6 = (bf16[2,256,256]{2,1,0:T(8,128)(2,1)S(1)}, bf16[2,256,256]{2,1,0:T(8,128)(2,1)S(1)}, u32[]{:S(2)}, u32[]{:S(2)}) collective-permute-start(bf16[2,256,256]{2,1,0:T(8,128)(2,1)S(1)} %copy-done.3), channel_id=1, source_target_pairs={{0,128},{128,0},{1,129},{129,1},{2,130},{130,2},{3,131},{131,3},{4... | collective-permute-start | bytes 786440 | tf_op jit(solution)/shard_map/ppermute | solution.py:59
  72.1 42.5 %collective-permute-start.5 = (bf16[2,256,256]{2,1,0:T(8,128)(2,1)S(1)}, bf16[2,256,256]{2,1,0:T(8,128)(2,1)S(1)}, u32[]{:S(2)}, u32[]{:S(2)}) collective-permute-start(bf16[2,256,256]{2,1,0:T(8,128)(2,1)S(1)} %collective-permute-done.refs_4_), channel_id=1, source_target_pairs={{0,128},{128,0},{1,129},{129,1},{2,130},{130,2},{3,131},{131,3},{4... | collective-permute-start | bytes 786440 | tf_op jit(solution)/shard_map/ppermute | solution.py:59
  74.4 40.2 %collective-permute-start.7 = (bf16[2,256,256]{2,1,0:T(8,128)(2,1)S(1)}, bf16[2,256,256]{2,1,0:T(8,128)(2,1)S(1)}, u32[]{:S(2)}, u32[]{:S(2)}) collective-permute-start(bf16[2,256,256]{2,1,0:T(8,128)(2,1)S(1)} %collective-permute-done.1.refs_8_), channel_id=1, source_target_pairs={{0,128},{128,0},{1,129},{129,1},{2,130},{130,2},{3,131},{131,3},{4... | collective-permute-start | bytes 786440 | tf_op jit(solution)/shard_map/ppermute | solution.py:59
  94.8 12.6 %collective-permute-start.3 = (bf16[2,8,256]{2,1,0:T(8,128)(2,1)S(1)}, bf16[2,8,256]{2,1,0:T(8,128)(2,1)S(1)}, u32[]{:S(2)}, u32[]{:S(2)}) collective-permute-start(bf16[2,8,256]{2,1,0:T(8,128)(2,1)S(1)} %pad.4), channel_id=1, source_target_pairs={{0,0},{8,8},{16,128},{24,136},{32,256},{40,264},{48,384},{56,392},... | collective-permute-start | bytes 24584 | tf_op jit(solution)/shard_map/ppermute | solution.py:196
  101.2 13.4 %collective-permute-start.4 = (bf16[2,8,256]{2,1,0:T(8,128)(2,1)S(1)}, bf16[2,8,256]{2,1,0:T(8,128)(2,1)S(1)}, u32[]{:S(2)}, u32[]{:S(2)}) collective-permute-start(bf16[2,8,256]{2,1,0:T(8,128)(2,1)S(1)} %pad.4), channel_id=1, source_target_pairs={{0,512},{8,520},{16,640},{24,648},{32,768},{40,776},{48,896},{56,9... | collective-permute-start | bytes 24584 | tf_op jit(solution)/shard_map/ppermute | solution.py:196
  114.6 8.2 %copy-start.4 = (bf16[2,2,256]{2,1,0:T(2,128)(2,1)S(1)}, bf16[2,2,256]{2,1,0:T(2,128)(2,1)}, u32[]{:S(2)}) copy-start(bf16[2,2,256]{2,1,0:T(2,128)(2,1)} %refs_3_.3) | copy-start | bytes 6148
  116.1 6.6 %collective-permute-start.8 = (f32[2,8,384]{2,1,0:T(8,128)S(1)}, f32[2,8,384]{2,1,0:T(8,128)S(1)}, u32[]{:S(2)}, u32[]{:S(2)}) collective-permute-start(f32[2,8,384]{2,1,0:T(8,128)S(1)} %get-tuple-element.15), channel_id=1, source_target_pairs={{0,512},{256,768},{512,0},{768,256},{1,513},{257,769},{513,1},{769... | collective-permute-start | bytes 73736 | tf_op jit(solution)/shard_map/ppermute | solution.py:55

commit v6 on v1

--- a/solution.py
+++ b/solution.py
@@ -93,10 +93,11 @@
 
 def attend_kernel(order, place_ref, lengths_ref, q_ref, *refs):
     n = len(order)
-    keys, values, (mine_ref, theirs_ref) = refs[:n], refs[n : 2 * n], refs[2 * n :]
+    keys, values, out_ref = refs[:n], refs[n : 2 * n], refs[2 * n]
     seqs, block_len, head_dim = keys[0].shape
     scale = head_dim ** (-0.5)
-    slot = lax.broadcasted_iota(jnp.int32, (16, block_len), 1)
+    slot = lax.broadcasted_iota(jnp.int32, (8, block_len), 1)
+    lane = lax.broadcasted_iota(jnp.int32, (8, 128), 1)
     for r in range(seqs):
         q = q_ref[r]
         scores, valid = [], []
@@ -109,22 +110,21 @@
         for s in scores[1:]:
             top = jnp.maximum(top, s)
         top = jnp.max(top, axis=1, keepdims=True)
-        total = jnp.zeros((16, 1), jnp.float32)
-        mixed = jnp.zeros((16, head_dim), jnp.float32)
-        for j in range(n):
-            p = jnp.where(valid[j], jnp.exp(scores[j] - top), 0.0)
-            total += jnp.sum(p, axis=1, keepdims=True)
-            mixed += jnp.dot(p.astype(jnp.bfloat16), values[j][r], preferred_element_type=jnp.float32)
-        for ref, rows in ((mine_ref, slice(0, 8)), (theirs_ref, slice(8, 16))):
-            ref[r, :, :head_dim] = mixed[rows]
-            lane = lax.broadcasted_iota(jnp.int32, (8, 128), 1)
-            ref[r, :, head_dim:] = jnp.where(lane < 64, top[rows], total[rows])
+        probs = [jnp.where(ok, jnp.exp(s - top), 0.0) for s, ok in zip(scores, valid)]
+        total = probs[0]
+        for p in probs[1:]:
+            total = total + p
+        total = jnp.sum(total, axis=1, keepdims=True)
+        mixed = jnp.zeros((8, head_dim), jnp.float32)
+        for p, v in zip(probs, values):
+            mixed += jnp.dot(p.astype(jnp.bfloat16), v[r], preferred_element_type=jnp.float32)
+        out_ref[r, :, :head_dim] = mixed
+        out_ref[r, :, head_dim:] = jnp.where(lane < 64, top, total)
 
 
 def attend(place, lengths, queries, keys, values, order):
     seqs, _, head_dim = queries.shape
     smem, vmem = pl.BlockSpec(memory_space=pltpu.SMEM), pl.BlockSpec(memory_space=pltpu.VMEM)
-    out = jax.ShapeDtypeStruct((seqs, 8, head_dim + 128), jnp.float32)
 
     def kernel(*refs):
         attend_kernel(order, *refs)
@@ -132,8 +132,8 @@
     return pl.pallas_call(
         kernel,
         in_specs=[smem, smem] + [vmem] * (1 + 2 * len(order)),
-        out_specs=(vmem, vmem),
-        out_shape=(out, out),
+        out_specs=vmem,
+        out_shape=jax.ShapeDtypeStruct((seqs, 8, head_dim + 128), jnp.float32),
         compiler_params=LIMIT,
     )(place.reshape(1).astype(jnp.int32), lengths, queries, *keys, *values)
 
@@ -145,7 +145,7 @@
     for r in range(seqs):
         mine, theirs = mine_ref[r], theirs_ref[r]
         new = new_ref[r].astype(jnp.float32)
-        q = q_ref[r].astype(jnp.float32)[:8]
+        q = q_ref[r].astype(jnp.float32)
         own = jnp.sum(q * new[0:1], axis=1, keepdims=True) * scale
         tops = [p[:, head_dim : head_dim + 1] for p in (mine, theirs)]
         sums = [p[:, head_dim + 64 : head_dim + 65] for p in (mine, theirs)]
@@ -198,12 +198,12 @@
     per_dev = 16 * qw // head_dim
     query = query.transpose(1, 0, 2).reshape(seqs, per_dev, head_dim)
     query = jnp.pad(query, ((0, 0), (0, 8 - per_dev), (0, 0)))
-    queries = jnp.concatenate([query, across(query)], axis=1)
 
     keys = (key_cache, keys_b, keys_c, keys_d)
     values = (value_cache, values_b, values_c, values_d)
-    mine, theirs = attend(place, lengths, queries, keys, values, (0, 2, 1, 3))
-    attended = finish(mine, across(theirs), queries, new_kv, per_dev)
+    mine = attend(place, lengths, query, keys, values, (0, 2, 1, 3))
+    theirs = attend(place, lengths, across(query), keys, values, (0, 2, 1, 3))
+    attended = finish(mine, across(theirs), query, new_kv, per_dev)
     return (hidden, attended)
 
 

time: 121 us -> 121 us (level)
  Pallas kernels: 4.66 us -> 6.17 us
    pallas_call x1 -> x2, Pallas kernels: 1.53 us -> 3.04 us  [attend(): pl.pallas_call(kernel, in_specs=[smem, smem] + [vmem] * (1 + 2 * len(orde...]
  transfers between devices with their start and end apart: 12 -> 12, of which waited for: 7 -> 6; matrix products, arithmetic and copies ran while one was open for 1% -> 1% of each run, Pallas kernels for 0% -> 1%
where the time goes in v6:
time: 121 us; the launch traced here: 120 us
  starting transfers between devices  80.3 us (66%)
  waiting for transfers between devices  27 us (22%)
  Pallas kernels  6.17 us (5%)
  local copies, waits for them, and re-layouts  5.99 us (5%)
    all_to_all x4, starting transfers between devices, exchange(): return lax.all_to_all(x, axis, 0, 0, axis_index_groups=groups, tiled=True)  49.5 us
    all_to_all x4, waiting for transfers between devices, exchange(): return lax.all_to_all(x, axis, 0, 0, axis_index_groups=groups, tiled=True)  22.2 us
    ppermute x2, starting transfers between devices, across(): return lax.ppermute(x, 'xl', [(i, i ^ 2) for i in range(4)])  14 us
    ppermute x4, starting transfers between devices, other_core(): return lax.ppermute(x, 'core', [(0, 1), (1, 0)])  9.5 us
    ppermute x2, starting transfers between devices, beside(): return lax.ppermute(x, 'xl', [(i, i ^ 1) for i in range(4)])  7.24 us
    ppermute x2, waiting for transfers between devices, beside(): return lax.ppermute(x, 'xl', [(i, i ^ 1) for i in range(4)])  3.18 us
    pallas_call x2, Pallas kernels, attend(): pl.pallas_call(kernel, in_specs=[smem, smem] + [vmem] * (1 + 2 * len(orde...  3.04 us
    broadcast_in_dim x2, local copies, waits for them, and re-layouts, spread(): return exchange(jnp.broadcast_to(x[None], (n,) + x.shape), axis, groups)  2.69 us
  transfers between devices with their start and end apart: 12, of which 6 were waited for; matrix products, arithmetic and copies ran while one was open for 1% of the time, Pallas kernels for 1%

profile of v6, /device:TPU:14, one launch (start us, length us, event | category | flops | bytes accessed | tf_op | source)
XLA Modules:
  0.0 120.5 jit_solution(11516839286744698741)
XLA Ops:
  0.6 1.6 %broadcast_in_dim.4 = bf16[32,2,2304]{2,1,0:T(2,128)(2,1)} broadcast(bf16[2,2304]{1,0:T(2,128)(2,1)} %param.7), dimensions={1,2} | broadcast | bytes 304128 | tf_op jit(solution)/shard_map/broadcast_in_dim | solution.py:48
  2.2 27.0 %all-to-all-start = ((bf16[32,2,2304]{2,1,0:T(2,128)(2,1)}), bf16[32,2,2304]{2,1,0:T(2,128)(2,1)S(1)}, u32[]{:S(2)}, u32[]{:S(2)}) async-start(bf16[32,2,2304]{2,1,0:T(2,128)(2,1)} %broadcast_in_dim.4), calls=%async_computation | async-start | bytes 589824 | tf_op jit(solution)/shard_map/all_to_all | solution.py:44
  29.2 3.3 %collective-permute-start = (bf16[2,256,256]{2,1,0:T(8,128)(2,1)}, bf16[2,256,256]{2,1,0:T(8,128)(2,1)S(1)}, u32[]{:S(2)}, u32[]{:S(2)}) collective-permute-start(bf16[2,256,256]{2,1,0:T(8,128)(2,1)} %refs_3_.4), channel_id=1, source_target_pairs={{0,256},{256,0},{512,768},{768,512},{1,257},{257,1},{513,769},{769... | collective-permute-start | bytes 786440 | tf_op jit(solution)/shard_map/ppermute | solution.py:52
  32.6 11.4 %all-to-all-done = bf16[32,2,2304]{2,1,0:T(2,128)(2,1)S(1)} async-done(((bf16[32,2,2304]{2,1,0:T(2,128)(2,1)}), bf16[32,2,2304]{2,1,0:T(2,128)(2,1)S(1)}, u32[]{:S(2)}, u32[]{:S(2)}) %all-to-all-start) | async-done | bytes 294944 | tf_op jit(solution)/shard_map/all_to_all | solution.py:44
  43.9 0.1 reshape.34
  44.0 0.0 collective-permute-done.refs_4_
  44.0 1.1 broadcast_in_dim.5
  45.2 0.0 copy-start.2
  45.2 0.0 copy-start.1
  45.2 0.0 copy-start.3
  45.2 3.8 %all-to-all-start.1 = ((bf16[4,64,2304]{2,1,0:T(8,128)(2,1)}), bf16[4,64,2304]{2,1,0:T(8,128)(2,1)S(1)}, u32[]{:S(2)}, u32[]{:S(2)}) async-start(bf16[4,64,2304]{2,1,0:T(8,128)(2,1)} %broadcast_in_dim.5), calls=%async_computation.1 | async-start | bytes 2359296 | tf_op jit(solution)/shard_map/all_to_all | solution.py:44
  49.0 0.0 copy-done.2
  49.0 3.9 %collective-permute-start.1 = (bf16[2,256,256]{2,1,0:T(8,128)(2,1)S(1)}, bf16[2,256,256]{2,1,0:T(8,128)(2,1)S(1)}, u32[]{:S(2)}, u32[]{:S(2)}) collective-permute-start(bf16[2,256,256]{2,1,0:T(8,128)(2,1)S(1)} %copy-done.2), channel_id=1, source_target_pairs={{0,256},{256,0},{512,768},{768,512},{1,257},{257,1},{513,769},{769... | collective-permute-start | bytes 786440 | tf_op jit(solution)/shard_map/ppermute | solution.py:52
  52.9 0.0 copy-done.1
  52.9 3.1 %collective-permute-start.2 = (bf16[2,256,256]{2,1,0:T(8,128)(2,1)S(1)}, bf16[2,256,256]{2,1,0:T(8,128)(2,1)S(1)}, u32[]{:S(2)}, u32[]{:S(2)}) collective-permute-start(bf16[2,256,256]{2,1,0:T(8,128)(2,1)S(1)} %copy-done.1), channel_id=1, source_target_pairs={{0,128},{128,0},{1,129},{129,1},{2,130},{130,2},{3,131},{131,3},{4... | collective-permute-start | bytes 786440 | tf_op jit(solution)/shard_map/ppermute | solution.py:60
  56.0 3.2 %collective-permute-done.1.refs_8_ = bf16[2,256,256]{2,1,0:T(8,128)(2,1)S(1)} collective-permute-done((bf16[2,256,256]{2,1,0:T(8,128)(2,1)S(1)}, bf16[2,256,256]{2,1,0:T(8,128)(2,1)S(1)}, u32[]{:S(2)}, u32[]{:S(2)}) %collective-permute-start.1) | collective-permute-done | bytes 262176 | tf_op jit(solution)/shard_map/ppermute | solution.py:52
  59.2 0.0 collective-permute-done.2.refs_5_
  59.2 0.1 all-to-all-done.1
  59.3 0.0 copy-done.3
  59.3 0.0 copy-start
  59.3 1.7 %copy-done = bf16[2304,2,288]{0,2,1:T(8,128)(2,1)S(1)} copy-done((bf16[2304,2,288]{0,2,1:T(8,128)(2,1)S(1)}, bf16[2304,2,288]{0,2,1:T(8,128)(2,1)}, u32[]{:S(2)}) %copy-start) | copy-done | bytes 2654232
  61.0 2.3 %shard_map.86 = bf16[8,32,768]{2,1,0:T(8,128)(2,1)} custom-call(bf16[256,2304]{1,0:T(8,128)(2,1)S(1)} %bitcast.13, bf16[576,2304]{1,0:T(8,128)(2,1)S(1)} %bitcast.14, bf16[96,2304]{1,0:T(8,128)(2,1)S(1)} %bitcast.15), custom_call_target="tpu_custom_call" | custom-call | tf_op jit(solution)/shard_map/pallas_call | solution.py:86
  63.3 0.0 copy-start.5
  63.3 6.7 %all-to-all-start.2 = ((bf16[8,32,768]{2,1,0:T(8,128)(2,1)}), bf16[8,32,768]{2,1,0:T(8,128)(2,1)S(1)}, u32[]{:S(2)}, u32[]{:S(2)}) async-start(bf16[8,32,768]{2,1,0:T(8,128)(2,1)} %shard_map.86), calls=%async_computation.2 | async-start | bytes 786432 | tf_op jit(solution)/shard_map/all_to_all | solution.py:44
  70.0 2.0 %collective-permute-start.4 = (bf16[2,256,256]{2,1,0:T(8,128)(2,1)S(1)}, bf16[2,256,256]{2,1,0:T(8,128)(2,1)S(1)}, u32[]{:S(2)}, u32[]{:S(2)}) collective-permute-start(bf16[2,256,256]{2,1,0:T(8,128)(2,1)S(1)} %copy-done.2), channel_id=1, source_target_pairs={{0,128},{128,0},{1,129},{129,1},{2,130},{130,2},{3,131},{131,3},{4... | collective-permute-start | bytes 786440 | tf_op jit(solution)/shard_map/ppermute | solution.py:60
  72.1 2.3 %collective-permute-start.3 = (bf16[2,256,256]{2,1,0:T(8,128)(2,1)S(1)}, bf16[2,256,256]{2,1,0:T(8,128)(2,1)S(1)}, u32[]{:S(2)}, u32[]{:S(2)}) collective-permute-start(bf16[2,256,256]{2,1,0:T(8,128)(2,1)S(1)} %collective-permute-done.refs_4_), channel_id=1, source_target_pairs={{0,128},{128,0},{1,129},{129,1},{2,130},{130,2},{3,131},{131,3},{4... | collective-permute-start | bytes 786440 | tf_op jit(solution)/shard_map/ppermute | solution.py:60
  74.4 2.1 %collective-permute-start.5 = (bf16[2,256,256]{2,1,0:T(8,128)(2,1)S(1)}, bf16[2,256,256]{2,1,0:T(8,128)(2,1)S(1)}, u32[]{:S(2)}, u32[]{:S(2)}) collective-permute-start(bf16[2,256,256]{2,1,0:T(8,128)(2,1)S(1)} %collective-permute-done.1.refs_8_), channel_id=1, source_target_pairs={{0,128},{128,0},{1,129},{129,1},{2,130},{130,2},{3,131},{131,3},{4... | collective-permute-start | bytes 786440 | tf_op jit(solution)/shard_map/ppermute | solution.py:60
  76.4 3.8 %all-to-all-done.2 = bf16[8,32,768]{2,1,0:T(8,128)(2,1)S(1)} async-done(((bf16[8,32,768]{2,1,0:T(8,128)(2,1)}), bf16[8,32,768]{2,1,0:T(8,128)(2,1)S(1)}, u32[]{:S(2)}, u32[]{:S(2)}) %all-to-all-start.2) | async-done | bytes 393248 | tf_op jit(solution)/shard_map/all_to_all | solution.py:44
  80.2 0.1 convert_reduce_fusion
  80.3 0.1 fusion.1
  80.4 0.6 copy.13
  81.0 12.0 %all-to-all-start.3 = ((bf16[32,2,96]{2,1,0:T(2,128)(2,1)}), bf16[32,2,96]{2,1,0:T(2,128)(2,1)S(1)}, u32[]{:S(2)}, u32[]{:S(2)}) async-start(bf16[32,2,96]{2,1,0:T(2,128)(2,1)} %copy.13), calls=%async_computation.3 | async-start | bytes 32768 | tf_op jit(solution)/shard_map/all_to_all | solution.py:44
  93.0 7.0 %all-to-all-done.3 = bf16[32,2,96]{2,1,0:T(2,128)(2,1)S(1)} async-done(((bf16[32,2,96]{2,1,0:T(2,128)(2,1)}), bf16[32,2,96]{2,1,0:T(2,128)(2,1)S(1)}, u32[]{:S(2)}, u32[]{:S(2)}) %all-to-all-start.3) | async-done | bytes 12320 | tf_op jit(solution)/shard_map/all_to_all | solution.py:44
  100.0 0.1 reshape.42
  100.1 9.1 %collective-permute-start.6 = (bf16[2,8,256]{2,1,0:T(8,128)(2,1)S(1)}, bf16[2,8,256]{2,1,0:T(8,128)(2,1)S(1)}, u32[]{:S(2)}, u32[]{:S(2)}) collective-permute-start(bf16[2,8,256]{2,1,0:T(8,128)(2,1)S(1)} %pad.4.refs_2_), channel_id=1, source_target_pairs={{0,512},{256,768},{512,0},{768,256},{1,513},{257,769},{513,1},{769... | collective-permute-start | bytes 24584 | tf_op jit(solution)/shard_map/ppermute | solution.py:56
  109.2 0.0 collective-permute-done.4.refs_9_
  109.2 0.0 collective-permute-done.3.refs_6_
  109.2 0.0 collective-permute-done.5.refs_10_
  109.2 1.6 %collective-permute-done.6.refs_2_ = bf16[2,8,256]{2,1,0:T(8,128)(2,1)S(1)} collective-permute-done((bf16[2,8,256]{2,1,0:T(8,128)(2,1)S(1)}, bf16[2,8,256]{2,1,0:T(8,128)(2,1)S(1)}, u32[]{:S(2)}, u32[]{:S(2)}) %collective-permute-start.6) | collective-permute-done | bytes 8224 | tf_op jit(solution)/shard_map/ppermute | solution.py:56
  110.8 0.0 copy-done.5
  110.8 1.5 %shard_map.88 = f32[2,8,384]{2,1,0:T(8,128)S(1)} custom-call(s32[1]{0:T(128)} %bitcast.5.refs_0_, s32[2]{0:T(128)S(1)} %copy-done.5, bf16[2,8,256]{2,1,0:T(8,128)(2,1)S(1)} %collective-permute-done.6.refs_2_, bf16[2,256,256]{2,1,0:T(8,128)(2,1)S(1)} %copy-done.1, bf16[2,256,256]{2,1,0:T(8,128)(2,1)S(1)} %collective-permute-done.refs_4_, ...), custom_call_target="tpu_custom_call" | custom-call | tf_op jit(solution)/shard_map/pallas_call | solution.py:132
  112.3 0.0 copy-start.4
  112.3 5.0 %collective-permute-start.7 = (f32[2,8,384]{2,1,0:T(8,128)S(1)}, f32[2,8,384]{2,1,0:T(8,128)S(1)}, u32[]{:S(2)}, u32[]{:S(2)}) collective-permute-start(f32[2,8,384]{2,1,0:T(8,128)S(1)} %shard_map.88), channel_id=1, source_target_pairs={{0,512},{256,768},{512,0},{768,256},{1,513},{257,769},{513,1},{769... | collective-permute-start | bytes 73736 | tf_op jit(solution)/shard_map/ppermute | solution.py:56
  117.3 0.1 fusion
  117.4 0.6 reshape.38
  118.1 1.5 %shard_map.87.refs_0_ = f32[2,8,384]{2,1,0:T(8,128)S(1)} custom-call(s32[1]{0:T(128)} %bitcast.5.refs_0_, s32[2]{0:T(128)S(1)} %copy-done.5, bf16[2,8,256]{2,1,0:T(8,128)(2,1)S(1)} %pad.4.refs_2_, bf16[2,256,256]{2,1,0:T(8,128)(2,1)S(1)} %copy-done.1, bf16[2,256,256]{2,1,0:T(8,128)(2,1)S(1)} %collective-permute-done.refs_4_, ...), custom_call_target="tpu_custom_call" | custom-call | tf_op jit(solution)/shard_map/pallas_call | solution.py:132
  119.6 0.0 collective-permute-done.7.refs_1_
  119.6 0.0 copy-done.4
  119.6 0.9 shard_map.89
  (7 shorter events, 0.1 us)
Async XLA Ops:
  2.2 41.7 %all-to-all-start = ((bf16[32,2,2304]{2,1,0:T(2,128)(2,1)}), bf16[32,2,2304]{2,1,0:T(2,128)(2,1)S(1)}, u32[]{:S(2)}, u32[]{:S(2)}) async-start(bf16[32,2,2304]{2,1,0:T(2,128)(2,1)} %broadcast_in_dim.4), calls=%async_computation | async-start | bytes 589824 | tf_op jit(solution)/shard_map/all_to_all | solution.py:44
  29.2 14.8 %collective-permute-start = (bf16[2,256,256]{2,1,0:T(8,128)(2,1)}, bf16[2,256,256]{2,1,0:T(8,128)(2,1)S(1)}, u32[]{:S(2)}, u32[]{:S(2)}) collective-permute-start(bf16[2,256,256]{2,1,0:T(8,128)(2,1)} %refs_3_.4), channel_id=1, source_target_pairs={{0,256},{256,0},{512,768},{768,512},{1,257},{257,1},{513,769},{769... | collective-permute-start | bytes 786440 | tf_op jit(solution)/shard_map/ppermute | solution.py:52
  45.2 3.8 %copy-start.2 = (bf16[2,256,256]{2,1,0:T(8,128)(2,1)S(1)}, bf16[2,256,256]{2,1,0:T(8,128)(2,1)}, u32[]{:S(2)}) copy-start(bf16[2,256,256]{2,1,0:T(8,128)(2,1)} %refs_7_.3) | copy-start | bytes 786436
  45.2 7.7 %copy-start.1 = (bf16[2,256,256]{2,1,0:T(8,128)(2,1)S(1)}, bf16[2,256,256]{2,1,0:T(8,128)(2,1)}, u32[]{:S(2)}) copy-start(bf16[2,256,256]{2,1,0:T(8,128)(2,1)} %refs_3_.4) | copy-start | bytes 786436
  45.2 14.1 %copy-start.3 = (bf16[2304,96]{0,1:T(8,128)(2,1)S(1)}, bf16[2304,96]{0,1:T(8,128)(2,1)}, u32[]{:S(2)}) copy-start(bf16[2304,96]{0,1:T(8,128)(2,1)} %param.8) | copy-start | bytes 1327108
  45.2 14.1 %all-to-all-start.1 = ((bf16[4,64,2304]{2,1,0:T(8,128)(2,1)}), bf16[4,64,2304]{2,1,0:T(8,128)(2,1)S(1)}, u32[]{:S(2)}, u32[]{:S(2)}) async-start(bf16[4,64,2304]{2,1,0:T(8,128)(2,1)} %broadcast_in_dim.5), calls=%async_computation.1 | async-start | bytes 2359296 | tf_op jit(solution)/shard_map/all_to_all | solution.py:44
  49.0 10.2 %collective-permute-start.1 = (bf16[2,256,256]{2,1,0:T(8,128)(2,1)S(1)}, bf16[2,256,256]{2,1,0:T(8,128)(2,1)S(1)}, u32[]{:S(2)}, u32[]{:S(2)}) collective-permute-start(bf16[2,256,256]{2,1,0:T(8,128)(2,1)S(1)} %copy-done.2), channel_id=1, source_target_pairs={{0,256},{256,0},{512,768},{768,512},{1,257},{257,1},{513,769},{769... | collective-permute-start | bytes 786440 | tf_op jit(solution)/shard_map/ppermute | solution.py:52
  52.9 6.3 %collective-permute-start.2 = (bf16[2,256,256]{2,1,0:T(8,128)(2,1)S(1)}, bf16[2,256,256]{2,1,0:T(8,128)(2,1)S(1)}, u32[]{:S(2)}, u32[]{:S(2)}) collective-permute-start(bf16[2,256,256]{2,1,0:T(8,128)(2,1)S(1)} %copy-done.1), channel_id=1, source_target_pairs={{0,128},{128,0},{1,129},{129,1},{2,130},{130,2},{3,131},{131,3},{4... | collective-permute-start | bytes 786440 | tf_op jit(solution)/shard_map/ppermute | solution.py:60
  59.3 1.8 %copy-start = (bf16[2304,2,288]{0,2,1:T(8,128)(2,1)S(1)}, bf16[2304,2,288]{0,2,1:T(8,128)(2,1)}, u32[]{:S(2)}) copy-start(bf16[2304,2,288]{0,2,1:T(8,128)(2,1)} %param.9) | copy-start | bytes 7962628
  63.3 47.5 %copy-start.5 = (s32[2]{0:T(128)S(1)}, s32[2]{0:T(128)}, u32[]{:S(2)}) copy-start(s32[2]{0:T(128)} %refs_1_.3) | copy-start | bytes 28
  63.3 16.9 %all-to-all-start.2 = ((bf16[8,32,768]{2,1,0:T(8,128)(2,1)}), bf16[8,32,768]{2,1,0:T(8,128)(2,1)S(1)}, u32[]{:S(2)}, u32[]{:S(2)}) async-start(bf16[8,32,768]{2,1,0:T(8,128)(2,1)} %shard_map.86), calls=%async_computation.2 | async-start | bytes 786432 | tf_op jit(solution)/shard_map/all_to_all | solution.py:44
  70.0 39.1 %collective-permute-start.4 = (bf16[2,256,256]{2,1,0:T(8,128)(2,1)S(1)}, bf16[2,256,256]{2,1,0:T(8,128)(2,1)S(1)}, u32[]{:S(2)}, u32[]{:S(2)}) collective-permute-start(bf16[2,256,256]{2,1,0:T(8,128)(2,1)S(1)} %copy-done.2), channel_id=1, source_target_pairs={{0,128},{128,0},{1,129},{129,1},{2,130},{130,2},{3,131},{131,3},{4... | collective-permute-start | bytes 786440 | tf_op jit(solution)/shard_map/ppermute | solution.py:60
  72.1 37.1 %collective-permute-start.3 = (bf16[2,256,256]{2,1,0:T(8,128)(2,1)S(1)}, bf16[2,256,256]{2,1,0:T(8,128)(2,1)S(1)}, u32[]{:S(2)}, u32[]{:S(2)}) collective-permute-start(bf16[2,256,256]{2,1,0:T(8,128)(2,1)S(1)} %collective-permute-done.refs_4_), channel_id=1, source_target_pairs={{0,128},{128,0},{1,129},{129,1},{2,130},{130,2},{3,131},{131,3},{4... | collective-permute-start | bytes 786440 | tf_op jit(solution)/shard_map/ppermute | solution.py:60
  74.4 34.8 %collective-permute-start.5 = (bf16[2,256,256]{2,1,0:T(8,128)(2,1)S(1)}, bf16[2,256,256]{2,1,0:T(8,128)(2,1)S(1)}, u32[]{:S(2)}, u32[]{:S(2)}) collective-permute-start(bf16[2,256,256]{2,1,0:T(8,128)(2,1)S(1)} %collective-permute-done.1.refs_8_), channel_id=1, source_target_pairs={{0,128},{128,0},{1,129},{129,1},{2,130},{130,2},{3,131},{131,3},{4... | collective-permute-start | bytes 786440 | tf_op jit(solution)/shard_map/ppermute | solution.py:60
  81.0 19.0 %all-to-all-start.3 = ((bf16[32,2,96]{2,1,0:T(2,128)(2,1)}), bf16[32,2,96]{2,1,0:T(2,128)(2,1)S(1)}, u32[]{:S(2)}, u32[]{:S(2)}) async-start(bf16[32,2,96]{2,1,0:T(2,128)(2,1)} %copy.13), calls=%async_computation.3 | async-start | bytes 32768 | tf_op jit(solution)/shard_map/all_to_all | solution.py:44
  100.1 10.7 %collective-permute-start.6 = (bf16[2,8,256]{2,1,0:T(8,128)(2,1)S(1)}, bf16[2,8,256]{2,1,0:T(8,128)(2,1)S(1)}, u32[]{:S(2)}, u32[]{:S(2)}) collective-permute-start(bf16[2,8,256]{2,1,0:T(8,128)(2,1)S(1)} %pad.4.refs_2_), channel_id=1, source_target_pairs={{0,512},{256,768},{512,0},{768,256},{1,513},{257,769},{513,1},{769... | collective-permute-start | bytes 24584 | tf_op jit(solution)/shard_map/ppermute | solution.py:56
  112.3 7.3 %copy-start.4 = (bf16[2,2,256]{2,1,0:T(2,128)(2,1)S(1)}, bf16[2,2,256]{2,1,0:T(2,128)(2,1)}, u32[]{:S(2)}) copy-start(bf16[2,2,256]{2,1,0:T(2,128)(2,1)} %refs_3_.5) | copy-start | bytes 6148
  112.3 7.3 %collective-permute-start.7 = (f32[2,8,384]{2,1,0:T(8,128)S(1)}, f32[2,8,384]{2,1,0:T(8,128)S(1)}, u32[]{:S(2)}, u32[]{:S(2)}) collective-permute-start(f32[2,8,384]{2,1,0:T(8,128)S(1)} %shard_map.88), channel_id=1, source_target_pairs={{0,512},{256,768},{512,0},{768,256},{1,513},{257,769},{513,1},{769... | collective-permute-start | bytes 73736 | tf_op jit(solution)/shard_map/ppermute | solution.py:56

commit v7 on v1

--- a/solution.py
+++ b/solution.py
@@ -64,31 +64,28 @@
 LIMIT = pltpu.CompilerParams(vmem_limit_bytes=16 * 2**20)
 
 
-def project_kernel(x_ref, wg_ref, wq_ref, out_ref, acc_ref):
-    x = x_ref[...]
-    width, qw = wg_ref.shape[0], wq_ref.shape[0]
-    gate_up = lax.dot_general(x, wg_ref[...], NT, preferred_element_type=jnp.float32)
-    query = lax.dot_general(x, wq_ref[...], NT, preferred_element_type=jnp.float32)
+def project_kernel(low, x_ref, w_ref, out_ref, acc_ref):
+    full = lax.dot_general(x_ref[...], w_ref[...], NT, preferred_element_type=jnp.float32)
+    width = full.shape[1]
     for p in range(4):
-        rows = slice(p * 64, p * 64 + 64)
-        acc_ref[:, p * 8 : p * 8 + 8, :width] = gate_up[rows].reshape(8, 8, width)
-        part = query[rows].reshape(8, 8, qw)
-        acc_ref[:, p * 8 : p * 8 + 8, width : width + qw] = part
-        acc_ref[:, p * 8 : p * 8 + 8, width + qw :] = part - part.astype(jnp.bfloat16).astype(jnp.float32)
+        part = full[p * 64 : p * 64 + 64].reshape(8, 8, width)
+        acc_ref[:, p * 8 : p * 8 + 8, :width] = part
+        if low:
+            acc_ref[:, p * 8 : p * 8 + 8, width:] = part - part.astype(jnp.bfloat16).astype(jnp.float32)
     out_ref[...] = acc_ref[...].astype(jnp.bfloat16)
 
 
-def project(rows, w_query, w_gate_up):
-    d, _, width = w_gate_up.shape
-    wg = w_gate_up.transpose(1, 2, 0).reshape(2 * width, d)
-    wq = w_query.T
-    shape = (8, rows.shape[0] // 8, 2 * width + 2 * wq.shape[0])
+def project(rows, weights, low):
+    def kernel(*refs):
+        project_kernel(low, *refs)
+
+    shape = (8, rows.shape[0] // 8, weights.shape[0] * (1 + low))
     return pl.pallas_call(
-        project_kernel,
+        kernel,
         out_shape=jax.ShapeDtypeStruct(shape, jnp.bfloat16),
         scratch_shapes=[pltpu.VMEM(shape, jnp.float32)],
         compiler_params=LIMIT,
-    )(rows, wg, wq)
+    )(rows, weights)
 
 
 def attend_kernel(order, place_ref, lengths_ref, q_ref, *refs):
@@ -175,22 +172,23 @@
     d, width, qw = tokens.shape[1], w_gate_up.shape[2], w_query.shape[1]
     seqs, _, head_dim = key_cache.shape
 
-    keys_b = beside(key_cache)
+    keys_b, keys_c = beside(key_cache), other_core(key_cache)
     rows = spread(tokens, LATTICE, 32, far_groups()).reshape(64, d)
-    rows, keys_b = lax.optimization_barrier((rows, keys_b))
-    values_b, keys_c = beside(value_cache), other_core(key_cache)
+    rows, keys_b, keys_c = lax.optimization_barrier((rows, keys_b, keys_c))
+    values_b = beside(value_cache)
     rows = spread(rows, PLANE, 4, near_groups()).reshape(256, d)
-    rows, values_b, keys_c = lax.optimization_barrier((rows, values_b, keys_c))
+    rows, values_b = lax.optimization_barrier((rows, values_b))
     values_c, keys_d, values_d = other_core(value_cache), other_core(keys_b), other_core(values_b)
 
-    got = exchange(project(rows, w_query, w_gate_up), GX).astype(f32)
-    total = jnp.sum(got, axis=0)
-    hidden = (jax.nn.silu(total[:, :width]) * total[:, width : 2 * width]).astype(bf16)
-    hidden = hidden.reshape(2, 2, 4, 2, width).transpose(0, 2, 1, 3, 4).reshape(32, width)
-    query = (total[:, 2 * width : 2 * width + qw] + total[:, 2 * width + qw :]).astype(bf16)
+    got = exchange(project(rows, w_query.T, True), GX)
+    got, values_c, keys_d = lax.optimization_barrier((got, values_c, keys_d))
+    total = jnp.sum(got.astype(f32), axis=0)
+    query = (total[:, :qw] + total[:, qw:]).astype(bf16)
 
     query = query.reshape(2, 2, 4, 2, qw).transpose(0, 2, 1, 3, 4).reshape(16, 2, qw)
     query = exchange(jnp.concatenate([query, query], axis=0), ALL, query_groups())
+    gate_up = project(rows, w_gate_up.transpose(1, 2, 0).reshape(2 * width, d), False)
+    query, gate_up, values_d = lax.optimization_barrier((query, gate_up, values_d))
     place = lax.axis_index(GX)
     block = lax.axis_index("xh") * 4 + lax.axis_index("z") // 2
     sender = jnp.where(place == block, place % 2, (place < block).astype(place.dtype))
@@ -204,6 +202,9 @@
     values = (value_cache, values_b, values_c, values_d)
     mine, theirs = attend(place, lengths, queries, keys, values, (0, 2, 1, 3))
     attended = finish(mine, across(theirs), queries, new_kv, per_dev)
+    total = jnp.sum(exchange(gate_up, GX).astype(f32), axis=0)
+    hidden = (jax.nn.silu(total[:, :width]) * total[:, width:]).astype(bf16)
+    hidden = hidden.reshape(2, 2, 4, 2, width).transpose(0, 2, 1, 3, 4).reshape(32, width)
     return (hidden, attended)
 
 

time: 121 us -> 121 us (level)
    all_to_all x4 -> x5, starting transfers between devices: 49.5 us -> 59.7 us  [exchange(): return lax.all_to_all(x, axis, 0, 0, axis_index_groups=groups, tiled=True)]
    ppermute x2, starting transfers between devices: 13.9 us -> 5.26 us  [across(): return lax.ppermute(x, 'xl', [(i, i ^ 2) for i in range(4)])]
    ppermute x2, waiting for transfers between devices: 2.63 us -> 10.2 us  [across(): return lax.ppermute(x, 'xl', [(i, i ^ 2) for i in range(4)])]
    all_to_all x4 -> x5, waiting for transfers between devices: 22.2 us -> 15.4 us  [exchange(): return lax.all_to_all(x, axis, 0, 0, axis_index_groups=groups, tiled=True)]
    ppermute x2, waiting for transfers between devices: 3.18 us -> 1.27 us  [beside(): return lax.ppermute(x, 'xl', [(i, i ^ 1) for i in range(4)])]
    pallas_call x1 -> x2, Pallas kernels: 2.27 us -> 3.08 us  [project(): pl.pallas_call(kernel, out_shape=jax.ShapeDtypeStruct(shape, jnp.bfloat16...]
  transfers between devices with their start and end apart: 12 -> 13, of which waited for: 7 -> 7; matrix products, arithmetic and copies ran while one was open for 1% -> 1% of each run, Pallas kernels for 0% -> 5%
where the time goes in v7:
time: 121 us
  starting transfers between devices  81.2 us (67%)
  waiting for transfers between devices  26.8 us (22%)
  local copies, waits for them, and re-layouts  5.99 us (5%)
  Pallas kernels  5.47 us (5%)
    all_to_all x5, starting transfers between devices, exchange(): return lax.all_to_all(x, axis, 0, 0, axis_index_groups=groups, tiled=True)  59.7 us
    all_to_all x5, waiting for transfers between devices, exchange(): return lax.all_to_all(x, axis, 0, 0, axis_index_groups=groups, tiled=True)  15.4 us
    ppermute x2, waiting for transfers between devices, across(): return lax.ppermute(x, 'xl', [(i, i ^ 2) for i in range(4)])  10.2 us
    ppermute x4, starting transfers between devices, other_core(): return lax.ppermute(x, 'core', [(0, 1), (1, 0)])  9.01 us
    ppermute x2, starting transfers between devices, beside(): return lax.ppermute(x, 'xl', [(i, i ^ 1) for i in range(4)])  7.24 us
    ppermute x2, starting transfers between devices, across(): return lax.ppermute(x, 'xl', [(i, i ^ 2) for i in range(4)])  5.26 us
    pallas_call x2, Pallas kernels, project(): pl.pallas_call(kernel, out_shape=jax.ShapeDtypeStruct(shape, jnp.bfloat16...  3.08 us
    broadcast_in_dim x2, local copies, waits for them, and re-layouts, spread(): return exchange(jnp.broadcast_to(x[None], (n,) + x.shape), axis, groups)  2.69 us
  transfers between devices with their start and end apart: 13, of which 7 were waited for; matrix products, arithmetic and copies ran while one was open for 1% of the time, Pallas kernels for 5%

profile of v7, /device:TPU:14, one launch (start us, length us, event | category | flops | bytes accessed | tf_op | source)
XLA Modules:
  0.0 120.5 jit_solution(14848588043213260236)
XLA Ops:
  0.6 1.6 %broadcast_in_dim.4 = bf16[32,2,2304]{2,1,0:T(2,128)(2,1)} broadcast(bf16[2,2304]{1,0:T(2,128)(2,1)} %param.7), dimensions={1,2} | broadcast | bytes 304128 | tf_op jit(solution)/shard_map/broadcast_in_dim | solution.py:48
  2.2 27.0 %all-to-all-start = ((bf16[32,2,2304]{2,1,0:T(2,128)(2,1)}), bf16[32,2,2304]{2,1,0:T(2,128)(2,1)S(1)}, u32[]{:S(2)}, u32[]{:S(2)}) async-start(bf16[32,2,2304]{2,1,0:T(2,128)(2,1)} %broadcast_in_dim.4), calls=%async_computation | async-start | bytes 589824 | tf_op jit(solution)/shard_map/all_to_all | solution.py:44
  29.2 3.3 %collective-permute-start = (bf16[2,256,256]{2,1,0:T(8,128)(2,1)}, bf16[2,256,256]{2,1,0:T(8,128)(2,1)S(1)}, u32[]{:S(2)}, u32[]{:S(2)}) collective-permute-start(bf16[2,256,256]{2,1,0:T(8,128)(2,1)} %refs_3_.2), channel_id=1, source_target_pairs={{0,256},{256,0},{512,768},{768,512},{1,257},{257,1},{513,769},{769... | collective-permute-start | bytes 786440 | tf_op jit(solution)/shard_map/ppermute | solution.py:52
  32.6 1.9 %collective-permute-start.1 = (bf16[2,256,256]{2,1,0:T(8,128)(2,1)}, bf16[2,256,256]{2,1,0:T(8,128)(2,1)S(1)}, u32[]{:S(2)}, u32[]{:S(2)}) collective-permute-start(bf16[2,256,256]{2,1,0:T(8,128)(2,1)} %refs_3_.2), channel_id=1, source_target_pairs={{0,128},{128,0},{1,129},{129,1},{2,130},{130,2},{3,131},{131,3},{4... | collective-permute-start | bytes 786440 | tf_op jit(solution)/shard_map/ppermute | solution.py:60
  34.5 9.4 %all-to-all-done = bf16[32,2,2304]{2,1,0:T(2,128)(2,1)S(1)} async-done(((bf16[32,2,2304]{2,1,0:T(2,128)(2,1)}), bf16[32,2,2304]{2,1,0:T(2,128)(2,1)S(1)}, u32[]{:S(2)}, u32[]{:S(2)}) %all-to-all-start) | async-done | bytes 294944 | tf_op jit(solution)/shard_map/all_to_all | solution.py:44
  43.9 0.1 reshape.33
  44.0 0.0 collective-permute-done.refs_4_
  44.0 0.0 collective-permute-done.1.refs_5_
  44.1 1.1 broadcast_in_dim.5
  45.2 0.0 copy-start.3
  45.2 0.0 copy-start.1
  45.2 3.8 %all-to-all-start.1 = ((bf16[4,64,2304]{2,1,0:T(8,128)(2,1)}), bf16[4,64,2304]{2,1,0:T(8,128)(2,1)S(1)}, u32[]{:S(2)}, u32[]{:S(2)}) async-start(bf16[4,64,2304]{2,1,0:T(8,128)(2,1)} %broadcast_in_dim.5), calls=%async_computation.1 | async-start | bytes 2359296 | tf_op jit(solution)/shard_map/all_to_all | solution.py:44
  49.0 0.0 copy-done.3
  49.0 3.9 %collective-permute-start.2 = (bf16[2,256,256]{2,1,0:T(8,128)(2,1)S(1)}, bf16[2,256,256]{2,1,0:T(8,128)(2,1)S(1)}, u32[]{:S(2)}, u32[]{:S(2)}) collective-permute-start(bf16[2,256,256]{2,1,0:T(8,128)(2,1)S(1)} %copy-done.3), channel_id=1, source_target_pairs={{0,256},{256,0},{512,768},{768,512},{1,257},{257,1},{513,769},{769... | collective-permute-start | bytes 786440 | tf_op jit(solution)/shard_map/ppermute | solution.py:52
  52.9 3.1 %collective-permute-start.3 = (bf16[2,256,256]{2,1,0:T(8,128)(2,1)S(1)}, bf16[2,256,256]{2,1,0:T(8,128)(2,1)S(1)}, u32[]{:S(2)}, u32[]{:S(2)}) collective-permute-start(bf16[2,256,256]{2,1,0:T(8,128)(2,1)S(1)} %copy-done.3), channel_id=1, source_target_pairs={{0,128},{128,0},{1,129},{129,1},{2,130},{130,2},{3,131},{131,3},{4... | collective-permute-start | bytes 786440 | tf_op jit(solution)/shard_map/ppermute | solution.py:60
  56.0 1.9 %collective-permute-start.4 = (bf16[2,256,256]{2,1,0:T(8,128)(2,1)S(1)}, bf16[2,256,256]{2,1,0:T(8,128)(2,1)S(1)}, u32[]{:S(2)}, u32[]{:S(2)}) collective-permute-start(bf16[2,256,256]{2,1,0:T(8,128)(2,1)S(1)} %collective-permute-done.refs_4_), channel_id=1, source_target_pairs={{0,128},{128,0},{1,129},{129,1},{2,130},{130,2},{3,131},{131,3},{4... | collective-permute-start | bytes 786440 | tf_op jit(solution)/shard_map/ppermute | solution.py:60
  57.9 1.3 %collective-permute-done.2.refs_8_ = bf16[2,256,256]{2,1,0:T(8,128)(2,1)S(1)} collective-permute-done((bf16[2,256,256]{2,1,0:T(8,128)(2,1)S(1)}, bf16[2,256,256]{2,1,0:T(8,128)(2,1)S(1)}, u32[]{:S(2)}, u32[]{:S(2)}) %collective-permute-start.2) | collective-permute-done | bytes 262176 | tf_op jit(solution)/shard_map/ppermute | solution.py:52
  59.2 0.1 all-to-all-done.1
  59.3 0.0 copy-done.1
  59.3 1.2 %shard_map.86 = bf16[8,32,192]{2,1,0:T(8,128)(2,1)} custom-call(bf16[256,2304]{1,0:T(8,128)(2,1)S(1)} %bitcast.13, bf16[96,2304]{1,0:T(8,128)(2,1)S(1)} %bitcast.16), custom_call_target="tpu_custom_call" | custom-call | tf_op jit(solution)/shard_map/pallas_call | solution.py:83
  60.5 6.6 %all-to-all-start.2 = ((bf16[8,32,192]{2,1,0:T(8,128)(2,1)}), bf16[8,32,192]{2,1,0:T(8,128)(2,1)S(1)}, u32[]{:S(2)}, u32[]{:S(2)}) async-start(bf16[8,32,192]{2,1,0:T(8,128)(2,1)} %shard_map.86), calls=%async_computation.2 | async-start | bytes 262144 | tf_op jit(solution)/shard_map/all_to_all | solution.py:44
  67.1 2.0 %collective-permute-start.5 = (bf16[2,256,256]{2,1,0:T(8,128)(2,1)S(1)}, bf16[2,256,256]{2,1,0:T(8,128)(2,1)S(1)}, u32[]{:S(2)}, u32[]{:S(2)}) collective-permute-start(bf16[2,256,256]{2,1,0:T(8,128)(2,1)S(1)} %collective-permute-done.2.refs_8_), channel_id=1, source_target_pairs={{0,128},{128,0},{1,129},{129,1},{2,130},{130,2},{3,131},{131,3},{4... | collective-permute-start | bytes 786440 | tf_op jit(solution)/shard_map/ppermute | solution.py:60
  69.2 0.0 collective-permute-done.3.refs_9_
  69.2 0.0 collective-permute-done.4.refs_6_
  69.2 2.5 %all-to-all-done.2 = bf16[8,32,192]{2,1,0:T(8,128)(2,1)S(1)} async-done(((bf16[8,32,192]{2,1,0:T(8,128)(2,1)}), bf16[8,32,192]{2,1,0:T(8,128)(2,1)S(1)}, u32[]{:S(2)}, u32[]{:S(2)}) %all-to-all-start.2) | async-done | bytes 98336 | tf_op jit(solution)/shard_map/all_to_all | solution.py:44
  71.7 0.1 fusion.1
  71.8 0.6 copy.12
  72.4 11.9 %all-to-all-start.3 = ((bf16[32,2,96]{2,1,0:T(2,128)(2,1)}), bf16[32,2,96]{2,1,0:T(2,128)(2,1)S(1)}, u32[]{:S(2)}, u32[]{:S(2)}) async-start(bf16[32,2,96]{2,1,0:T(2,128)(2,1)} %copy.12), calls=%async_computation.3 | async-start | bytes 32768 | tf_op jit(solution)/shard_map/all_to_all | solution.py:44
  84.3 0.0 copy-start
  84.3 1.7 %copy-done = bf16[2304,2,288]{0,2,1:T(8,128)(2,1)S(1)} copy-done((bf16[2304,2,288]{0,2,1:T(8,128)(2,1)S(1)}, bf16[2304,2,288]{0,2,1:T(8,128)(2,1)}, u32[]{:S(2)}) %copy-start) | copy-done | bytes 2654232
  86.0 0.0 copy-start.2
  86.1 0.0 copy-start.5
  86.1 1.9 %shard_map.87 = bf16[8,32,576]{2,1,0:T(8,128)(2,1)} custom-call(bf16[256,2304]{1,0:T(8,128)(2,1)S(1)} %bitcast.14, bf16[576,2304]{1,0:T(8,128)(2,1)S(1)} %bitcast.15), custom_call_target="tpu_custom_call" | custom-call | tf_op jit(solution)/shard_map/pallas_call | solution.py:83
  87.9 3.4 %all-to-all-done.3 = bf16[32,2,96]{2,1,0:T(2,128)(2,1)S(1)} async-done(((bf16[32,2,96]{2,1,0:T(2,128)(2,1)}), bf16[32,2,96]{2,1,0:T(2,128)(2,1)S(1)}, u32[]{:S(2)}, u32[]{:S(2)}) %all-to-all-start.3) | async-done | bytes 12320 | tf_op jit(solution)/shard_map/all_to_all | solution.py:44
  91.3 0.0 collective-permute-done.5.refs_10_
  91.3 10.4 %all-to-all-start.4 = ((bf16[8,32,576]{2,1,0:T(8,128)(2,1)}), bf16[8,32,576]{2,1,0:T(8,128)(2,1)S(1)}, u32[]{:S(2)}, u32[]{:S(2)}) async-start(bf16[8,32,576]{2,1,0:T(8,128)(2,1)} %shard_map.87), calls=%async_computation.4 | async-start | bytes 655360 | tf_op jit(solution)/shard_map/all_to_all | solution.py:44
  101.8 0.0 copy-start.4
  101.8 0.1 reshape.41
  101.9 2.6 %collective-permute-start.6 = (bf16[2,8,256]{2,1,0:T(8,128)(2,1)S(1)}, bf16[2,8,256]{2,1,0:T(8,128)(2,1)S(1)}, u32[]{:S(2)}, u32[]{:S(2)}) collective-permute-start(bf16[2,8,256]{2,1,0:T(8,128)(2,1)S(1)} %pad.4), channel_id=1, source_target_pairs={{0,512},{256,768},{512,0},{768,256},{1,513},{257,769},{513,1},{769... | collective-permute-start | bytes 24584 | tf_op jit(solution)/shard_map/ppermute | solution.py:56
  104.5 6.2 %collective-permute-done.6 = bf16[2,8,256]{2,1,0:T(8,128)(2,1)S(1)} collective-permute-done((bf16[2,8,256]{2,1,0:T(8,128)(2,1)S(1)}, bf16[2,8,256]{2,1,0:T(8,128)(2,1)S(1)}, u32[]{:S(2)}, u32[]{:S(2)}) %collective-permute-start.6) | collective-permute-done | bytes 8224 | tf_op jit(solution)/shard_map/ppermute | solution.py:56
  110.7 0.0 copy-done.2
  110.7 0.0 copy-done.5
  110.7 1.5 %shard_map.88 = (f32[2,8,384]{2,1,0:T(8,128)S(1)}, f32[2,8,384]{2,1,0:T(8,128)S(1)}) custom-call(s32[1]{0:T(128)} %bitcast.8.refs_0_, s32[2]{0:T(128)S(1)} %copy-done.5, bf16[2,16,256]{2,1,0:T(8,128)(2,1)S(1)} %pad_maximum_fusion.1.refs_2_, bf16[2,256,256]{2,1,0:T(8,128)(2,1)S(1)} %copy-done.2, bf16[2,256,256]{2,1,0:T(8,128)(2,1)S(1)} %collective-permute-done.refs_4_, ...), custom_call_target="tpu_custom_call" | custom-call | tf_op jit(solution)/shard_map/pallas_call | solution.py:129
  112.2 2.6 %collective-permute-start.7 = (f32[2,8,384]{2,1,0:T(8,128)S(1)}, f32[2,8,384]{2,1,0:T(8,128)S(1)}, u32[]{:S(2)}, u32[]{:S(2)}) collective-permute-start(f32[2,8,384]{2,1,0:T(8,128)S(1)} %get-tuple-element.27), channel_id=1, source_target_pairs={{0,512},{256,768},{512,0},{768,256},{1,513},{257,769},{513,1},{769... | collective-permute-start | bytes 73736 | tf_op jit(solution)/shard_map/ppermute | solution.py:56
  114.9 4.0 %collective-permute-done.7.refs_1_ = f32[2,8,384]{2,1,0:T(8,128)S(1)} collective-permute-done((f32[2,8,384]{2,1,0:T(8,128)S(1)}, f32[2,8,384]{2,1,0:T(8,128)S(1)}, u32[]{:S(2)}, u32[]{:S(2)}) %collective-permute-start.7) | collective-permute-done | bytes 24608 | tf_op jit(solution)/shard_map/ppermute | solution.py:56
  118.9 0.0 copy-done.4
  118.9 0.9 shard_map.89
  119.7 0.0 all-to-all-done.4
  119.7 0.1 convert_reduce_fusion
  119.8 0.1 fusion
  119.9 0.6 reshape.39
  (9 shorter events, 0.1 us)
Async XLA Ops:
  2.2 41.7 %all-to-all-start = ((bf16[32,2,2304]{2,1,0:T(2,128)(2,1)}), bf16[32,2,2304]{2,1,0:T(2,128)(2,1)S(1)}, u32[]{:S(2)}, u32[]{:S(2)}) async-start(bf16[32,2,2304]{2,1,0:T(2,128)(2,1)} %broadcast_in_dim.4), calls=%async_computation | async-start | bytes 589824 | tf_op jit(solution)/shard_map/all_to_all | solution.py:44
  29.2 14.8 %collective-permute-start = (bf16[2,256,256]{2,1,0:T(8,128)(2,1)}, bf16[2,256,256]{2,1,0:T(8,128)(2,1)S(1)}, u32[]{:S(2)}, u32[]{:S(2)}) collective-permute-start(bf16[2,256,256]{2,1,0:T(8,128)(2,1)} %refs_3_.2), channel_id=1, source_target_pairs={{0,256},{256,0},{512,768},{768,512},{1,257},{257,1},{513,769},{769... | collective-permute-start | bytes 786440 | tf_op jit(solution)/shard_map/ppermute | solution.py:52
  32.6 11.5 %collective-permute-start.1 = (bf16[2,256,256]{2,1,0:T(8,128)(2,1)}, bf16[2,256,256]{2,1,0:T(8,128)(2,1)S(1)}, u32[]{:S(2)}, u32[]{:S(2)}) collective-permute-start(bf16[2,256,256]{2,1,0:T(8,128)(2,1)} %refs_3_.2), channel_id=1, source_target_pairs={{0,128},{128,0},{1,129},{129,1},{2,130},{130,2},{3,131},{131,3},{4... | collective-permute-start | bytes 786440 | tf_op jit(solution)/shard_map/ppermute | solution.py:60
  45.2 3.8 %copy-start.3 = (bf16[2,256,256]{2,1,0:T(8,128)(2,1)S(1)}, bf16[2,256,256]{2,1,0:T(8,128)(2,1)}, u32[]{:S(2)}) copy-start(bf16[2,256,256]{2,1,0:T(8,128)(2,1)} %refs_7_.1) | copy-start | bytes 786436
  45.2 14.1 %copy-start.1 = (bf16[2304,96]{0,1:T(8,128)(2,1)S(1)}, bf16[2304,96]{0,1:T(8,128)(2,1)}, u32[]{:S(2)}) copy-start(bf16[2304,96]{0,1:T(8,128)(2,1)} %param.8) | copy-start | bytes 1327108
  45.2 14.1 %all-to-all-start.1 = ((bf16[4,64,2304]{2,1,0:T(8,128)(2,1)}), bf16[4,64,2304]{2,1,0:T(8,128)(2,1)S(1)}, u32[]{:S(2)}, u32[]{:S(2)}) async-start(bf16[4,64,2304]{2,1,0:T(8,128)(2,1)} %broadcast_in_dim.5), calls=%async_computation.1 | async-start | bytes 2359296 | tf_op jit(solution)/shard_map/all_to_all | solution.py:44
  49.0 10.2 %collective-permute-start.2 = (bf16[2,256,256]{2,1,0:T(8,128)(2,1)S(1)}, bf16[2,256,256]{2,1,0:T(8,128)(2,1)S(1)}, u32[]{:S(2)}, u32[]{:S(2)}) collective-permute-start(bf16[2,256,256]{2,1,0:T(8,128)(2,1)S(1)} %copy-done.3), channel_id=1, source_target_pairs={{0,256},{256,0},{512,768},{768,512},{1,257},{257,1},{513,769},{769... | collective-permute-start | bytes 786440 | tf_op jit(solution)/shard_map/ppermute | solution.py:52
  52.9 16.3 %collective-permute-start.3 = (bf16[2,256,256]{2,1,0:T(8,128)(2,1)S(1)}, bf16[2,256,256]{2,1,0:T(8,128)(2,1)S(1)}, u32[]{:S(2)}, u32[]{:S(2)}) collective-permute-start(bf16[2,256,256]{2,1,0:T(8,128)(2,1)S(1)} %copy-done.3), channel_id=1, source_target_pairs={{0,128},{128,0},{1,129},{129,1},{2,130},{130,2},{3,131},{131,3},{4... | collective-permute-start | bytes 786440 | tf_op jit(solution)/shard_map/ppermute | solution.py:60
  56.0 13.2 %collective-permute-start.4 = (bf16[2,256,256]{2,1,0:T(8,128)(2,1)S(1)}, bf16[2,256,256]{2,1,0:T(8,128)(2,1)S(1)}, u32[]{:S(2)}, u32[]{:S(2)}) collective-permute-start(bf16[2,256,256]{2,1,0:T(8,128)(2,1)S(1)} %collective-permute-done.refs_4_), channel_id=1, source_target_pairs={{0,128},{128,0},{1,129},{129,1},{2,130},{130,2},{3,131},{131,3},{4... | collective-permute-start | bytes 786440 | tf_op jit(solution)/shard_map/ppermute | solution.py:60
  60.5 11.2 %all-to-all-start.2 = ((bf16[8,32,192]{2,1,0:T(8,128)(2,1)}), bf16[8,32,192]{2,1,0:T(8,128)(2,1)S(1)}, u32[]{:S(2)}, u32[]{:S(2)}) async-start(bf16[8,32,192]{2,1,0:T(8,128)(2,1)} %shard_map.86), calls=%async_computation.2 | async-start | bytes 262144 | tf_op jit(solution)/shard_map/all_to_all | solution.py:44
  67.1 24.2 %collective-permute-start.5 = (bf16[2,256,256]{2,1,0:T(8,128)(2,1)S(1)}, bf16[2,256,256]{2,1,0:T(8,128)(2,1)S(1)}, u32[]{:S(2)}, u32[]{:S(2)}) collective-permute-start(bf16[2,256,256]{2,1,0:T(8,128)(2,1)S(1)} %collective-permute-done.2.refs_8_), channel_id=1, source_target_pairs={{0,128},{128,0},{1,129},{129,1},{2,130},{130,2},{3,131},{131,3},{4... | collective-permute-start | bytes 786440 | tf_op jit(solution)/shard_map/ppermute | solution.py:60
  72.4 18.9 %all-to-all-start.3 = ((bf16[32,2,96]{2,1,0:T(2,128)(2,1)}), bf16[32,2,96]{2,1,0:T(2,128)(2,1)S(1)}, u32[]{:S(2)}, u32[]{:S(2)}) async-start(bf16[32,2,96]{2,1,0:T(2,128)(2,1)} %copy.12), calls=%async_computation.3 | async-start | bytes 32768 | tf_op jit(solution)/shard_map/all_to_all | solution.py:44
  84.3 1.8 %copy-start = (bf16[2304,2,288]{0,2,1:T(8,128)(2,1)S(1)}, bf16[2304,2,288]{0,2,1:T(8,128)(2,1)}, u32[]{:S(2)}) copy-start(bf16[2304,2,288]{0,2,1:T(8,128)(2,1)} %param.9) | copy-start | bytes 7962628
  86.0 24.6 %copy-start.2 = (bf16[2,256,256]{2,1,0:T(8,128)(2,1)S(1)}, bf16[2,256,256]{2,1,0:T(8,128)(2,1)}, u32[]{:S(2)}) copy-start(bf16[2,256,256]{2,1,0:T(8,128)(2,1)} %refs_3_.2) | copy-start | bytes 786436
  86.1 24.6 %copy-start.5 = (s32[2]{0:T(128)S(1)}, s32[2]{0:T(128)}, u32[]{:S(2)}) copy-start(s32[2]{0:T(128)} %refs_1_.1) | copy-start | bytes 28
  91.3 28.4 %all-to-all-start.4 = ((bf16[8,32,576]{2,1,0:T(8,128)(2,1)}), bf16[8,32,576]{2,1,0:T(8,128)(2,1)S(1)}, u32[]{:S(2)}, u32[]{:S(2)}) async-start(bf16[8,32,576]{2,1,0:T(8,128)(2,1)} %shard_map.87), calls=%async_computation.4 | async-start | bytes 655360 | tf_op jit(solution)/shard_map/all_to_all | solution.py:44
  101.8 17.1 %copy-start.4 = (bf16[2,2,256]{2,1,0:T(2,128)(2,1)S(1)}, bf16[2,2,256]{2,1,0:T(2,128)(2,1)}, u32[]{:S(2)}) copy-start(bf16[2,2,256]{2,1,0:T(2,128)(2,1)} %refs_3_.3) | copy-start | bytes 6148
  101.9 8.8 %collective-permute-start.6 = (bf16[2,8,256]{2,1,0:T(8,128)(2,1)S(1)}, bf16[2,8,256]{2,1,0:T(8,128)(2,1)S(1)}, u32[]{:S(2)}, u32[]{:S(2)}) collective-permute-start(bf16[2,8,256]{2,1,0:T(8,128)(2,1)S(1)} %pad.4), channel_id=1, source_target_pairs={{0,512},{256,768},{512,0},{768,256},{1,513},{257,769},{513,1},{769... | collective-permute-start | bytes 24584 | tf_op jit(solution)/shard_map/ppermute | solution.py:56
  112.2 6.6 %collective-permute-start.7 = (f32[2,8,384]{2,1,0:T(8,128)S(1)}, f32[2,8,384]{2,1,0:T(8,128)S(1)}, u32[]{:S(2)}, u32[]{:S(2)}) collective-permute-start(f32[2,8,384]{2,1,0:T(8,128)S(1)} %get-tuple-element.27), channel_id=1, source_target_pairs={{0,512},{256,768},{512,0},{768,256},{1,513},{257,769},{513,1},{769... | collective-permute-start | bytes 73736 | tf_op jit(solution)/shard_map/ppermute | solution.py:56

commit v8 on v7

--- a/solution.py
+++ b/solution.py
@@ -196,7 +196,8 @@
     per_dev = 16 * qw // head_dim
     query = query.transpose(1, 0, 2).reshape(seqs, per_dev, head_dim)
     query = jnp.pad(query, ((0, 0), (0, 8 - per_dev), (0, 0)))
-    queries = jnp.concatenate([query, across(query)], axis=1)
+    gate_up, other = lax.optimization_barrier((gate_up, across(query)))
+    queries = jnp.concatenate([query, other], axis=1)
 
     keys = (key_cache, keys_b, keys_c, keys_d)
     values = (value_cache, values_b, values_c, values_d)

time: 121 us -> 121 us (level)
  waiting for transfers between devices: 26.8 us -> 23.7 us
  starting transfers between devices: 81.2 us -> 83.4 us
    ppermute x2, starting transfers between devices: 5.26 us -> 12.2 us  [across(): return lax.ppermute(x, 'xl', [(i, i ^ 2) for i in range(4)])]
    all_to_all x5, starting transfers between devices: 59.7 us -> 54.9 us  [exchange(): return lax.all_to_all(x, axis, 0, 0, axis_index_groups=groups, tiled=True)]
    ppermute x2, waiting for transfers between devices: 10.2 us -> 7.11 us  [across(): return lax.ppermute(x, 'xl', [(i, i ^ 2) for i in range(4)])]
where the time goes in v8:
time: 121 us; the launch traced here: 120 us
  starting transfers between devices  83.4 us (69%)
  waiting for transfers between devices  23.7 us (20%)
  local copies, waits for them, and re-layouts  5.99 us (5%)
  Pallas kernels  5.48 us (5%)
    all_to_all x5, starting transfers between devices, exchange(): return lax.all_to_all(x, axis, 0, 0, axis_index_groups=groups, tiled=True)  54.9 us
    all_to_all x5, waiting for transfers between devices, exchange(): return lax.all_to_all(x, axis, 0, 0, axis_index_groups=groups, tiled=True)  15.3 us
    ppermute x2, starting transfers between devices, across(): return lax.ppermute(x, 'xl', [(i, i ^ 2) for i in range(4)])  12.2 us
    ppermute x4, starting transfers between devices, other_core(): return lax.ppermute(x, 'core', [(0, 1), (1, 0)])  9.01 us
    ppermute x2, starting transfers between devices, beside(): return lax.ppermute(x, 'xl', [(i, i ^ 1) for i in range(4)])  7.24 us
    ppermute x2, waiting for transfers between devices, across(): return lax.ppermute(x, 'xl', [(i, i ^ 2) for i in range(4)])  7.11 us
    pallas_call x2, Pallas kernels, project(): pl.pallas_call(kernel, out_shape=jax.ShapeDtypeStruct(shape, jnp.bfloat16...  3.09 us
    broadcast_in_dim x2, local copies, waits for them, and re-layouts, spread(): return exchange(jnp.broadcast_to(x[None], (n,) + x.shape), axis, groups)  2.69 us
  transfers between devices with their start and end apart: 13, of which 7 were waited for; matrix products, arithmetic and copies ran while one was open for 1% of the time, Pallas kernels for 5%

profile of v8, /device:TPU:14, one launch (start us, length us, event | category | flops | bytes accessed | tf_op | source)
XLA Modules:
  0.0 119.6 jit_solution(13472001749995749073)
XLA Ops:
  0.6 1.6 %broadcast_in_dim.4 = bf16[32,2,2304]{2,1,0:T(2,128)(2,1)} broadcast(bf16[2,2304]{1,0:T(2,128)(2,1)} %param.7), dimensions={1,2} | broadcast | bytes 304128 | tf_op jit(solution)/shard_map/broadcast_in_dim | solution.py:48
  2.2 27.0 %all-to-all-start = ((bf16[32,2,2304]{2,1,0:T(2,128)(2,1)}), bf16[32,2,2304]{2,1,0:T(2,128)(2,1)S(1)}, u32[]{:S(2)}, u32[]{:S(2)}) async-start(bf16[32,2,2304]{2,1,0:T(2,128)(2,1)} %broadcast_in_dim.4), calls=%async_computation | async-start | bytes 589824 | tf_op jit(solution)/shard_map/all_to_all | solution.py:44
  29.2 3.3 %collective-permute-start = (bf16[2,256,256]{2,1,0:T(8,128)(2,1)}, bf16[2,256,256]{2,1,0:T(8,128)(2,1)S(1)}, u32[]{:S(2)}, u32[]{:S(2)}) collective-permute-start(bf16[2,256,256]{2,1,0:T(8,128)(2,1)} %refs_3_.2), channel_id=1, source_target_pairs={{0,256},{256,0},{512,768},{768,512},{1,257},{257,1},{513,769},{769... | collective-permute-start | bytes 786440 | tf_op jit(solution)/shard_map/ppermute | solution.py:52
  32.6 1.9 %collective-permute-start.1 = (bf16[2,256,256]{2,1,0:T(8,128)(2,1)}, bf16[2,256,256]{2,1,0:T(8,128)(2,1)S(1)}, u32[]{:S(2)}, u32[]{:S(2)}) collective-permute-start(bf16[2,256,256]{2,1,0:T(8,128)(2,1)} %refs_3_.2), channel_id=1, source_target_pairs={{0,128},{128,0},{1,129},{129,1},{2,130},{130,2},{3,131},{131,3},{4... | collective-permute-start | bytes 786440 | tf_op jit(solution)/shard_map/ppermute | solution.py:60
  34.5 9.4 %all-to-all-done = bf16[32,2,2304]{2,1,0:T(2,128)(2,1)S(1)} async-done(((bf16[32,2,2304]{2,1,0:T(2,128)(2,1)}), bf16[32,2,2304]{2,1,0:T(2,128)(2,1)S(1)}, u32[]{:S(2)}, u32[]{:S(2)}) %all-to-all-start) | async-done | bytes 294944 | tf_op jit(solution)/shard_map/all_to_all | solution.py:44
  43.9 0.1 reshape.33
  44.0 0.0 collective-permute-done.refs_4_
  44.0 0.0 collective-permute-done.1.refs_5_
  44.1 1.1 broadcast_in_dim.5
  45.2 0.0 copy-start.3
  45.2 0.0 copy-start.1
  45.2 3.8 %all-to-all-start.1 = ((bf16[4,64,2304]{2,1,0:T(8,128)(2,1)}), bf16[4,64,2304]{2,1,0:T(8,128)(2,1)S(1)}, u32[]{:S(2)}, u32[]{:S(2)}) async-start(bf16[4,64,2304]{2,1,0:T(8,128)(2,1)} %broadcast_in_dim.5), calls=%async_computation.1 | async-start | bytes 2359296 | tf_op jit(solution)/shard_map/all_to_all | solution.py:44
  49.0 0.0 copy-done.3
  49.0 3.9 %collective-permute-start.2 = (bf16[2,256,256]{2,1,0:T(8,128)(2,1)S(1)}, bf16[2,256,256]{2,1,0:T(8,128)(2,1)S(1)}, u32[]{:S(2)}, u32[]{:S(2)}) collective-permute-start(bf16[2,256,256]{2,1,0:T(8,128)(2,1)S(1)} %copy-done.3), channel_id=1, source_target_pairs={{0,256},{256,0},{512,768},{768,512},{1,257},{257,1},{513,769},{769... | collective-permute-start | bytes 786440 | tf_op jit(solution)/shard_map/ppermute | solution.py:52
  52.9 3.1 %collective-permute-start.3 = (bf16[2,256,256]{2,1,0:T(8,128)(2,1)S(1)}, bf16[2,256,256]{2,1,0:T(8,128)(2,1)S(1)}, u32[]{:S(2)}, u32[]{:S(2)}) collective-permute-start(bf16[2,256,256]{2,1,0:T(8,128)(2,1)S(1)} %copy-done.3), channel_id=1, source_target_pairs={{0,128},{128,0},{1,129},{129,1},{2,130},{130,2},{3,131},{131,3},{4... | collective-permute-start | bytes 786440 | tf_op jit(solution)/shard_map/ppermute | solution.py:60
  56.0 1.9 %collective-permute-start.4 = (bf16[2,256,256]{2,1,0:T(8,128)(2,1)S(1)}, bf16[2,256,256]{2,1,0:T(8,128)(2,1)S(1)}, u32[]{:S(2)}, u32[]{:S(2)}) collective-permute-start(bf16[2,256,256]{2,1,0:T(8,128)(2,1)S(1)} %collective-permute-done.refs_4_), channel_id=1, source_target_pairs={{0,128},{128,0},{1,129},{129,1},{2,130},{130,2},{3,131},{131,3},{4... | collective-permute-start | bytes 786440 | tf_op jit(solution)/shard_map/ppermute | solution.py:60
  57.9 1.3 %collective-permute-done.2.refs_8_ = bf16[2,256,256]{2,1,0:T(8,128)(2,1)S(1)} collective-permute-done((bf16[2,256,256]{2,1,0:T(8,128)(2,1)S(1)}, bf16[2,256,256]{2,1,0:T(8,128)(2,1)S(1)}, u32[]{:S(2)}, u32[]{:S(2)}) %collective-permute-start.2) | collective-permute-done | bytes 262176 | tf_op jit(solution)/shard_map/ppermute | solution.py:52
  59.2 0.1 all-to-all-done.1
  59.3 0.0 copy-done.1
  59.3 1.2 %shard_map.86 = bf16[8,32,192]{2,1,0:T(8,128)(2,1)} custom-call(bf16[256,2304]{1,0:T(8,128)(2,1)S(1)} %bitcast.13, bf16[96,2304]{1,0:T(8,128)(2,1)S(1)} %bitcast.16), custom_call_target="tpu_custom_call" | custom-call | tf_op jit(solution)/shard_map/pallas_call | solution.py:83
  60.5 6.6 %all-to-all-start.2 = ((bf16[8,32,192]{2,1,0:T(8,128)(2,1)}), bf16[8,32,192]{2,1,0:T(8,128)(2,1)S(1)}, u32[]{:S(2)}, u32[]{:S(2)}) async-start(bf16[8,32,192]{2,1,0:T(8,128)(2,1)} %shard_map.86), calls=%async_computation.2 | async-start | bytes 262144 | tf_op jit(solution)/shard_map/all_to_all | solution.py:44
  67.1 2.0 %collective-permute-start.5 = (bf16[2,256,256]{2,1,0:T(8,128)(2,1)S(1)}, bf16[2,256,256]{2,1,0:T(8,128)(2,1)S(1)}, u32[]{:S(2)}, u32[]{:S(2)}) collective-permute-start(bf16[2,256,256]{2,1,0:T(8,128)(2,1)S(1)} %collective-permute-done.2.refs_8_), channel_id=1, source_target_pairs={{0,128},{128,0},{1,129},{129,1},{2,130},{130,2},{3,131},{131,3},{4... | collective-permute-start | bytes 786440 | tf_op jit(solution)/shard_map/ppermute | solution.py:60
  69.2 0.0 collective-permute-done.3.refs_9_
  69.2 0.0 collective-permute-done.4.refs_6_
  69.2 2.5 %all-to-all-done.2 = bf16[8,32,192]{2,1,0:T(8,128)(2,1)S(1)} async-done(((bf16[8,32,192]{2,1,0:T(8,128)(2,1)}), bf16[8,32,192]{2,1,0:T(8,128)(2,1)S(1)}, u32[]{:S(2)}, u32[]{:S(2)}) %all-to-all-start.2) | async-done | bytes 98336 | tf_op jit(solution)/shard_map/all_to_all | solution.py:44
  71.7 0.1 fusion.1
  71.8 0.6 copy.12
  72.4 11.9 %all-to-all-start.3 = ((bf16[32,2,96]{2,1,0:T(2,128)(2,1)}), bf16[32,2,96]{2,1,0:T(2,128)(2,1)S(1)}, u32[]{:S(2)}, u32[]{:S(2)}) async-start(bf16[32,2,96]{2,1,0:T(2,128)(2,1)} %copy.12), calls=%async_computation.3 | async-start | bytes 32768 | tf_op jit(solution)/shard_map/all_to_all | solution.py:44
  84.3 0.0 copy-start
  84.3 1.7 %copy-done = bf16[2304,2,288]{0,2,1:T(8,128)(2,1)S(1)} copy-done((bf16[2304,2,288]{0,2,1:T(8,128)(2,1)S(1)}, bf16[2304,2,288]{0,2,1:T(8,128)(2,1)}, u32[]{:S(2)}) %copy-start) | copy-done | bytes 2654232
  86.1 0.0 copy-start.2
  86.1 0.0 copy-start.5
  86.1 1.9 %shard_map.87 = bf16[8,32,576]{2,1,0:T(8,128)(2,1)} custom-call(bf16[256,2304]{1,0:T(8,128)(2,1)S(1)} %bitcast.14, bf16[576,2304]{1,0:T(8,128)(2,1)S(1)} %bitcast.15), custom_call_target="tpu_custom_call" | custom-call | tf_op jit(solution)/shard_map/pallas_call | solution.py:83
  88.0 3.3 %all-to-all-done.3 = bf16[32,2,96]{2,1,0:T(2,128)(2,1)S(1)} async-done(((bf16[32,2,96]{2,1,0:T(2,128)(2,1)}), bf16[32,2,96]{2,1,0:T(2,128)(2,1)S(1)}, u32[]{:S(2)}, u32[]{:S(2)}) %all-to-all-start.3) | async-done | bytes 12320 | tf_op jit(solution)/shard_map/all_to_all | solution.py:44
  91.3 0.0 collective-permute-done.5.refs_10_
  91.3 0.1 reshape.38
  91.4 9.6 %collective-permute-start.6 = (bf16[2,8,256]{2,1,0:T(8,128)(2,1)S(1)}, bf16[2,8,256]{2,1,0:T(8,128)(2,1)S(1)}, u32[]{:S(2)}, u32[]{:S(2)}) collective-permute-start(bf16[2,8,256]{2,1,0:T(8,128)(2,1)S(1)} %pad.4), channel_id=1, source_target_pairs={{0,512},{256,768},{512,0},{768,256},{1,513},{257,769},{513,1},{769... | collective-permute-start | bytes 24584 | tf_op jit(solution)/shard_map/ppermute | solution.py:56
  101.1 1.6 %collective-permute-done.6 = bf16[2,8,256]{2,1,0:T(8,128)(2,1)S(1)} collective-permute-done((bf16[2,8,256]{2,1,0:T(8,128)(2,1)S(1)}, bf16[2,8,256]{2,1,0:T(8,128)(2,1)S(1)}, u32[]{:S(2)}, u32[]{:S(2)}) %collective-permute-start.6) | collective-permute-done | bytes 8224 | tf_op jit(solution)/shard_map/ppermute | solution.py:56
  102.7 5.7 %all-to-all-start.4 = ((bf16[8,32,576]{2,1,0:T(8,128)(2,1)}), bf16[8,32,576]{2,1,0:T(8,128)(2,1)S(1)}, u32[]{:S(2)}, u32[]{:S(2)}) async-start(bf16[8,32,576]{2,1,0:T(8,128)(2,1)} %shard_map.87), calls=%async_computation.4 | async-start | bytes 655360 | tf_op jit(solution)/shard_map/all_to_all | solution.py:44
  108.3 0.0 copy-start.4
  108.3 0.0 copy-done.2
  108.3 0.0 copy-done.5
  108.3 1.5 %shard_map.88 = (f32[2,8,384]{2,1,0:T(8,128)S(1)}, f32[2,8,384]{2,1,0:T(8,128)S(1)}) custom-call(s32[1]{0:T(128)} %bitcast.9.refs_0_, s32[2]{0:T(128)S(1)} %copy-done.5, bf16[2,16,256]{2,1,0:T(8,128)(2,1)S(1)} %pad_maximum_fusion.1.refs_2_, bf16[2,256,256]{2,1,0:T(8,128)(2,1)S(1)} %copy-done.2, bf16[2,256,256]{2,1,0:T(8,128)(2,1)S(1)} %collective-permute-done.refs_4_, ...), custom_call_target="tpu_custom_call" | custom-call | tf_op jit(solution)/shard_map/pallas_call | solution.py:129
  109.9 2.6 %collective-permute-start.7 = (f32[2,8,384]{2,1,0:T(8,128)S(1)}, f32[2,8,384]{2,1,0:T(8,128)S(1)}, u32[]{:S(2)}, u32[]{:S(2)}) collective-permute-start(f32[2,8,384]{2,1,0:T(8,128)S(1)} %get-tuple-element.31), channel_id=1, source_target_pairs={{0,512},{256,768},{512,0},{768,256},{1,513},{257,769},{513,1},{769... | collective-permute-start | bytes 73736 | tf_op jit(solution)/shard_map/ppermute | solution.py:56
  112.5 5.5 %collective-permute-done.7.refs_1_ = f32[2,8,384]{2,1,0:T(8,128)S(1)} collective-permute-done((f32[2,8,384]{2,1,0:T(8,128)S(1)}, f32[2,8,384]{2,1,0:T(8,128)S(1)}, u32[]{:S(2)}, u32[]{:S(2)}) %collective-permute-start.7) | collective-permute-done | bytes 24608 | tf_op jit(solution)/shard_map/ppermute | solution.py:56
  118.0 0.0 copy-done.4
  118.0 0.9 shard_map.89
  118.8 0.0 all-to-all-done.4
  118.8 0.1 convert_reduce_fusion
  118.9 0.1 fusion
  119.0 0.6 reshape.40
  (9 shorter events, 0.1 us)
Async XLA Ops:
  2.2 41.7 %all-to-all-start = ((bf16[32,2,2304]{2,1,0:T(2,128)(2,1)}), bf16[32,2,2304]{2,1,0:T(2,128)(2,1)S(1)}, u32[]{:S(2)}, u32[]{:S(2)}) async-start(bf16[32,2,2304]{2,1,0:T(2,128)(2,1)} %broadcast_in_dim.4), calls=%async_computation | async-start | bytes 589824 | tf_op jit(solution)/shard_map/all_to_all | solution.py:44
  29.2 14.8 %collective-permute-start = (bf16[2,256,256]{2,1,0:T(8,128)(2,1)}, bf16[2,256,256]{2,1,0:T(8,128)(2,1)S(1)}, u32[]{:S(2)}, u32[]{:S(2)}) collective-permute-start(bf16[2,256,256]{2,1,0:T(8,128)(2,1)} %refs_3_.2), channel_id=1, source_target_pairs={{0,256},{256,0},{512,768},{768,512},{1,257},{257,1},{513,769},{769... | collective-permute-start | bytes 786440 | tf_op jit(solution)/shard_map/ppermute | solution.py:52
  32.6 11.5 %collective-permute-start.1 = (bf16[2,256,256]{2,1,0:T(8,128)(2,1)}, bf16[2,256,256]{2,1,0:T(8,128)(2,1)S(1)}, u32[]{:S(2)}, u32[]{:S(2)}) collective-permute-start(bf16[2,256,256]{2,1,0:T(8,128)(2,1)} %refs_3_.2), channel_id=1, source_target_pairs={{0,128},{128,0},{1,129},{129,1},{2,130},{130,2},{3,131},{131,3},{4... | collective-permute-start | bytes 786440 | tf_op jit(solution)/shard_map/ppermute | solution.py:60
  45.2 3.8 %copy-start.3 = (bf16[2,256,256]{2,1,0:T(8,128)(2,1)S(1)}, bf16[2,256,256]{2,1,0:T(8,128)(2,1)}, u32[]{:S(2)}) copy-start(bf16[2,256,256]{2,1,0:T(8,128)(2,1)} %refs_7_.1) | copy-start | bytes 786436
  45.2 14.1 %copy-start.1 = (bf16[2304,96]{0,1:T(8,128)(2,1)S(1)}, bf16[2304,96]{0,1:T(8,128)(2,1)}, u32[]{:S(2)}) copy-start(bf16[2304,96]{0,1:T(8,128)(2,1)} %param.8) | copy-start | bytes 1327108
  45.2 14.1 %all-to-all-start.1 = ((bf16[4,64,2304]{2,1,0:T(8,128)(2,1)}), bf16[4,64,2304]{2,1,0:T(8,128)(2,1)S(1)}, u32[]{:S(2)}, u32[]{:S(2)}) async-start(bf16[4,64,2304]{2,1,0:T(8,128)(2,1)} %broadcast_in_dim.5), calls=%async_computation.1 | async-start | bytes 2359296 | tf_op jit(solution)/shard_map/all_to_all | solution.py:44
  49.0 10.2 %collective-permute-start.2 = (bf16[2,256,256]{2,1,0:T(8,128)(2,1)S(1)}, bf16[2,256,256]{2,1,0:T(8,128)(2,1)S(1)}, u32[]{:S(2)}, u32[]{:S(2)}) collective-permute-start(bf16[2,256,256]{2,1,0:T(8,128)(2,1)S(1)} %copy-done.3), channel_id=1, source_target_pairs={{0,256},{256,0},{512,768},{768,512},{1,257},{257,1},{513,769},{769... | collective-permute-start | bytes 786440 | tf_op jit(solution)/shard_map/ppermute | solution.py:52
  52.9 16.3 %collective-permute-start.3 = (bf16[2,256,256]{2,1,0:T(8,128)(2,1)S(1)}, bf16[2,256,256]{2,1,0:T(8,128)(2,1)S(1)}, u32[]{:S(2)}, u32[]{:S(2)}) collective-permute-start(bf16[2,256,256]{2,1,0:T(8,128)(2,1)S(1)} %copy-done.3), channel_id=1, source_target_pairs={{0,128},{128,0},{1,129},{129,1},{2,130},{130,2},{3,131},{131,3},{4... | collective-permute-start | bytes 786440 | tf_op jit(solution)/shard_map/ppermute | solution.py:60
  56.0 13.2 %collective-permute-start.4 = (bf16[2,256,256]{2,1,0:T(8,128)(2,1)S(1)}, bf16[2,256,256]{2,1,0:T(8,128)(2,1)S(1)}, u32[]{:S(2)}, u32[]{:S(2)}) collective-permute-start(bf16[2,256,256]{2,1,0:T(8,128)(2,1)S(1)} %collective-permute-done.refs_4_), channel_id=1, source_target_pairs={{0,128},{128,0},{1,129},{129,1},{2,130},{130,2},{3,131},{131,3},{4... | collective-permute-start | bytes 786440 | tf_op jit(solution)/shard_map/ppermute | solution.py:60
  60.5 11.2 %all-to-all-start.2 = ((bf16[8,32,192]{2,1,0:T(8,128)(2,1)}), bf16[8,32,192]{2,1,0:T(8,128)(2,1)S(1)}, u32[]{:S(2)}, u32[]{:S(2)}) async-start(bf16[8,32,192]{2,1,0:T(8,128)(2,1)} %shard_map.86), calls=%async_computation.2 | async-start | bytes 262144 | tf_op jit(solution)/shard_map/all_to_all | solution.py:44
  67.1 24.2 %collective-permute-start.5 = (bf16[2,256,256]{2,1,0:T(8,128)(2,1)S(1)}, bf16[2,256,256]{2,1,0:T(8,128)(2,1)S(1)}, u32[]{:S(2)}, u32[]{:S(2)}) collective-permute-start(bf16[2,256,256]{2,1,0:T(8,128)(2,1)S(1)} %collective-permute-done.2.refs_8_), channel_id=1, source_target_pairs={{0,128},{128,0},{1,129},{129,1},{2,130},{130,2},{3,131},{131,3},{4... | collective-permute-start | bytes 786440 | tf_op jit(solution)/shard_map/ppermute | solution.py:60
  72.4 18.9 %all-to-all-start.3 = ((bf16[32,2,96]{2,1,0:T(2,128)(2,1)}), bf16[32,2,96]{2,1,0:T(2,128)(2,1)S(1)}, u32[]{:S(2)}, u32[]{:S(2)}) async-start(bf16[32,2,96]{2,1,0:T(2,128)(2,1)} %copy.12), calls=%async_computation.3 | async-start | bytes 32768 | tf_op jit(solution)/shard_map/all_to_all | solution.py:44
  84.3 1.8 %copy-start = (bf16[2304,2,288]{0,2,1:T(8,128)(2,1)S(1)}, bf16[2304,2,288]{0,2,1:T(8,128)(2,1)}, u32[]{:S(2)}) copy-start(bf16[2304,2,288]{0,2,1:T(8,128)(2,1)} %param.9) | copy-start | bytes 7962628
  86.1 22.2 %copy-start.2 = (bf16[2,256,256]{2,1,0:T(8,128)(2,1)S(1)}, bf16[2,256,256]{2,1,0:T(8,128)(2,1)}, u32[]{:S(2)}) copy-start(bf16[2,256,256]{2,1,0:T(8,128)(2,1)} %refs_3_.2) | copy-start | bytes 786436
  86.1 22.2 %copy-start.5 = (s32[2]{0:T(128)S(1)}, s32[2]{0:T(128)}, u32[]{:S(2)}) copy-start(s32[2]{0:T(128)} %refs_1_.1) | copy-start | bytes 28
  91.4 11.2 %collective-permute-start.6 = (bf16[2,8,256]{2,1,0:T(8,128)(2,1)S(1)}, bf16[2,8,256]{2,1,0:T(8,128)(2,1)S(1)}, u32[]{:S(2)}, u32[]{:S(2)}) collective-permute-start(bf16[2,8,256]{2,1,0:T(8,128)(2,1)S(1)} %pad.4), channel_id=1, source_target_pairs={{0,512},{256,768},{512,0},{768,256},{1,513},{257,769},{513,1},{769... | collective-permute-start | bytes 24584 | tf_op jit(solution)/shard_map/ppermute | solution.py:56
  102.7 16.2 %all-to-all-start.4 = ((bf16[8,32,576]{2,1,0:T(8,128)(2,1)}), bf16[8,32,576]{2,1,0:T(8,128)(2,1)S(1)}, u32[]{:S(2)}, u32[]{:S(2)}) async-start(bf16[8,32,576]{2,1,0:T(8,128)(2,1)} %shard_map.87), calls=%async_computation.4 | async-start | bytes 655360 | tf_op jit(solution)/shard_map/all_to_all | solution.py:44
  108.3 9.6 %copy-start.4 = (bf16[2,2,256]{2,1,0:T(2,128)(2,1)S(1)}, bf16[2,2,256]{2,1,0:T(2,128)(2,1)}, u32[]{:S(2)}) copy-start(bf16[2,2,256]{2,1,0:T(2,128)(2,1)} %refs_3_.3) | copy-start | bytes 6148
  109.9 8.1 %collective-permute-start.7 = (f32[2,8,384]{2,1,0:T(8,128)S(1)}, f32[2,8,384]{2,1,0:T(8,128)S(1)}, u32[]{:S(2)}, u32[]{:S(2)}) collective-permute-start(f32[2,8,384]{2,1,0:T(8,128)S(1)} %get-tuple-element.31), channel_id=1, source_target_pairs={{0,512},{256,768},{512,0},{768,256},{1,513},{257,769},{513,1},{769... | collective-permute-start | bytes 73736 | tf_op jit(solution)/shard_map/ppermute | solution.py:56
